TPU v7x, 32 devices: a whole 2x2x4 slice. The times are simulated.
32 devices in a mesh: expert: 4 (over x, core), shard: 8 (over z, y).
Axes of the slice: x: 2, y: 2, z: 4, core: 2. Of those that a mesh axis runs over, the one named last changes fastest.
Arguments:
- tokens_in: bfloat16 [4096, 2048], P(('expert', 'shard')), may hold values from -6 to 6
- cotangent: bfloat16 [4096, 2048], P(('expert', 'shard')), may hold values from -6 to 6
- norm1_gain: float32 [2048], replicated, may hold values from 0.5 to 1.5
- kv_weight: bfloat16 [2048, 4096], P('shard'), may hold values from -0.125 to 0.125
- query_weight: bfloat16 [4, 2048, 2048], P('expert', 'shard'), may hold values from -0.125 to 0.125
- attn_out_weight: bfloat16 [4, 2048, 2048], P('expert', 'shard'), may hold values from -1 to 1
- attn_router: bfloat16 [2048, 4], replicated, may hold values from -0.09375 to 0.09375
- norm2_gain: float32 [2048], replicated, may hold values from 0.5 to 1.5
- in_weight: bfloat16 [4, 2048, 11264], P('expert', 'shard'), may hold values from -0.125 to 0.125
- out_weight: bfloat16 [4, 5632, 2048], P('expert', 'shard'), may hold values from -0.078125 to 0.078125
- mlp_router: bfloat16 [2048, 4], replicated, may hold values from -0.09375 to 0.09375
- attn_routes: int32 [4096, 2], P(('expert', 'shard')), may hold values from 0 to 3, all different within a row; in each aligned block of 128 rows (0 to 127, 128 to 255, ...) at most 80 rows name the same one
- mlp_routes: int32 [4096, 2], P(('expert', 'shard')), may hold values from 0 to 3, all different within a row; in each aligned block of 128 rows (0 to 127, 128 to 255, ...) at most 80 rows name the same one
- place_order: int32 [4, 1024], P('expert', 'shard'), may hold values from 0 to 1023, each once within a row
- seq_lengths: int32 [4, 4], P('expert'), may hold values from 1 to 512, 1024 in all within a row
Outputs:
- output: bfloat16 [4096, 2048], P(('expert', 'shard'))
- grad_input: float32 [4096, 2048], P(('expert', 'shard'))
- grad_norm1: float32 [2048], replicated
- grad_kv_weight: float32 [2048, 4096], P('shard')
- grad_query_weight: float32 [4, 2048, 2048], P('expert', 'shard')
- grad_attn_out: float32 [4, 2048, 2048], P('expert', 'shard')
- grad_router_attn: float32 [2048, 4], replicated
- grad_norm2: float32 [2048], replicated
- grad_in_weight: float32 [4, 2048, 11264], P('expert', 'shard')
- grad_out_weight: float32 [4, 5632, 2048], P('expert', 'shard')
- grad_router_mlp: float32 [2048, 4], replicated
Inputs may be any that keep to these rules, and one draw needn't show every extreme that they name: `attn_routes`: in the 128 rows of one device no expert is named by more than 80 rows, and in some devices one expert is named by exactly 80; a row's two experts differ. `mlp_routes`: in the 128 rows of one device no expert is named by more than 80 rows, and in some devices one expert is named by exactly 80; a row's two experts differ. `place_order`: each row is a permutation of the places of its group. `seq_lengths`: each row sums to 1024 and its largest entry is 512.
All inputs are finite; a program needn't handle non-finite values.
Results may differ from a plain program's by a relative error of at most 0.023.
Values may be sent and summed in bfloat16 or wider, within the bound.
No kernel may reach another device: no remote copies, remote signals or barrier semaphores. Data moves between devices by JAX's collectives and lax.ppermute only.
A program may use at most 512 MiB of HBM per device.

v0:
```python
import jax
import jax.numpy as jnp
from jax import lax
from jax.sharding import PartitionSpec as P

HD = 128


EPS = 1e-05
THETA = 10000.0
NEG = -1e30


def norm_rows(values, norm_gain):
    row_scale = lax.rsqrt(jnp.mean(values * values, axis=-1, keepdims=True) + EPS)
    return (values * row_scale * norm_gain, row_scale)


def norm_back(grad_rows, values, row_scale, norm_gain):
    gain_grad = jnp.sum(grad_rows * values * row_scale, axis=0)
    scaled_grad = grad_rows * norm_gain
    mean_term = jnp.mean(scaled_grad * values, axis=-1, keepdims=True)
    return (
        row_scale * scaled_grad - values * row_scale * row_scale * row_scale * mean_term,
        gain_grad,
    )


def seq_of(places, lengths):
    seq_ends = jnp.cumsum(lengths)
    passed = seq_ends[None, :] <= places[:, None]
    return (passed, jnp.sum(passed.astype(jnp.int32), axis=1))


def rope_tables(places, lengths):
    passed, seq_ids = seq_of(places, lengths)
    starts = jnp.sum(jnp.where(passed, lengths[None, :], 0), axis=1)
    where_in = (places - starts).astype(jnp.float32)
    frequency = THETA ** (-jnp.arange(0, HD // 2, dtype=jnp.float32) * (2.0 / HD))
    angles = where_in[:, None] * frequency[None, :]
    return (jnp.cos(angles), jnp.sin(angles), seq_ids)


def rotate(values, cosine, sine_table):
    half_width = values.shape[-1] // 2
    leading = values[..., :half_width]
    trailing = values[..., half_width:]
    return jnp.concatenate(
        [leading * cosine - trailing * sine_table, trailing * cosine + leading * sine_table],
        axis=-1,
    )


def slot_index(routes, experts, capacity):
    flat_routes = routes.reshape(-1)
    onehot = (flat_routes[:, None] == jnp.arange(experts, dtype=jnp.int32)[None, :]).astype(
        jnp.int32
    )
    before = jnp.cumsum(onehot, axis=0) - onehot
    slot_rank = jnp.sum(before * onehot, axis=1)
    return (flat_routes * capacity + slot_rank, onehot)


def to_owner(slot_rows, slot_pos, experts, capacity):
    buffer = jnp.zeros((experts * capacity, slot_rows.shape[1]), slot_rows.dtype)
    buffer = buffer.at[slot_pos].set(slot_rows).reshape(experts, capacity, -1)
    arrived = lax.all_to_all(buffer, "expert", split_axis=0, concat_axis=0, tiled=True)
    return arrived.reshape(experts * capacity, -1)


def to_home(owner_rows, slot_pos, experts, capacity):
    buffer = owner_rows.reshape(experts, capacity, -1)
    returned = lax.all_to_all(buffer, "expert", split_axis=0, concat_axis=0, tiled=True)
    return returned.reshape(experts * capacity, -1)[slot_pos]


def pair_gates(logits, hot):
    picked = jnp.sum(logits[:, None, :] * hot, axis=-1)
    return jax.nn.softmax(picked, axis=-1)


def gates_back(gate_vals, grad_gates, hot):
    slot_grad = gate_vals * (grad_gates - jnp.sum(gate_vals * grad_gates, axis=-1, keepdims=True))
    return jnp.sum(slot_grad[..., None] * hot, axis=1)


def column_product(left_side, right_side):
    return lax.dot_general(
        left_side, right_side, (((0,), (0,)), ((), ())), preferred_element_type=jnp.float32
    )


def head_spans(query_width):
    group_count = 4
    span = query_width // group_count
    return [
        slice(group_index * span, (group_index + 1) * span) for group_index in range(group_count)
    ]


def group_scores(query_part, key_part, allowed):
    scores = jnp.einsum(
        "qhd,khd->hqk", query_part, key_part, preferred_element_type=jnp.float32
    ) * HD ** (-0.5)
    return jnp.where(allowed[None], scores, NEG)


def attend(query_rows, key_rows, value_rows, allowed):
    row_count = query_rows.shape[0]
    key_count = key_rows.shape[0]
    results, row_tops, row_sums = ([], [], [])
    for column_span in head_spans(query_rows.shape[1]):
        query_part = query_rows[:, column_span].reshape(row_count, -1, HD)
        key_part = key_rows[:, column_span].reshape(key_count, -1, HD)
        value_part = value_rows[:, column_span].reshape(key_count, -1, HD)
        scores = group_scores(query_part, key_part, allowed)
        row_top = jnp.max(scores, axis=-1, keepdims=True)
        exp_scores = jnp.exp(scores - row_top)
        row_total = jnp.sum(exp_scores, axis=-1, keepdims=True)
        prob_low = (exp_scores / row_total).astype(jnp.bfloat16)
        result = jnp.einsum(
            "hqk,khd->qhd", prob_low, value_part, preferred_element_type=jnp.float32
        )
        results.append(result.reshape(row_count, -1))
        row_tops.append(row_top)
        row_sums.append(row_total)
    return (jnp.concatenate(results, axis=1), row_tops, row_sums)


def attend_back(query_rows, key_rows, value_rows, allowed, row_tops, row_sums, grad_rows):
    row_count = query_rows.shape[0]
    key_count = key_rows.shape[0]
    query_grads, key_grads, value_grads = ([], [], [])
    for group_index, column_span in enumerate(head_spans(query_rows.shape[1])):
        query_part = query_rows[:, column_span].reshape(row_count, -1, HD)
        key_part = key_rows[:, column_span].reshape(key_count, -1, HD)
        value_part = value_rows[:, column_span].reshape(key_count, -1, HD)
        grad_part = grad_rows[:, column_span].reshape(row_count, -1, HD)
        scores = group_scores(query_part, key_part, allowed)
        prob_vals = jnp.exp(scores - row_tops[group_index]) / row_sums[group_index]
        prob_low = prob_vals.astype(jnp.bfloat16)
        grad_probs = jnp.einsum(
            "qhd,khd->hqk", grad_part, value_part, preferred_element_type=jnp.float32
        )
        grad_scores = prob_vals * (
            grad_probs - jnp.sum(prob_vals * grad_probs, axis=-1, keepdims=True)
        )
        grad_scaled = (grad_scores * HD ** (-0.5)).astype(jnp.bfloat16)
        grad_query = jnp.einsum(
            "hqk,khd->qhd", grad_scaled, key_part, preferred_element_type=jnp.float32
        )
        grad_keys = jnp.einsum(
            "hqk,qhd->khd", grad_scaled, query_part, preferred_element_type=jnp.float32
        )
        grad_values = jnp.einsum(
            "hqk,qhd->khd", prob_low, grad_part, preferred_element_type=jnp.float32
        )
        query_grads.append(grad_query.reshape(row_count, -1))
        key_grads.append(grad_keys.reshape(key_count, -1))
        value_grads.append(grad_values.reshape(key_count, -1))
    return (
        jnp.concatenate(query_grads, axis=1),
        jnp.concatenate(key_grads, axis=1),
        jnp.concatenate(value_grads, axis=1),
    )


def body(
    tokens_in,
    cotangent,
    norm1_gain,
    kv_weight,
    query_weight,
    attn_out_weight,
    attn_router,
    norm2_gain,
    in_weight,
    out_weight,
    mlp_router,
    attn_routes,
    mlp_routes,
    place_order,
    seq_lengths,
):
    experts = lax.axis_size("expert")
    tok_rows = tokens_in.shape[0]
    capacity = 5 * tok_rows // (2 * experts)
    fetched = (
        lax.all_gather(kv_weight, "shard", axis=0, tiled=True),
        lax.all_gather(query_weight, "shard", axis=1, tiled=True),
        lax.all_gather(attn_out_weight, "shard", axis=1, tiled=True),
        lax.all_gather(in_weight, "shard", axis=1, tiled=True),
        lax.all_gather(out_weight, "shard", axis=1, tiled=True),
    )
    kv_full, query_full, attn_full, in_full, out_full = fetched
    stream = tokens_in.astype(jnp.float32)
    places = place_order[0]
    lengths = seq_lengths[0]
    cosine, sine_table, seq_ids = rope_tables(places, lengths)
    normed1, row_scale1 = norm_rows(stream, norm1_gain)
    hidden1 = normed1.astype(jnp.bfloat16)
    kv_proj = jnp.dot(hidden1, kv_full, preferred_element_type=jnp.float32)
    query_width = kv_proj.shape[1] // 2
    keys_local = (
        rotate(
            kv_proj[:, :query_width].reshape(tok_rows, -1, HD), cosine[:, None], sine_table[:, None]
        )
        .reshape(tok_rows, query_width)
        .astype(jnp.bfloat16)
    )
    values_local = kv_proj[:, query_width:].astype(jnp.bfloat16)
    all_keys, all_values, all_places = (
        lax.all_gather(keys_local, "shard", axis=0, tiled=True),
        lax.all_gather(values_local, "shard", axis=0, tiled=True),
        lax.all_gather(place_order, "shard", axis=1, tiled=True),
    )
    key_places = all_places[0]
    _, key_seq = seq_of(key_places, lengths)
    query_seq = jnp.repeat(seq_ids, 2)
    query_place = jnp.repeat(places, 2)
    allowed = (query_seq[:, None] == key_seq[None, :]) & (
        key_places[None, :] <= query_place[:, None]
    )
    index_attn, hot_attn = slot_index(attn_routes, experts, capacity)
    hot_attn = hot_attn.astype(jnp.float32).reshape(tok_rows, 2, experts)
    gates_attn = pair_gates(
        jnp.dot(hidden1, attn_router, preferred_element_type=jnp.float32), hot_attn
    )
    rows_attn = to_owner(jnp.repeat(hidden1, 2, axis=0), index_attn, experts, capacity)
    query_raw = jnp.dot(rows_attn, query_full[0], preferred_element_type=jnp.float32).astype(
        jnp.bfloat16
    )
    query_tok = to_home(query_raw, index_attn, experts, capacity)
    query_rot = rotate(
        query_tok.astype(jnp.float32).reshape(tok_rows, 2, -1, HD),
        cosine[:, None, None],
        sine_table[:, None, None],
    )
    query_rot = query_rot.astype(jnp.bfloat16).reshape(2 * tok_rows, query_width)
    attn_vec, row_tops, row_sums = attend(query_rot, all_keys, all_values, allowed)
    owner_attn_in = to_owner(attn_vec.astype(jnp.bfloat16), index_attn, experts, capacity)
    proj_attn = jnp.dot(owner_attn_in, attn_full[0], preferred_element_type=jnp.float32).astype(
        jnp.bfloat16
    )
    back_attn = (
        to_home(proj_attn, index_attn, experts, capacity)
        .astype(jnp.float32)
        .reshape(tok_rows, 2, -1)
    )
    middle = stream + jnp.sum(gates_attn[..., None] * back_attn, axis=1)
    normed2, row_scale2 = norm_rows(middle, norm2_gain)
    hidden2 = normed2.astype(jnp.bfloat16)
    index_mlp, hot_mlp = slot_index(mlp_routes, experts, capacity)
    hot_mlp = hot_mlp.astype(jnp.float32).reshape(tok_rows, 2, experts)
    gates_mlp = pair_gates(
        jnp.dot(hidden2, mlp_router, preferred_element_type=jnp.float32), hot_mlp
    )
    rows_mlp = to_owner(jnp.repeat(hidden2, 2, axis=0), index_mlp, experts, capacity)
    joint_proj = jnp.dot(rows_mlp, in_full[0], preferred_element_type=jnp.float32)
    inner_width = joint_proj.shape[1] // 2
    gate_part = joint_proj[:, :inner_width]
    up_part = joint_proj[:, inner_width:]
    sigmoid_gate = jax.nn.sigmoid(gate_part)
    activated = (gate_part * sigmoid_gate * up_part).astype(jnp.bfloat16)
    proj_mlp = jnp.dot(activated, out_full[0], preferred_element_type=jnp.float32).astype(
        jnp.bfloat16
    )
    back_mlp = (
        to_home(proj_mlp, index_mlp, experts, capacity).astype(jnp.float32).reshape(tok_rows, 2, -1)
    )
    result = middle + jnp.sum(gates_mlp[..., None] * back_mlp, axis=1)
    output = result.astype(jnp.bfloat16)
    kv_back, query_back, attn_back, in_back, out_back = (
        lax.all_gather(kv_weight, "shard", axis=0, tiled=True),
        lax.all_gather(query_weight, "shard", axis=1, tiled=True),
        lax.all_gather(attn_out_weight, "shard", axis=1, tiled=True),
        lax.all_gather(in_weight, "shard", axis=1, tiled=True),
        lax.all_gather(out_weight, "shard", axis=1, tiled=True),
    )
    grad_res = cotangent.astype(jnp.float32)
    grad_gates_mlp = jnp.sum(back_mlp * grad_res[:, None, :], axis=-1)
    slot_grad_mlp = (
        (gates_mlp[..., None] * grad_res[:, None, :]).astype(jnp.bfloat16).reshape(2 * tok_rows, -1)
    )
    owner_grad_mlp = to_owner(slot_grad_mlp, index_mlp, experts, capacity)
    grad_act = jnp.dot(owner_grad_mlp, out_back[0].T, preferred_element_type=jnp.float32)
    grad_gate = grad_act * up_part * sigmoid_gate * (1.0 + gate_part * (1.0 - sigmoid_gate))
    grad_up = grad_act * gate_part * sigmoid_gate
    grad_joint = jnp.concatenate([grad_gate, grad_up], axis=1).astype(jnp.bfloat16)
    grad_rows_mlp = jnp.dot(grad_joint, in_back[0].T, preferred_element_type=jnp.float32).astype(
        jnp.bfloat16
    )
    back_rows_mlp = (
        to_home(grad_rows_mlp, index_mlp, experts, capacity)
        .astype(jnp.float32)
        .reshape(tok_rows, 2, -1)
    )
    grad_in_w = lax.psum_scatter(
        column_product(rows_mlp, grad_joint).astype(jnp.bfloat16),
        "shard",
        scatter_dimension=0,
        tiled=True,
    ).astype(jnp.float32)[None]
    logit_grad_mlp = gates_back(gates_mlp, grad_gates_mlp, hot_mlp)
    grad_hidden2 = jnp.sum(back_rows_mlp, axis=1) + jnp.dot(
        logit_grad_mlp, mlp_router.astype(jnp.float32).T, precision=lax.Precision.HIGHEST
    )
    grad_router_mlp = jnp.dot(
        hidden2.astype(jnp.float32).T, logit_grad_mlp, precision=lax.Precision.HIGHEST
    )
    grad_middle, grad_gain2 = norm_back(grad_hidden2, middle, row_scale2, norm2_gain)
    grad_middle = grad_middle + grad_res
    grad_gates_attn = jnp.sum(back_attn * grad_middle[:, None, :], axis=-1)
    slot_grad_attn = (
        (gates_attn[..., None] * grad_middle[:, None, :])
        .astype(jnp.bfloat16)
        .reshape(2 * tok_rows, -1)
    )
    owner_grad_attn = to_owner(slot_grad_attn, index_attn, experts, capacity)
    grad_attn_w = lax.dot_general(
        owner_attn_in, owner_grad_attn, (((0,), (0,)), ((), ())), preferred_element_type=jnp.float32
    )
    grad_attn_rows = jnp.dot(
        owner_grad_attn, attn_back[0].T, preferred_element_type=jnp.float32
    ).astype(jnp.bfloat16)
    grad_attn_vec = to_home(grad_attn_rows, index_attn, experts, capacity)
    grad_query, grad_keys_all, grad_values_all = attend_back(
        query_rot, all_keys, all_values, allowed, row_tops, row_sums, grad_attn_vec
    )
    grad_keys, grad_values = (
        lax.psum_scatter(
            grad_keys_all.astype(jnp.bfloat16), "shard", scatter_dimension=0, tiled=True
        ).astype(jnp.float32),
        lax.psum_scatter(
            grad_values_all.astype(jnp.bfloat16), "shard", scatter_dimension=0, tiled=True
        ).astype(jnp.float32),
    )
    grad_query_raw = rotate(
        grad_query.reshape(tok_rows, 2, -1, HD), cosine[:, None, None], -sine_table[:, None, None]
    )
    grad_query_raw = grad_query_raw.reshape(2 * tok_rows, query_width).astype(jnp.bfloat16)
    owner_grad_query = to_owner(grad_query_raw, index_attn, experts, capacity)
    grad_query_w = lax.dot_general(
        rows_attn, owner_grad_query, (((0,), (0,)), ((), ())), preferred_element_type=jnp.float32
    )
    grad_rows_attn = jnp.dot(
        owner_grad_query, query_back[0].T, preferred_element_type=jnp.float32
    ).astype(jnp.bfloat16)
    back_rows_attn = (
        to_home(grad_rows_attn, index_attn, experts, capacity)
        .astype(jnp.float32)
        .reshape(tok_rows, 2, -1)
    )
    grad_keys_raw = rotate(
        grad_keys.reshape(tok_rows, -1, HD), cosine[:, None], -sine_table[:, None]
    ).reshape(tok_rows, query_width)
    grad_kv = jnp.concatenate([grad_keys_raw, grad_values], axis=1).astype(jnp.bfloat16)
    logit_grad_attn = gates_back(gates_attn, grad_gates_attn, hot_attn)
    grad_router_attn = jnp.dot(
        hidden1.astype(jnp.float32).T, logit_grad_attn, precision=lax.Precision.HIGHEST
    )
    grad_hidden1 = jnp.sum(back_rows_attn, axis=1) + jnp.dot(
        grad_kv, kv_back.T, preferred_element_type=jnp.float32
    )
    grad_hidden1 = grad_hidden1 + jnp.dot(
        logit_grad_attn, attn_router.astype(jnp.float32).T, precision=lax.Precision.HIGHEST
    )
    grad_stream, grad_gain1 = norm_back(grad_hidden1, stream, row_scale1, norm1_gain)
    grad_input = grad_stream + grad_middle
    contract_rows = (((0,), (0,)), ((), ()))
    grad_out_w = lax.psum_scatter(
        column_product(activated, owner_grad_mlp).astype(jnp.bfloat16),
        "shard",
        scatter_dimension=0,
        tiled=True,
    ).astype(jnp.float32)[None]
    grad_kv_w = lax.dot_general(hidden1, grad_kv, contract_rows, preferred_element_type=jnp.float32)
    kv_grad_part, query_grad, attn_grad = (
        lax.psum_scatter(
            grad_kv_w.astype(jnp.bfloat16), "shard", scatter_dimension=0, tiled=True
        ).astype(jnp.float32),
        lax.psum_scatter(
            grad_query_w[None].astype(jnp.bfloat16), "shard", scatter_dimension=1, tiled=True
        ).astype(jnp.float32),
        lax.psum_scatter(
            grad_attn_w[None].astype(jnp.bfloat16), "shard", scatter_dimension=1, tiled=True
        ).astype(jnp.float32),
    )
    kv_grad = lax.psum(kv_grad_part.astype(jnp.bfloat16), "expert").astype(jnp.float32)
    gain1_grad, gain2_grad, router_attn_grad, router_mlp_grad = lax.psum(
        (grad_gain1, grad_gain2, grad_router_attn, grad_router_mlp), ("expert", "shard")
    )
    return (
        output,
        grad_input,
        gain1_grad,
        kv_grad,
        query_grad,
        attn_grad,
        router_attn_grad,
        gain2_grad,
        grad_in_w,
        grad_out_w,
        router_mlp_grad,
    )


def solution(mesh):
    return jax.shard_map(
        body,
        mesh=mesh,
        in_specs=(
            P(("expert", "shard"), None),
            P(("expert", "shard"), None),
            P(),
            P("shard", None),
            P("expert", "shard", None),
            P("expert", "shard", None),
            P(),
            P(),
            P("expert", "shard", None),
            P("expert", "shard", None),
            P(),
            P(("expert", "shard"), None),
            P(("expert", "shard"), None),
            P("expert", "shard"),
            P("expert", None),
        ),
        out_specs=(
            P(("expert", "shard"), None),
            P(("expert", "shard"), None),
            P(),
            P("shard", None),
            P("expert", "shard", None),
            P("expert", "shard", None),
            P(),
            P(),
            P("expert", "shard", None),
            P("expert", "shard", None),
            P(),
        ),
        check_vma=False,
    )
```

profile of v0, /device:TPU:0, one launch (start us, length us, event | category | flops | bytes accessed | tf_op | source)
XLA Modules:
  0.0 4272.5 jit_solution(9259532856106891577)
XLA Ops:
  11.8 228.7 %all-gather.8.cloned.1.call-done = bf16[2048,4096]{1,0:T(8,128)(2,1)} async-done(((bf16[256,4096]{1,0:T(8,128)(2,1)}), bf16[2048,4096]{1,0:T(8,128)(2,1)}) %all-gather.8.cloned.1.call-update) | async-done | bytes 16777232 | tf_op jit(solution)/shard_map/all_gather | solution.py:189
  261.0 20.4 all_to_all.60
  281.4 84.3 %all-gather.12.cloned.1.call-done = bf16[1,2048,2048]{2,1,0:T(8,128)(2,1)} async-done(((bf16[1,256,2048]{2,1,0:T(8,128)(2,1)}), bf16[1,2048,2048]{2,1,0:T(8,128)(2,1)}) %all-gather.12.cloned.1.call-update) | async-done | bytes 8388624 | tf_op jit(solution)/shard_map/all_gather | solution.py:190
  377.5 18.1 all_gather.31
  401.7 38.3 all-gather.10.cloned.1.call-done
  444.6 71.3 %all-gather.14.cloned.1.call-done = bf16[1024,2048]{0,1:T(8,128)(2,1)} async-done(((bf16[128,2048]{0,1:T(8,128)(2,1)}), bf16[1024,2048]{0,1:T(8,128)(2,1)}) %all-gather.14.cloned.1.call-update) | async-done | bytes 4194320 | tf_op jit(solution)/shard_map/all_gather | solution.py:213
  567.2 73.8 %all-gather.16.cloned.1.call-done = bf16[1,2048,2048]{2,1,0:T(8,128)(2,1)} async-done(((bf16[1,256,2048]{2,1,0:T(8,128)(2,1)}), bf16[1,2048,2048]{2,1,0:T(8,128)(2,1)}) %all-gather.16.cloned.1.call-update) | async-done | bytes 8388624 | tf_op jit(solution)/shard_map/all_gather | solution.py:191
  654.5 15.3 all-to-all-done.3
  712.7 801.5 %all-gather.18.cloned.1.call-done = bf16[1,2048,11264]{2,1,0:T(8,128)(2,1)} async-done(((bf16[1,256,11264]{2,1,0:T(8,128)(2,1)}), bf16[1,2048,11264]{2,1,0:T(8,128)(2,1)}) %all-gather.18.cloned.1.call-update) | async-done | bytes 46137360 | tf_op jit(solution)/shard_map/all_gather | solution.py:192
  1514.3 27.1 fusion.10
  1541.3 415.6 %all-gather.20.cloned.1.call-done = bf16[1,5632,2048]{2,1,0:T(8,128)(2,1)} async-done(((bf16[1,704,2048]{2,1,0:T(8,128)(2,1)}), bf16[1,5632,2048]{2,1,0:T(8,128)(2,1)}) %all-gather.20.cloned.1.call-update) | async-done | bytes 23068688 | tf_op jit(solution)/shard_map/all_gather | solution.py:193
  1956.9 27.3 multiply_convert_fusion.1
  1984.2 23.1 fusion.57
  2011.0 13.9 fusion.54
  2077.7 19.7 all_to_all.61
  2104.2 19.7 all_to_all.62
  2174.0 12.8 fusion.113
  2215.4 68.4 %reduce-scatter.22.cloned.1.call-done = bf16[128,2048]{1,0:T(8,128)(2,1)} async-done(((bf16[1024,2048]{1,0:T(8,128)(2,1)}), bf16[128,2048]{1,0:T(8,128)(2,1)}) %reduce-scatter.22.cloned.1.call-update) | async-done | bytes 524304
  2287.3 88.2 %reduce-scatter.24.cloned.1.call-done = bf16[128,2048]{1,0:T(8,128)(2,1)} async-done(((bf16[1024,2048]{1,0:T(8,128)(2,1)}), bf16[128,2048]{1,0:T(8,128)(2,1)}) %reduce-scatter.24.cloned.1.call-update) | async-done | bytes 524304
  2419.7 12.7 fusion.70
  2451.5 19.8 all_to_all.63
  2479.9 187.6 %reduce-scatter.14.cloned.1.call-done = bf16[256,4096]{1,0:T(8,128)(2,1)} async-done(((bf16[2048,4096]{1,0:T(8,128)(2,1)}), bf16[256,4096]{1,0:T(8,128)(2,1)}) %reduce-scatter.14.cloned.1.call-update) | async-done | bytes 2097168 | tf_op jit(solution)/shard_map/reduce_scatter | solution.py:379
  2667.6 17.4 convolution_convert_fusion.1
  2685.3 31.6 convolution_convert_fusion
  2734.2 12.4 all-to-all-done.11
  2758.0 13.1 convolution_add_fusion.2
  2775.2 44.5 %reduce-scatter.18.cloned.1.call-done = bf16[1,256,2048]{2,1,0:T(8,128)(2,1)} async-done(((bf16[1,2048,2048]{2,1,0:T(8,128)(2,1)}), bf16[1,256,2048]{2,1,0:T(8,128)(2,1)}) %reduce-scatter.18.cloned.1.call-update) | async-done | bytes 1048592 | tf_op jit(solution)/shard_map/reduce_scatter | solution.py:385
  2822.5 149.3 %reduce-scatter.16.cloned.1.call-done = bf16[1,256,2048]{2,1,0:T(8,128)(2,1)} async-done(((bf16[1,2048,2048]{2,1,0:T(8,128)(2,1)}), bf16[1,256,2048]{2,1,0:T(8,128)(2,1)}) %reduce-scatter.16.cloned.1.call-update) | async-done | bytes 1048592 | tf_op jit(solution)/shard_map/reduce_scatter | solution.py:382
  2974.6 50.1 %all-reduce.5.cloned.1.call-done = bf16[256,4096]{1,0:T(8,128)(2,1)} async-done(((bf16[256,4096]{1,0:T(8,128)(2,1)}), bf16[256,4096]{1,0:T(8,128)(2,1)}) %all-reduce.5.cloned.1.call-update) | async-done | bytes 2097168 | tf_op jit(solution)/shard_map/psum | solution.py:389
  3028.8 373.4 %reduce-scatter.20.cloned.1.call-done = bf16[704,2048]{1,0:T(8,128)(2,1)} async-done(((bf16[5632,2048]{1,0:T(8,128)(2,1)}), bf16[704,2048]{1,0:T(8,128)(2,1)}) %reduce-scatter.20.cloned.1.call-update) | async-done | bytes 2883600 | tf_op jit(solution)/shard_map/reduce_scatter | solution.py:371
  3407.3 724.6 %reduce-scatter.26.cloned.1.call-done = bf16[256,11264]{1,0:T(8,128)(2,1)} async-done(((bf16[2048,11264]{1,0:T(8,128)(2,1)}), bf16[256,11264]{1,0:T(8,128)(2,1)}) %reduce-scatter.26.cloned.1.call-update) | async-done | bytes 5767184
  4140.4 120.0 %all-reduce.7.cloned.1.call-done = (f32[2048]{0:T(1024)}, f32[2048,4]{0,1:T(4,128)}, f32[2048]{0:T(1024)}, f32[2048,4]{0,1:T(4,128)}) async-done(((f32[2048]{0:T(1024)}, f32[2048,4]{0,1:T(4,128)}, f32[2048]{0:T(1024)}, f32[2048,4]{0,1:T(4,128)}), (f32[2048]{0:T(1024)}, f32[2048,4]{0,1:T(4,128)}, f32[2048]{0:T(1024)}, f32[2048,4]{0,1:T(4,128)})) %all-reduce.7.cloned.1.call-update) | async-done | bytes 81936 | tf_op jit(solution)/shard_map/psum | solution.py:390
  (413 shorter events, 432.9 us)
Async XLA Ops:
  7.2 687.7 %copy-start = (bf16[2048,4]{0,1:T(4,128)(2,1)S(1)}, bf16[2048,4]{0,1:T(4,128)(2,1)}, u32[]{:S(2)}) copy-start(bf16[2048,4]{0,1:T(4,128)(2,1)} %param.25) | copy-start | bytes 49156
  7.2 233.3 %all-gather.8.cloned.1.call-start = ((), (), s32[]{:S(2)}) async-start(), calls=%async_computation.19 | async-start | bytes 18874368 | tf_op jit(solution)/shard_map/all_gather | solution.py:189
  7.9 357.8 %all-gather.12.cloned.1.call-start = ((), (), s32[]{:S(2)}) async-start(), calls=%async_computation.21 | async-start | bytes 9437184 | tf_op jit(solution)/shard_map/all_gather | solution.py:190
  8.7 431.4 %all-gather.10.cloned.1.call-start = ((), (), s32[]{:S(2)}) async-start(), calls=%async_computation.20 | async-start | bytes 4718592 | tf_op jit(solution)/shard_map/all_gather | solution.py:214
  11.7 555.0 %copy-start.2 = (bf16[128,2048]{1,0:T(8,128)(2,1)}, bf16[128,2048]{1,0:T(8,128)(2,1)S(1)}, u32[]{:S(2)}) copy-start(bf16[128,2048]{1,0:T(8,128)(2,1)S(1)} %fusion.118) | copy-start | bytes 1572868
  11.7 237.8 %copy-start.73 = (s32[1,4]{1,0:T(1,128)S(1)}, s32[1,4]{1,0:T(1,128)}, u32[]{:S(2)}) copy-start(s32[1,4]{1,0:T(1,128)} %param.29) | copy-start | bytes 52
  11.8 238.0 %copy-start.70 = (s32[1,128]{1,0:T(1,128)S(1)}, s32[1,128]{1,0:T(1,128)}, u32[]{:S(2)}) copy-start(s32[1,128]{1,0:T(1,128)} %param.28) | copy-start | bytes 1540
  249.5 266.4 %all-gather.14.cloned.1.call-start = ((), (), s32[]{:S(2)}) async-start(), calls=%async_computation.22 | async-start | bytes 4718592 | tf_op jit(solution)/shard_map/all_gather | solution.py:213
  250.8 147.9 %copy-start.25 = (f32[128,64]{1,0:T(8,128)}, f32[128,64]{1,0:T(8,128)S(1)}, u32[]{:S(2)}) copy-start(f32[128,64]{1,0:T(8,128)S(1)} %get-tuple-element.58) | copy-start | bytes 98308
  253.2 387.8 %all-gather.16.cloned.1.call-start = ((), (), s32[]{:S(2)}) async-start(), calls=%async_computation.23 | async-start | bytes 9437184 | tf_op jit(solution)/shard_map/all_gather | solution.py:191
  253.8 1260.5 %all-gather.18.cloned.1.call-start = ((), (), s32[]{:S(2)}) async-start(), calls=%async_computation.24 | async-start | bytes 51904512 | tf_op jit(solution)/shard_map/all_gather | solution.py:192
  254.3 1702.6 %all-gather.20.cloned.1.call-start = ((), (), s32[]{:S(2)}) async-start(), calls=%async_computation.25 | async-start | bytes 25952256 | tf_op jit(solution)/shard_map/all_gather | solution.py:193
  373.4 23.2 all-to-all-start.1
  395.6 1728.3 %copy-start.62 = (s32[1024]{0:T(1024)}, s32[1024]{0:T(1024)S(1)}, u32[]{:S(2)}) copy-start(s32[1024]{0:T(1024)S(1)} %pad_clamp_fusion.1) | copy-start | bytes 12292
  562.7 78.3 %all-to-all-start.2 = ((bf16[4,80,2048]{2,1,0:T(8,128)(2,1)}), bf16[4,80,2048]{2,1,0:T(8,128)(2,1)S(1)}, u32[]{:S(2)}, u32[]{:S(2)}) async-start(bf16[4,80,2048]{2,1,0:T(8,128)(2,1)} %bitcast.31), calls=%async_computation.2 | async-start | bytes 2621440 | tf_op jit(solution)/shard_map/all_to_all | solution.py:67
  648.8 21.0 all-to-all-start.3
  687.1 21.6 all-to-all-start.4
  708.7 832.6 %all-to-all-start.6 = ((bf16[4,80,2048]{2,1,0:T(8,128)(2,1)}), bf16[4,80,2048]{2,1,0:T(8,128)(2,1)S(1)}, u32[]{:S(2)}, u32[]{:S(2)}) async-start(bf16[4,80,2048]{2,1,0:T(8,128)(2,1)} %bitcast.46), calls=%async_computation.6 | async-start | bytes 2621440 | tf_op jit(solution)/shard_map/all_to_all | solution.py:67
  1541.3 442.8 %copy-start.29 = (bf16[4,80,2048]{2,1,0:T(8,128)(2,1)}, bf16[4,80,2048]{2,1,0:T(8,128)(2,1)S(1)}, u32[]{:S(2)}) copy-start(bf16[4,80,2048]{2,1,0:T(8,128)(2,1)S(1)} %all-to-all-done.6) | copy-start | bytes 3932164
  2007.3 20.9 all-to-all-start.7
  2028.2 20.8 all-to-all-start.5
  2031.8 252.0 %reduce-scatter.22.cloned.1.call-start = ((), (), s32[]{:S(2)}) async-start(), calls=%async_computation.31 | async-start | bytes 4718592
  2196.6 178.9 %reduce-scatter.24.cloned.1.call-start = ((), (), s32[]{:S(2)}) async-start(), calls=%async_computation.32 | async-start | bytes 4718592
  2215.3 452.2 %reduce-scatter.14.cloned.1.call-start = ((), (), s32[]{:S(2)}) async-start(), calls=%async_computation.26 | async-start | bytes 18874368 | tf_op jit(solution)/shard_map/reduce_scatter | solution.py:379
  2385.6 434.1 %reduce-scatter.18.cloned.1.call-start = ((), (), s32[]{:S(2)}) async-start(), calls=%async_computation.29 | async-start | bytes 9437184 | tf_op jit(solution)/shard_map/reduce_scatter | solution.py:385
  2394.2 577.6 %reduce-scatter.16.cloned.1.call-start = ((), (), s32[]{:S(2)}) async-start(), calls=%async_computation.28 | async-start | bytes 9437184 | tf_op jit(solution)/shard_map/reduce_scatter | solution.py:382
  2479.9 187.7 %copy-start.30 = (bf16[4,80,2048]{2,1,0:T(8,128)(2,1)S(1)}, bf16[4,80,2048]{2,1,0:T(8,128)(2,1)}, u32[]{:S(2)}) copy-start(bf16[4,80,2048]{2,1,0:T(8,128)(2,1)} %copy-done.29) | copy-start | bytes 3932164
  2479.9 544.8 %all-reduce.5.cloned.1.call-start = ((), (), s32[]{:S(2)}) async-start(), calls=%async_computation.27 | async-start | bytes 4194304 | tf_op jit(solution)/shard_map/psum | solution.py:389
  2667.5 734.6 %reduce-scatter.20.cloned.1.call-start = ((), (), s32[]{:S(2)}) async-start(), calls=%async_computation.30 | async-start | bytes 25952256 | tf_op jit(solution)/shard_map/reduce_scatter | solution.py:371
  2685.0 1446.9 %reduce-scatter.26.cloned.1.call-start = ((), (), s32[]{:S(2)}) async-start(), calls=%async_computation.33 | async-start | bytes 51904512
  2725.7 20.9 all-to-all-start.11
  2729.4 1530.9 %all-reduce.7.cloned.1.call-start = ((), (), s32[]{:S(2)}) async-start(), calls=%async_computation.34 | async-start | bytes 163840 | tf_op jit(solution)/shard_map/psum | solution.py:390
  (77 other events, 1722.5 us)
Sparse Core Ops, SparseCore 0:
  10.2 230.2 all-gather.7
  242.6 123.0 all-gather.11
  368.4 71.6 all-gather.9
  442.5 73.2 all-gather.13
  517.8 123.1 all-gather.15
  642.4 871.8 all-gather.17
  1515.8 441.0 all-gather.19
  2196.7 86.9 reduce-scatter.21
  2287.9 87.5 reduce-scatter.23
  2385.8 281.7 reduce-scatter.13
  2671.6 148.0 reduce-scatter.17
  2823.8 147.9 reduce-scatter.15
  2974.3 50.3 all-reduce.4
  3028.4 373.7 reduce-scatter.19
  3405.9 725.9 reduce-scatter.25
  4140.1 120.2 all-reduce.6
where the time goes:
time: 4280 us; the launch traced here: 4270 us
  waiting for transfers between devices  3570 us (83%)
  matrix products  370 us (9%)
  local copies, waits for them, and re-layouts  106 us (2%)
  blocking collectives  97.8 us (2%)
  other arithmetic  78.8 us (2%)
    unnamed x19, waiting for transfers between devices  884 us
    all_gather x1, waiting for transfers between devices, body(): lax.all_gather(in_weight, 'shard', axis=1, tiled=True)  802 us
    all_gather x1, waiting for transfers between devices, body(): lax.all_gather(out_weight, 'shard', axis=1, tiled=True)  416 us
    reduce_scatter x1, waiting for transfers between devices, body(): lax.psum_scatter(column_product(activated, owner_grad_mlp).astype(jnp.bfl...  373 us
    all_gather x1, waiting for transfers between devices, body(): lax.all_gather(kv_weight, 'shard', axis=0, tiled=True)  229 us
    reduce_scatter x1, waiting for transfers between devices, body(): lax.psum_scatter(grad_kv_w.astype(jnp.bfloat16), 'shard', scatter_dimensi...  188 us
    reduce_scatter x1, waiting for transfers between devices, body(): lax.psum_scatter(grad_query_w[None].astype(jnp.bfloat16), 'shard', scatte...  149 us
    psum x1, waiting for transfers between devices, body(): lax.psum((grad_gain1, grad_gain2, grad_router_attn, grad_router_mlp), ('e...  120 us
  transfers between devices with their start and end apart: 24, of which 21 were waited for; matrix products, arithmetic and copies ran while one was open for 9% of the time, Pallas kernels for 0%

commit v1 on v0

v1 whole, which is shorter than its diff:
```python
import functools

import jax
import jax.numpy as jnp
from jax import lax
from jax.experimental import pallas as pl
from jax.experimental.pallas import tpu as pltpu
from jax.sharding import PartitionSpec as P

HD = 128


EPS = 1e-05
THETA = 10000.0
NEG = -1e30
F32 = jnp.float32
BF16 = jnp.bfloat16
VMEM_LIMIT = 60 * 1024 * 1024


def dot(left, right, contract=((1,), (0,))):
    return lax.dot_general(left, right, (contract, ((), ())), preferred_element_type=F32)


def norm_rows(values, norm_gain):
    row_scale = lax.rsqrt(jnp.mean(values * values, axis=-1, keepdims=True) + EPS)
    return (values * row_scale * norm_gain, row_scale)


def norm_back(grad_rows, values, row_scale, norm_gain):
    gain_grad = jnp.sum(grad_rows * values * row_scale, axis=0)
    scaled_grad = grad_rows * norm_gain
    mean_term = jnp.mean(scaled_grad * values, axis=-1, keepdims=True)
    return (
        row_scale * scaled_grad - values * row_scale * row_scale * row_scale * mean_term,
        gain_grad,
    )


def seq_of(places, lengths):
    seq_ends = jnp.cumsum(lengths)
    passed = seq_ends[None, :] <= places[:, None]
    return (passed, jnp.sum(passed.astype(jnp.int32), axis=1))


def rope_tables(places, lengths):
    passed, seq_ids = seq_of(places, lengths)
    starts = jnp.sum(jnp.where(passed, lengths[None, :], 0), axis=1)
    where_in = (places - starts).astype(F32)
    frequency = THETA ** (-jnp.arange(0, HD // 2, dtype=F32) * (2.0 / HD))
    angles = where_in[:, None] * frequency[None, :]
    return (jnp.cos(angles), jnp.sin(angles), seq_ids)


def rotate(values, cosine, sine_table):
    half_width = values.shape[-1] // 2
    leading = values[..., :half_width]
    trailing = values[..., half_width:]
    return jnp.concatenate(
        [leading * cosine - trailing * sine_table, trailing * cosine + leading * sine_table],
        axis=-1,
    )


def ring_cycle(count):
    if count == 8:
        return [0, 2, 4, 6, 7, 5, 3, 1]
    if count == 16:
        return [0, 1, 2, 3, 7, 6, 5, 9, 10, 11, 15, 14, 13, 12, 8, 4]
    return list(range(count))


def ring_move(value, hops):
    cycle = ring_cycle(lax.axis_size("shard"))
    count = len(cycle)
    return lax.ppermute(
        value, "shard", [(cycle[i], cycle[(i + hops) % count]) for i in range(count)]
    )


def after(value, *others):
    return lax.optimization_barrier((value,) + others)[0] if others else value


def ring_gather(block, ties=()):
    count = lax.axis_size("shard")
    far = count // 2
    ahead, behind = [block], [block]
    for step in range(far):
        if step < len(ties):
            ahead[-1] = after(ahead[-1], *ties[step])
        if step < far - 1:
            ahead.append(ring_move(ahead[-1], 1))
            behind.append(ring_move(behind[-1], -1))
    cut = block.shape[0] // 2
    last = [ring_move(ahead[-1][:cut], 1), ring_move(behind[-1][cut:], -1)]
    return jnp.concatenate(ahead + last + behind[:0:-1], axis=0)


def direct_gather(block):
    count = lax.axis_size("shard")
    return jnp.stack([block] + [ring_move(block, r) for r in range(1, count)])


def ring_scatter(partial, ties=()):
    count = lax.axis_size("shard")
    far = count // 2
    rows = partial.shape[0] // count
    cut = rows // 2
    tie = lambda value, step: after(value, *ties[step]) if step < len(ties) else value
    partial = tie(partial, 0)
    part = [partial[r * rows : (r + 1) * rows] for r in range(count)]
    low = ring_move(part[far][:cut], -1)
    high = ring_move(part[far][cut:], 1)
    empty = jnp.zeros_like(low)
    back = part[far - 1] + jnp.concatenate([low, empty], axis=0)
    fore = part[far + 1] + jnp.concatenate([empty, high], axis=0)
    for r in range(far - 2, 0, -1):
        back = tie(back, far - 1 - r)
        back = part[r] + ring_move(back, -1)
        fore = part[count - r] + ring_move(fore, 1)
    back = tie(back, far - 1)
    return part[0].astype(F32) + ring_move(back, -1).astype(F32) + ring_move(fore, 1).astype(F32)


def direct_scatter(partial):
    count = lax.axis_size("shard")
    total = partial[0]
    for r in range(1, count):
        total = total + ring_move(partial[r], -r)
    return total


def core_swap(value):
    return lax.ppermute(value, "expert", [(i, i ^ 1) for i in range(lax.axis_size("expert"))])


def chip_shift(value, hops):
    count = lax.axis_size("expert")
    chips = count // 2
    return lax.ppermute(
        value, "expert", [(i, (i // 2 + hops) % chips * 2 + i % 2) for i in range(count)]
    )


def expert_order():
    index = lax.axis_index("expert")
    chips = lax.axis_size("expert") // 2
    return [
        (index // 2 + dx) % chips * 2 + (index % 2 + dc) % 2
        for dx in range(chips)
        for dc in range(2)
    ]


def expert_gather(value):
    chips = lax.axis_size("expert") // 2
    own = [value] + [chip_shift(value, -dx) for dx in range(1, chips)]
    return [piece for item in own for piece in (item, core_swap(item))]


def after_all(values, *others):
    return [after(item, *others) for item in values]


def far_halves(sums):
    cut = sums[0].shape[0] // 2
    return [item[:cut] for item in sums], [item[cut:] for item in sums]


def whole_halves(first, second):
    return [jnp.concatenate(pair, axis=0) for pair in zip(first, second)]


def expert_sums(pieces, firsts):
    return [
        (pieces[k].astype(F32) + core_swap(pieces[k + 1]).astype(F32)).astype(BF16) for k in firsts
    ]


def far_exchange(sums):
    return [chip_shift(item, dx + 1) for dx, item in enumerate(sums)]


def sum_f32(parts):
    return sum(item.astype(F32) for item in parts)


def expert_reduce(pieces):
    sums = expert_sums(pieces, range(0, len(pieces), 2))
    return sum_f32(sums[:1] + far_exchange(sums[1:]))


def shard_exchange(pieces):
    return lax.all_to_all(pieces, "shard", split_axis=0, concat_axis=0, tiled=True)


def sum_all(value):
    for axis in ("expert", "shard"):
        count = lax.axis_size(axis)
        step = 1
        while step < count:
            value = value + lax.ppermute(value, axis, [(i, i ^ step) for i in range(count)])
            step *= 2
    return value


def turn(values, cosine, sine_table):
    return values * cosine + pltpu.roll(values, HD // 2, 1) * sine_table


def whole(shape):
    zeros = (0,) * len(shape)
    return pl.BlockSpec(shape, lambda *_: zeros, pipeline_mode=pl.Buffered(1))


def tiles(shape):
    return pl.BlockSpec(shape, lambda i: (i,) + (0,) * (len(shape) - 1))


def named_by(routes, order, slot, k):
    return (routes[:, slot : slot + 1] == order[0, k]).astype(F32)


def columns(parts):
    lane = lax.broadcasted_iota(jnp.int32, (parts[0].shape[0], len(parts)), 1)
    total = jnp.zeros(lane.shape, F32)
    for k, part in enumerate(parts):
        total = jnp.where(lane == k, part, total)
    return total


def attend_kernel(experts, order, hidden, *refs):
    query_w, refs = refs[:experts], refs[experts:]
    kv_w, refs = refs[0], refs[1:]
    out_w, refs = refs[:experts], refs[experts:]
    router, routes_ref, bounds, place_row, cosine, sine_table = refs[:6]
    mixed, query_out, keys, values, wide, gates_out = refs[6:]
    step = pl.program_id(0)
    tile = mixed.shape[0]
    total_rows, span = keys.shape

    @pl.when(step == 0)
    def _():
        @pl.loop(0, total_rows // tile)
        def _(i):
            here = pl.ds(pl.multiple_of(i * tile, tile), tile)
            both = dot(hidden[here, :], kv_w[...])
            for h in range(span // HD):
                cols = slice(h * HD, (h + 1) * HD)
                keys[here, cols] = turn(both[:, cols], cosine[here, :], sine_table[here, :]).astype(BF16)
            values[here, :] = both[:, span:].astype(BF16)

    here = pl.ds(pl.multiple_of(step * tile, tile), tile)
    rows_in = hidden[here, :]
    routes = routes_ref[...]
    hot = [[named_by(routes, order, j, k) for k in range(experts)] for j in range(2)]
    logits = dot(rows_in, router[...])
    picked = [sum(hot[j][k] * logits[:, k : k + 1] for k in range(experts)) for j in range(2)]
    top = jnp.maximum(picked[0], picked[1])
    raised = [jnp.exp(value - top) for value in picked]
    gates = [value / (raised[0] + raised[1]) for value in raised]
    gates_out[...] = columns([hot[0][k] * gates[0] + hot[1][k] * gates[1] for k in range(experts)])
    query_all = [dot(rows_in, query_w[k][...]) for k in range(experts)]
    allowed = (place_row[...] >= bounds[:, 0:1]) & (place_row[...] <= bounds[:, 1:2])
    cos_here, sin_here = cosine[here, :], sine_table[here, :]
    vectors = []
    for j in range(2):
        raw = sum(hot[j][k] * query_all[k] for k in range(experts))
        heads = []
        for h in range(span // HD):
            cols = slice(h * HD, (h + 1) * HD)
            query = turn(raw[:, cols], cos_here, sin_here).astype(BF16)
            query_out[:, j * span + h * HD : j * span + (h + 1) * HD] = query
            scores = dot(query, keys[:, cols], ((1,), (1,))) * HD**-0.5
            scores = jnp.where(allowed, scores, NEG)
            row_top = jnp.max(scores, axis=1, keepdims=True)
            exp_scores = jnp.exp(scores - row_top)
            row_total = jnp.sum(exp_scores, axis=1, keepdims=True)
            heads.append(dot(exp_scores.astype(BF16), values[:, cols]) / row_total)
        vectors.append((jnp.concatenate(heads, axis=1) if len(heads) > 1 else heads[0]) * gates[j])
    total = 0.0
    for k in range(experts):
        part = (hot[0][k] * vectors[0] + hot[1][k] * vectors[1]).astype(BF16)
        wide[:, k * span : (k + 1) * span] = part
        total = total + dot(part, out_w[k][...])
    mixed[...] = total.astype(BF16)


def attend(hidden, query_w, kv_w, out_w, router, routes, order, bounds, place_row, cosine, sine_table):
    total_rows, width = hidden.shape
    experts = len(query_w)
    span = query_w[0].shape[1]
    tile = 256
    return pl.pallas_call(
        functools.partial(attend_kernel, experts),
        grid=(total_rows // tile,),
        in_specs=[pl.BlockSpec(memory_space=pltpu.SMEM), whole(hidden.shape)]
        + [whole(w.shape) for w in query_w]
        + [whole(kv_w.shape)]
        + [whole(w.shape) for w in out_w]
        + [
            whole(router.shape),
            tiles((tile, 2)),
            tiles((tile, 2)),
            whole(place_row.shape),
            whole(cosine.shape),
            whole(sine_table.shape),
        ],
        out_specs=[
            tiles((tile, width)),
            tiles((tile, 2 * span)),
            whole((total_rows, span)),
            whole((total_rows, span)),
            tiles((tile, experts * span)),
            tiles((tile, experts)),
        ],
        out_shape=[
            jax.ShapeDtypeStruct((total_rows, width), BF16),
            jax.ShapeDtypeStruct((total_rows, 2 * span), BF16),
            jax.ShapeDtypeStruct((total_rows, span), BF16),
            jax.ShapeDtypeStruct((total_rows, span), BF16),
            jax.ShapeDtypeStruct((total_rows, experts * span), BF16),
            jax.ShapeDtypeStruct((total_rows, experts), F32),
        ],
        compiler_params=pltpu.CompilerParams(vmem_limit_bytes=VMEM_LIMIT),
        cost_estimate=pl.CostEstimate(
            flops=2 * total_rows * width * span * (2 * experts + 2) + 16 * total_rows * total_rows * span,
            bytes_accessed=2 * width * span * (2 * experts + 2) + 8 * total_rows * width,
            transcendentals=2 * total_rows * total_rows * span // HD,
        ),
        name="attend",
    )(order, hidden, *query_w, kv_w, *out_w, router, routes, bounds, place_row, cosine, sine_table)


def attend_back_kernel(experts, steps, order, grad_mid, *refs):
    query_w, refs = refs[:experts], refs[experts:]
    kv_w, refs = refs[0], refs[1:]
    out_w, refs = refs[:experts], refs[experts:]
    routes_ref, gates_ref, bounds_row, place_col, cosine, sine_table, query_ref, keys, values, wide = refs[:10]
    grad_rows, grad_first, gate_sums, key_sum, value_sum = refs[10:]
    step = pl.program_id(0)
    tile = grad_rows.shape[0]
    total_rows, span = keys.shape

    @pl.when(step == 0)
    def _():
        key_sum[...] = jnp.zeros_like(key_sum)
        value_sum[...] = jnp.zeros_like(value_sum)

    @pl.when(step < steps)
    def _():
        here = pl.ds(pl.multiple_of(step * tile, tile), tile)
        routes = routes_ref[here, :]
        gates = gates_ref[here, :]
        hot = [[named_by(routes, order, j, k) for k in range(experts)] for j in range(2)]
        allowed = (place_col[...] >= bounds_row[0:1, here]) & (place_col[...] <= bounds_row[1:2, here])
        rows_in = grad_mid[...]
        slot_grads = [0.0, 0.0]
        sums = []
        for k in range(experts):
            grad = dot(rows_in, out_w[k][...], ((1,), (1,)))
            part = wide[:, k * span : (k + 1) * span].astype(F32)
            sums.append(jnp.sum(part * grad, axis=1, keepdims=True))
            for j in range(2):
                slot_grads[j] = slot_grads[j] + (hot[j][k] * gates[:, k : k + 1]) * grad
        gate_sums[...] = columns(sums)
        cos_here, sin_here = cosine[here, :], sine_table[here, :]
        slot_queries = []
        for j in range(2):
            heads = []
            for h in range(span // HD):
                cols = slice(h * HD, (h + 1) * HD)
                query = query_ref[:, j * span + h * HD : j * span + (h + 1) * HD]
                grad = slot_grads[j][:, cols].astype(BF16)
                scores = dot(keys[:, cols], query, ((1,), (1,))) * HD**-0.5
                scores = jnp.where(allowed, scores, NEG)
                exp_scores = jnp.exp(scores - jnp.max(scores, axis=0, keepdims=True))
                probs = exp_scores * (1.0 / jnp.sum(exp_scores, axis=0, keepdims=True))
                value_sum[:, cols] += dot(probs.astype(BF16), grad)
                grad_probs = dot(values[:, cols], grad, ((1,), (1,)))
                mean = jnp.sum(probs * grad_probs, axis=0, keepdims=True)
                grad_scores = (probs * (grad_probs - mean)).astype(BF16)
                key_sum[:, cols] += dot(grad_scores, query)
                grad_query = dot(grad_scores, keys[:, cols], ((0,), (0,))) * HD**-0.5
                heads.append(turn(grad_query, cos_here, -sin_here))
            slot_queries.append(jnp.concatenate(heads, axis=1) if len(heads) > 1 else heads[0])
        for k in range(experts):
            grad_first[here, k * span : (k + 1) * span] = (
                hot[0][k] * slot_queries[0] + hot[1][k] * slot_queries[1]
            ).astype(BF16)

    @pl.when(step == steps - 1)
    def _():
        for h in range(span // HD):
            cols = slice(h * HD, (h + 1) * HD)
            grad_first[:, experts * span + h * HD : experts * span + (h + 1) * HD] = turn(
                key_sum[:, cols] * HD**-0.5, cosine[...], -sine_table[...]
            ).astype(BF16)
        grad_first[:, (experts + 1) * span :] = value_sum[...].astype(BF16)

    @pl.when(step >= steps)
    def _():
        here = pl.ds(pl.multiple_of((step - steps) * tile, tile), tile)
        total = dot(grad_first[here, experts * span :], kv_w[...], ((1,), (1,)))
        for k in range(experts):
            total = total + dot(
                grad_first[here, k * span : (k + 1) * span], query_w[k][...], ((1,), (1,))
            )
        grad_rows[...] = total.astype(BF16)


def attend_back(
    grad_mid, query_w, kv_w, out_w, routes, order, gates, bounds_row, place_col, cosine, sine_table,
    query, keys, values, wide,
):
    total_rows, width = grad_mid.shape
    experts = len(query_w)
    span = query_w[0].shape[1]
    tile = 256
    steps = total_rows // tile

    def early(shape):
        return pl.BlockSpec(shape, lambda i: (jnp.minimum(i, steps - 1), 0))

    return pl.pallas_call(
        functools.partial(attend_back_kernel, experts, steps),
        grid=(2 * steps,),
        in_specs=[pl.BlockSpec(memory_space=pltpu.SMEM), early((tile, width))]
        + [whole(w.shape) for w in query_w]
        + [whole(kv_w.shape)]
        + [whole(w.shape) for w in out_w]
        + [
            whole(routes.shape),
            whole(gates.shape),
            whole(bounds_row.shape),
            whole(place_col.shape),
            whole(cosine.shape),
            whole(sine_table.shape),
            early((tile, 2 * span)),
            whole(keys.shape),
            whole(values.shape),
            early((tile, experts * span)),
        ],
        out_specs=[
            pl.BlockSpec((tile, width), lambda i: (jnp.maximum(i - steps, 0), 0)),
            whole((total_rows, (experts + 2) * span)),
            early((tile, experts)),
        ],
        out_shape=[
            jax.ShapeDtypeStruct((total_rows, width), BF16),
            jax.ShapeDtypeStruct((total_rows, (experts + 2) * span), BF16),
            jax.ShapeDtypeStruct((total_rows, experts), F32),
        ],
        scratch_shapes=[pltpu.VMEM((total_rows, span), F32), pltpu.VMEM((total_rows, span), F32)],
        compiler_params=pltpu.CompilerParams(vmem_limit_bytes=VMEM_LIMIT),
        cost_estimate=pl.CostEstimate(
            flops=2 * total_rows * width * span * (2 * experts + 2) + 40 * total_rows * total_rows * span,
            bytes_accessed=2 * width * span * (2 * experts + 2) + 8 * total_rows * width,
            transcendentals=2 * total_rows * total_rows * span // HD,
        ),
        name="attend_back",
    )(
        order, grad_mid, *query_w, kv_w, *out_w, routes, gates, bounds_row, place_col, cosine, sine_table,
        query, keys, values, wide,
    )


def split_kernel(block, gate, up):
    half = block.shape[1] // 2
    gate[...] = block[:, :half].T.reshape(gate.shape)
    up[...] = block[:, half:].T.reshape(up.shape)


def split_columns(weight, shards):
    depth, both = weight.shape
    inner = both // (2 * shards)
    tile = 128
    out = jax.ShapeDtypeStruct((shards, inner, depth), BF16)
    spec = pl.BlockSpec((shards, inner, tile), lambda i: (0, 0, i))
    return pl.pallas_call(
        split_kernel,
        grid=(depth // tile,),
        in_specs=[tiles((tile, both))],
        out_specs=[spec, spec],
        out_shape=[out, out],
        compiler_params=pltpu.CompilerParams(vmem_limit_bytes=VMEM_LIMIT),
        cost_estimate=pl.CostEstimate(flops=0, bytes_accessed=4 * depth * both, transcendentals=0),
        name="split_columns",
    )(weight)


def join_kernel(gate, up, out):
    shards, inner, tile = gate.shape
    half = shards * inner
    out[:, :half] = gate[...].reshape(half, tile).T.astype(F32)
    out[:, half:] = up[...].reshape(half, tile).T.astype(F32)


def join_columns(gate, up):
    shards, inner, depth = gate.shape
    tile = 128
    spec = pl.BlockSpec((shards, inner, tile), lambda i: (0, 0, i))
    return pl.pallas_call(
        join_kernel,
        grid=(depth // tile,),
        in_specs=[spec, spec],
        out_specs=tiles((tile, 2 * shards * inner)),
        out_shape=jax.ShapeDtypeStruct((depth, 2 * shards * inner), F32),
        compiler_params=pltpu.CompilerParams(vmem_limit_bytes=VMEM_LIMIT),
        cost_estimate=pl.CostEstimate(
            flops=0, bytes_accessed=12 * shards * depth * inner, transcendentals=0
        ),
        name="join_columns",
    )(gate, up)


def forward_kernel(capacity, hidden, rank, gates, gate_w, up_w, down_w, rows_out, gate_out, up_out, act_out, result):
    blocks, rows = rank.shape[1:]
    slot = lax.broadcasted_iota(jnp.int32, (capacity, rows), 0)
    scales = []
    for b in range(blocks):
        hit = slot == rank[0, b : b + 1, :]
        to, at = slice(b * capacity, (b + 1) * capacity), slice(b * rows, (b + 1) * rows)
        rows_out[to, :] = dot(hit.astype(BF16), hidden[at, :]).astype(BF16)
        scales.append(jnp.sum(jnp.where(hit, gates[0, b : b + 1, :], 0.0), axis=1, keepdims=True))
    scale = jnp.concatenate(scales, axis=0)
    gate = dot(rows_out[...], gate_w[...], ((1,), (1,)))
    up = dot(rows_out[...], up_w[...], ((1,), (1,)))
    act = (gate * jax.nn.sigmoid(gate) * up * scale).astype(BF16)
    gate_out[...] = gate.astype(BF16)
    up_out[...] = up.astype(BF16)
    act_out[...] = act
    result[...] = dot(act, down_w[...]).astype(BF16)


def backward_kernel(
    capacity, cot, rank, gates, gate_ref, up_ref, act, gate_w, up_w, down_w,
    cot_out, grad_gate_out, grad_up_out, grad_rows, gate_sums,
):
    blocks, rows = rank.shape[1:]
    slot = lax.broadcasted_iota(jnp.int32, (capacity, rows), 0)
    scales = []
    for b in range(blocks):
        hit = slot == rank[0, b : b + 1, :]
        to, at = slice(b * capacity, (b + 1) * capacity), slice(b * rows, (b + 1) * rows)
        cot_out[to, :] = dot(hit.astype(BF16), cot[at, :]).astype(BF16)
        scales.append(jnp.sum(jnp.where(hit, gates[0, b : b + 1, :], 0.0), axis=1, keepdims=True))
    scale = jnp.concatenate(scales, axis=0)
    back = dot(cot_out[...], down_w[...], ((1,), (1,)))
    sums = jnp.sum(act[...].astype(F32) * back, axis=1, keepdims=True)
    for b in range(blocks):
        hit = slot == rank[0, b : b + 1, :]
        part = sums[b * capacity : (b + 1) * capacity, :]
        gate_sums[0, b : b + 1, :] = jnp.sum(jnp.where(hit, part, 0.0), axis=0, keepdims=True)
    gate = gate_ref[...].astype(F32)
    sigmoid_gate = jax.nn.sigmoid(gate)
    grad_act = back * scale
    grad_up = (grad_act * gate * sigmoid_gate).astype(BF16)
    grad_gate = (
        grad_act * up_ref[...].astype(F32) * sigmoid_gate * (1.0 + gate * (1.0 - sigmoid_gate))
    ).astype(BF16)
    grad_up_out[...] = grad_up
    grad_gate_out[...] = grad_gate
    grad_rows[...] = (dot(grad_gate, gate_w[...]) + dot(grad_up, up_w[...])).astype(BF16)


def expert_call(kernel, name, products, block_args, part_args, weights, out_cols, sums, rank, gates, capacity):
    shards, rows = rank.shape
    inner, width = weights[0].shape
    blocks = 4
    steps = shards // blocks
    slots = shards * capacity
    part = blocks * capacity
    small = tiles((1, blocks, rows))
    sums_shape = [jax.ShapeDtypeStruct((steps, blocks, rows), F32)] * sums
    return pl.pallas_call(
        functools.partial(kernel, capacity),
        grid=(steps,),
        in_specs=[tiles((blocks * rows, width)) for _ in block_args]
        + [small, small]
        + [tiles((part, item.shape[1])) for item in part_args]
        + [whole(item.shape) for item in weights],
        out_specs=[tiles((part, cols)) for cols in out_cols] + [small] * sums,
        out_shape=[jax.ShapeDtypeStruct((slots, cols), BF16) for cols in out_cols] + sums_shape,
        compiler_params=pltpu.CompilerParams(vmem_limit_bytes=VMEM_LIMIT),
        cost_estimate=pl.CostEstimate(
            flops=2 * products * slots * width * inner,
            bytes_accessed=6 * width * inner + 2 * shards * rows * width + 4 * slots * (width + inner),
            transcendentals=slots * inner,
        ),
        name=name,
    )(
        *block_args, rank.reshape(steps, blocks, rows), gates.reshape(steps, blocks, rows), *part_args, *weights
    )


def combine_kernel(capacity, rank, *refs):
    parts, out = refs[:-1], refs[-1]
    rows = out.shape[0]
    total = 0.0
    slot = lax.broadcasted_iota(jnp.int32, (rows, capacity), 1)
    for k, part in enumerate(parts):
        pick = (slot == rank[:, k : k + 1]).astype(BF16)
        total = total + dot(pick, part[...])
    out[...] = total.astype(BF16)


def combine(rank_cols, parts, rows, capacity):
    total_rows, experts = rank_cols.shape
    width = parts[0].shape[1]
    return pl.pallas_call(
        functools.partial(combine_kernel, capacity),
        grid=(total_rows // rows,),
        in_specs=[tiles((rows, experts))] + [tiles((capacity, width)) for _ in parts],
        out_specs=tiles((rows, width)),
        out_shape=jax.ShapeDtypeStruct((total_rows, width), BF16),
        compiler_params=pltpu.CompilerParams(vmem_limit_bytes=VMEM_LIMIT),
        cost_estimate=pl.CostEstimate(
            flops=2 * total_rows * 256 * experts * width,
            bytes_accessed=2 * total_rows * width + 2 * experts * capacity * total_rows // rows * width,
            transcendentals=0,
        ),
        name="combine",
    )(rank_cols, *parts)


def pair_gates(hidden, router, hot):
    logits = dot(hidden, router)
    picked = jnp.sum(logits[:, None, :] * hot, axis=-1)
    return jax.nn.softmax(picked, axis=-1)


def logit_grads(gates, scaled_grads):
    return scaled_grads - gates * jnp.sum(scaled_grads, axis=-1, keepdims=True)


def exact(left, right):
    return jnp.dot(left, right, precision=lax.Precision.HIGHEST)


def body(
    tokens_in,
    cotangent,
    norm1_gain,
    kv_weight,
    query_weight,
    attn_out_weight,
    attn_router,
    norm2_gain,
    in_weight,
    out_weight,
    mlp_router,
    attn_routes,
    mlp_routes,
    place_order,
    seq_lengths,
):
    experts = lax.axis_size("expert")
    shards = lax.axis_size("shard")
    rows, width = tokens_in.shape
    total_rows = rows * shards
    capacity = -(-5 * rows // (2 * experts) // 16) * 16
    span = query_weight.shape[2] // shards
    inner = out_weight.shape[1]
    depth = in_weight.shape[1]
    order = jnp.stack(expert_order())
    own_expert = order[0]

    chunk = depth // experts
    kv_chunk = lax.dynamic_slice_in_dim(kv_weight, own_expert * chunk, chunk, axis=0)
    kv_chunk = kv_chunk.reshape(chunk, 2, shards, span).transpose(2, 0, 1, 3)
    query_blocks = query_weight[0].reshape(depth, shards, span).transpose(1, 0, 2)
    first_blocks = jnp.concatenate([query_blocks, kv_chunk.reshape(shards, 2 * chunk, span)], axis=1)

    info = jnp.concatenate(
        [place_order, attn_routes.T, mlp_routes.T, jnp.zeros((3, rows), jnp.int32)], axis=0
    )
    info = direct_gather(info)
    info, first_blocks = lax.optimization_barrier((info, first_blocks))
    first_cols = shard_exchange(first_blocks)
    inverse = jnp.argsort(order)
    first_all = expert_gather(first_cols)
    query_w = [item[:, :depth].reshape(width, span) for item in first_all]
    kv_w = jnp.take(jnp.stack([item[:, depth:] for item in first_all]), inverse, axis=0)
    kv_w = kv_w.reshape(experts, shards, chunk, 2 * span).transpose(1, 0, 2, 3).reshape(width, 2 * span)
    attn_out_w = expert_gather(attn_out_weight[0])

    stream = tokens_in.astype(F32)
    normed1, row_scale1 = norm_rows(stream, norm1_gain)
    hidden1_own = normed1.astype(BF16)
    hidden1 = ring_gather(after(hidden1_own, first_blocks), [(), (), (first_cols, attn_out_w[2])])
    lengths = seq_lengths[0]
    places = info[:, 0].reshape(total_rows)
    cosine, sine_table, seq_ids = rope_tables(places, lengths)
    starts = jnp.sum(
        jnp.where(jnp.arange(lengths.shape[0])[None, :] < seq_ids[:, None], lengths[None, :], 0), axis=1
    )
    cosine = jnp.concatenate([cosine, cosine], axis=1)
    sine_table = jnp.concatenate([-sine_table, sine_table], axis=1)
    bounds = jnp.stack([starts, places])

    def routes_of(first):
        return info[:, first : first + 2].transpose(0, 2, 1).reshape(total_rows, 2)

    routes_attn = routes_of(1)
    hot_mlp = (routes_of(3)[:, :, None] == order[None, None, :]).astype(F32)
    attn_router_rel = jnp.take(attn_router, order, axis=1)
    mlp_router_rel = jnp.take(mlp_router, order, axis=1)

    gate_blocks, up_blocks = split_columns(in_weight[0], shards)
    gate_cols = shard_exchange(after(gate_blocks, hidden1)).transpose(1, 0, 2).reshape(inner, width)
    up_cols = shard_exchange(after(up_blocks, gate_cols)).transpose(1, 0, 2).reshape(inner, width)
    gate_weights = expert_gather(gate_cols)
    up_weights = expert_gather(up_cols)
    down_weights = expert_gather(after(out_weight[0], hidden1))

    router_wide = jnp.pad(attn_router_rel, ((0, 0), (0, 128 - experts)))
    mixed, query, keys, values, vec_wide, gates_attn = attend(
        hidden1, query_w, kv_w, attn_out_w, router_wide, routes_attn, order[None], bounds.T,
        places[None], cosine, sine_table,
    )
    middle = stream + ring_scatter(mixed, [(gate_cols, down_weights[2]), (), (), (up_cols,)])

    normed2, row_scale2 = norm_rows(middle, norm2_gain)
    hidden2_own = normed2.astype(BF16)
    hidden2 = ring_gather(hidden2_own, [(gate_weights[2],)])
    cot = ring_gather(after(cotangent, hidden2))
    gates_mlp = pair_gates(hidden2, mlp_router_rel, hot_mlp)
    gates_wide = jnp.sum(hot_mlp * gates_mlp[..., None], axis=1).reshape(shards, rows, experts)
    named = jnp.sum(hot_mlp, axis=1).reshape(shards, rows, experts)
    earlier = (jnp.arange(rows)[:, None] > jnp.arange(rows)[None, :]).astype(BF16)
    rank = jnp.einsum("tu,bue->bte", earlier, named.astype(BF16), preferred_element_type=F32)
    rank = jnp.where(named > 0, rank, -1.0).astype(jnp.int32)
    rank_cols = rank.reshape(total_rows, experts)
    rank_rows = rank.transpose(2, 0, 1)
    gate_rows = gates_wide.transpose(2, 0, 1)

    weights = list(zip(gate_weights, up_weights, down_weights))
    rows_in, gates_low, ups_low, acts, results = zip(
        *[
            expert_call(
                forward_kernel, "expert_forward", 3, [hidden2], [], weights[k],
                [width, inner, inner, inner, width], 0, rank_rows[k], gate_rows[k], capacity,
            )
            for k in range(experts)
        ]
    )
    result_rows = ring_scatter(combine(rank_cols, results, rows, capacity))
    output = (middle + result_rows).astype(BF16)
    backs, gate_w_grads = {}, {}
    cot_now = after(cot, *results)
    for k in range(experts - 1, -1, -1):
        backs[k] = expert_call(
            backward_kernel, "expert_backward", 3, [cot_now], [gates_low[k], ups_low[k], acts[k]],
            weights[k], [width, inner, inner, width], 1, rank_rows[k], gate_rows[k], capacity,
        )
        cot_now = after(cot_now, backs[k][3])
        if k >= 2:
            gate_w_grads[k] = dot(backs[k][1], rows_in[k], ((0,), (0,))).astype(BF16)
            cot_now = after(cot_now, gate_w_grads[k])
    rows_cot, grad_gates, grad_ups, grads, gate_sums = zip(*[backs[k] for k in range(experts)])
    gate_far = far_halves(expert_sums(gate_w_grads, range(2, experts, 2)))
    gate_came = far_exchange(gate_far[0])
    combined = combine(rank_cols, [after(grads[0], *gate_far[0])] + list(grads[1:]), rows, capacity)
    late = after(rows_in[2], combined)
    up_w_grads = {
        k: dot(grad_ups[k], after(rows_in[k], late), ((0,), (0,))).astype(BF16)
        for k in range(experts - 1, 1, -1)
    }
    up_far = far_halves(expert_sums(up_w_grads, range(2, experts, 2)))
    second = far_exchange(after_all(gate_far[1], combined))
    third = far_exchange(after_all(up_far[0], *second))
    back_rows = ring_scatter(combined, [(result_rows, *gate_came), (), (*second, *up_far[0])])
    gate_came = whole_halves(gate_came, second)
    late = after(rows_in[0], *up_far[0])
    for k in (1, 0):
        gate_w_grads[k] = dot(grad_gates[k], after(rows_in[k], late), ((0,), (0,))).astype(BF16)
        up_w_grads[k] = dot(grad_ups[k], after(rows_in[k], late), ((0,), (0,))).astype(BF16)
    down_w_grads = {
        k: dot(acts[k], after(rows_cot[k], late), ((0,), (0,))).astype(BF16)
        for k in range(experts - 1, -1, -1)
    }
    down_far = far_halves(expert_sums(down_w_grads, range(2, experts, 2)))
    gate_sum = (expert_sums(gate_w_grads, [0])[0].astype(F32) + sum_f32(gate_came)).astype(BF16)
    up_near = expert_sums(up_w_grads, [0])[0].astype(F32)
    gate_sums = jnp.stack([item.reshape(shards, rows) for item in gate_sums], axis=1)

    logit_grad_mlp = logit_grads(gates_wide[0], direct_scatter(gate_sums).T)
    grad_hidden2 = back_rows + exact(logit_grad_mlp, mlp_router_rel.astype(F32).T)
    grad_router_mlp = exact(hidden2_own.astype(F32).T, logit_grad_mlp)
    grad_middle, grad_gain2 = norm_back(grad_hidden2, middle, row_scale2, norm2_gain)
    grad_middle = grad_middle + cotangent.astype(F32)

    fourth = far_exchange(after_all(up_far[1], *third))
    fifth = far_exchange(after_all(down_far[0], *fourth))
    grad_mid = ring_gather(grad_middle.astype(BF16), [third, (gate_sum,), fourth])
    up_sum = (up_near + sum_f32(whole_halves(third, fourth))).astype(BF16)
    gate_grad = shard_exchange(gate_sum.reshape(inner, shards, depth).transpose(1, 0, 2))
    grad_mid = after(grad_mid, gate_grad, up_sum, *fifth)
    up_grad = shard_exchange(
        after(up_sum, gate_grad).reshape(inner, shards, depth).transpose(1, 0, 2)
    )
    sixth = far_exchange(after_all(down_far[1], *fifth))
    grad_rows1, grad_first, gate_sums_attn = attend_back(
        grad_mid, query_w, kv_w, attn_out_w, routes_attn, order[None], gates_attn, bounds,
        places[:, None], cosine, sine_table, query, keys, values, vec_wide,
    )
    back_rows1 = ring_scatter(grad_rows1, [sixth, (up_grad,)])
    down_came = whole_halves(fifth, sixth)
    gate_sums_attn = direct_scatter(
        gate_sums_attn.reshape(shards, rows, experts).transpose(0, 2, 1)
    ).T
    grad_first_w = dot(hidden1, grad_first, ((0,), (0,))).astype(BF16)
    grad_second_w = dot(vec_wide, grad_mid, ((0,), (0,))).astype(BF16)

    logit_grad_attn = logit_grads(gates_attn[:rows], gate_sums_attn)
    grad_router_attn = exact(hidden1_own.astype(F32).T, logit_grad_attn)
    grad_hidden1 = back_rows1 + exact(logit_grad_attn, attn_router_rel.astype(F32).T)
    grad_stream, _ = norm_back(grad_hidden1, stream, row_scale1, norm1_gain)
    grad_gain1 = jnp.sum(grad_rows1.astype(F32) * hidden1.astype(F32), axis=0) / norm1_gain
    grad_gain1 = grad_gain1 + jnp.sum(
        exact(logit_grad_attn, attn_router_rel.astype(F32).T) * stream * row_scale1, axis=0
    )
    grad_input = grad_stream + grad_middle

    in_grad = join_columns(gate_grad, up_grad)[None]
    out_grad = (expert_sums(down_w_grads, [0])[0].astype(F32) + sum_f32(down_came))[None]
    attn_grad = expert_reduce(jnp.split(grad_second_w, experts, axis=0))[None]
    kv_grad = grad_first_w[:, experts * span :].reshape(shards, experts, chunk, 2 * span)
    kv_grad = jnp.take(kv_grad, order, axis=1).reshape(shards, experts, 2 * chunk, span)
    first_grad = expert_reduce(
        [
            jnp.concatenate(
                [
                    grad_first_w[:, k * span : (k + 1) * span].reshape(shards, depth, span),
                    kv_grad[:, k],
                ],
                axis=1,
            )
            for k in range(experts)
        ]
    )
    first_grad = shard_exchange(first_grad.astype(BF16))
    query_grad = first_grad[:, :depth].transpose(1, 0, 2).reshape(1, depth, shards * span).astype(F32)
    kv_grad = first_grad[:, depth:].reshape(shards, chunk, 2, span)
    kv_grad = kv_grad.transpose(1, 2, 0, 3).reshape(chunk, 2 * shards * span)
    kv_grad = jnp.take(jnp.stack(expert_gather(kv_grad)), inverse, axis=0)
    kv_grad = kv_grad.reshape(depth, 2 * shards * span).astype(F32)

    mlp_small = sum_all(
        jnp.concatenate([grad_gain2[None], jnp.take(grad_router_mlp.T, inverse, axis=0)], axis=0)
    )
    attn_small = sum_all(
        jnp.concatenate([grad_gain1[None], jnp.take(grad_router_attn.T, inverse, axis=0)], axis=0)
    )
    return (
        output,
        grad_input,
        attn_small[0],
        kv_grad,
        query_grad,
        attn_grad,
        attn_small[1:].T,
        mlp_small[0],
        in_grad,
        out_grad,
        mlp_small[1:].T,
    )


def solution(mesh):
    return jax.shard_map(
        body,
        mesh=mesh,
        in_specs=(
            P(("expert", "shard"), None),
            P(("expert", "shard"), None),
            P(),
            P("shard", None),
            P("expert", "shard", None),
            P("expert", "shard", None),
            P(),
            P(),
            P("expert", "shard", None),
            P("expert", "shard", None),
            P(),
            P(("expert", "shard"), None),
            P(("expert", "shard"), None),
            P("expert", "shard"),
            P("expert", None),
        ),
        out_specs=(
            P(("expert", "shard"), None),
            P(("expert", "shard"), None),
            P(),
            P("shard", None),
            P("expert", "shard", None),
            P("expert", "shard", None),
            P(),
            P(),
            P("expert", "shard", None),
            P("expert", "shard", None),
            P(),
        ),
        check_vma=False,
    )
```

time: 4280 us -> 1180 us (0.28)
  waiting for transfers between devices: 3570 us -> 422 us
  matrix products: 370 us -> 78.6 us
  Pallas kernels: 0 us -> 220 us
  starting transfers between devices: 31.4 us -> 239 us
  blocking collectives: 97.8 us -> 0 us
    all_gather x7 -> x0, waiting for transfers between devices: 1710 us -> none  [the longest x1 802 us: body(): lax.all_gather(in_weight, 'shard', axis=1, tiled=True)]
    unnamed x19 -> x0, waiting for transfers between devices: 884 us -> none
    reduce_scatter x4 -> x0, waiting for transfers between devices: 755 us -> none  [the longest x1 373 us: body(): lax.psum_scatter(column_product(activated, owner_grad_mlp).astype(jnp.bfl...]
    ppermute x0 -> x131, waiting for transfers between devices: none -> 422 us  [the longest x85 295 us: ring_move(): lax.ppermute(value, 'shard', [(cycle[i], cycle[(i + hops) % count]) for i...]
    dot_general x41 -> x20, matrix products: 350 us -> 78.6 us  [the longest x15 72.5 us: dot(): lax.dot_general(left, right, (contract, ((), ())), preferred_element_type...]
    pallas_call x0 -> x14, Pallas kernels: none -> 220 us  [the longest x8 112 us: expert_call(): pl.pallas_call(functools.partial(kernel, capacity), grid=(steps,), in_spe...]
    ppermute x0 -> x131, starting transfers between devices: none -> 210 us  [the longest x85 180 us: ring_move(): lax.ppermute(value, 'shard', [(cycle[i], cycle[(i + hops) % count]) for i...]
    psum x2 -> x0, waiting for transfers between devices: 170 us -> none  [the longest x1 120 us: body(): lax.psum((grad_gain1, grad_gain2, grad_router_attn, grad_router_mlp), ('e...]
  transfers between devices with their start and end apart: 24 -> 137, of which waited for: 21 -> 56; matrix products, arithmetic and copies ran while one was open for 9% -> 24% of each run, Pallas kernels for 0% -> 17%
where the time goes in v1:
time: 1180 us
  waiting for transfers between devices  422 us (36%)
  starting transfers between devices  239 us (20%)
  Pallas kernels  220 us (19%)
  local copies, waits for them, and re-layouts  115 us (10%)
  other arithmetic  98.6 us (8%)
  matrix products  78.6 us (7%)
    ppermute x85, waiting for transfers between devices, ring_move(): lax.ppermute(value, 'shard', [(cycle[i], cycle[(i + hops) % count]) for i...  295 us
    ppermute x85, starting transfers between devices, ring_move(): lax.ppermute(value, 'shard', [(cycle[i], cycle[(i + hops) % count]) for i...  180 us
    ppermute x14, waiting for transfers between devices, chip_shift(): lax.ppermute(value, 'expert', [(i, (i // 2 + hops) % chips * 2 + i % 2) f...  120 us
    pallas_call x8, Pallas kernels, expert_call(): pl.pallas_call(functools.partial(kernel, capacity), grid=(steps,), in_spe...  112 us
    dot_general x15, matrix products, dot(): lax.dot_general(left, right, (contract, ((), ())), preferred_element_type...  72.5 us
    pallas_call x1, Pallas kernels, attend_back(): pl.pallas_call(functools.partial(attend_back_kernel, experts, steps), gri...  41.9 us
    pallas_call x1, Pallas kernels, attend(): pl.pallas_call(functools.partial(attend_kernel, experts), grid=(total_row...  33 us
    unnamed x172, local copies, waits for them, and re-layouts  32.1 us
  transfers between devices with their start and end apart: 137, of which 56 were waited for; matrix products, arithmetic and copies ran while one was open for 24% of the time, Pallas kernels for 17%

profile of v1, /device:TPU:0, one launch (start us, length us, event | category | flops | bytes accessed | tf_op | source)
XLA Modules:
  0.0 1176.2 jit_solution(6018651065121329031)
XLA Ops:
  27.9 31.2 %collective-permute-done.12 = bf16[128,2048]{1,0:T(8,128)(2,1)} collective-permute-done((bf16[128,2048]{1,0:T(8,128)(2,1)S(1)}, bf16[128,2048]{1,0:T(8,128)(2,1)}, u32[]{:S(2)}, u32[]{:S(2)}) %collective-permute-start.12) | collective-permute-done | bytes 524320 | tf_op jit(solution)/shard_map/ppermute | solution.py:76
  60.1 10.7 collective-permute-start.8
  71.0 9.9 collective-permute-done.13
  121.3 12.8 %collective-permute-done.17 = bf16[8,384,256]{2,1,0:T(8,128)(2,1)} collective-permute-done((bf16[8,384,256]{2,1,0:T(8,128)(2,1)S(1)}, bf16[8,384,256]{2,1,0:T(8,128)(2,1)}, u32[]{:S(2)}, u32[]{:S(2)}) %collective-permute-start.17) | collective-permute-done | bytes 1572896 | tf_op jit(solution)/shard_map/ppermute | solution.py:141
  158.2 33.0 %attend.1 = (bf16[1024,2048]{1,0:T(8,128)(2,1)}, bf16[1024,512]{1,0:T(8,128)(2,1)}, bf16[1024,256]{1,0:T(8,128)(2,1)}, bf16[1024,256]{1,0:T(8,128)(2,1)}, bf16[1024,1024]{1,0:T(8,128)(2,1)}, /*index=5*/f32[1024,4]{1,0:T(8,128)}) custom-call(s32[1,4]{1,0:T(1,128)} %bitcast.385, bf16[1024,2048]{1,0:T(8,128)(2,1)} %constant_dynamic-update-slice_fusion.hidden, ...), custom_call_target="tpu_custom_call" | custom-call | flops 15032385536 | bytes 27262976 | tf_op jit(solution)/shard_map/attend/pallas_call | solution.py:295
  195.0 9.7 collective-permute-done.21.down_w
  214.3 36.7 %collective-permute-done.22 = bf16[64,2048]{1,0:T(8,128)(2,1)S(1)} collective-permute-done((bf16[64,2048]{1,0:T(8,128)(2,1)S(1)}, bf16[64,2048]{1,0:T(8,128)(2,1)S(1)}, u32[]{:S(2)}, u32[]{:S(2)}) %collective-permute-start.22) | collective-permute-done | bytes 262176 | tf_op jit(solution)/shard_map/ppermute | solution.py:76
  252.1 14.0 %collective-permute-start.23 = (bf16[128,2048]{1,0:T(8,128)(2,1)S(1)}, bf16[128,2048]{1,0:T(8,128)(2,1)S(1)}, u32[]{:S(2)}, u32[]{:S(2)}) collective-permute-start(bf16[128,2048]{1,0:T(8,128)(2,1)S(1)} %pad_add_fusion.5), channel_id=1, source_target_pairs={{0,1},{2,0},{4,2},{6,4},{7,6},{5,7},{3,5},{1,3},{8,9},{10,8},{12,1... | collective-permute-start | bytes 1572872 | tf_op jit(solution)/shard_map/ppermute | solution.py:76
  266.1 26.9 %collective-permute-done.23 = bf16[128,2048]{1,0:T(8,128)(2,1)S(1)} collective-permute-done((bf16[128,2048]{1,0:T(8,128)(2,1)S(1)}, bf16[128,2048]{1,0:T(8,128)(2,1)S(1)}, u32[]{:S(2)}, u32[]{:S(2)}) %collective-permute-start.23) | collective-permute-done | bytes 524320 | tf_op jit(solution)/shard_map/ppermute | solution.py:76
  309.8 10.0 collective-permute-done.27
  321.2 12.3 %collective-permute-done.28 = bf16[128,2048]{1,0:T(8,128)(2,1)S(1)} collective-permute-done((bf16[128,2048]{1,0:T(8,128)(2,1)S(1)}, bf16[128,2048]{1,0:T(8,128)(2,1)S(1)}, u32[]{:S(2)}, u32[]{:S(2)}) %collective-permute-start.28) | collective-permute-done | bytes 524320 | tf_op jit(solution)/shard_map/ppermute | solution.py:76
  352.4 17.7 %collective-permute-done.30.gate_w = bf16[704,2048]{1,0:T(8,128)(2,1)} collective-permute-done((bf16[704,2048]{1,0:T(8,128)(2,1)}, bf16[704,2048]{1,0:T(8,128)(2,1)}, u32[]{:S(2)}, u32[]{:S(2)}) %collective-permute-start.30) | collective-permute-done | bytes 2883616 | tf_op jit(solution)/shard_map/ppermute | solution.py:141
  430.4 33.5 %collective-permute-done.42.up_w = bf16[704,2048]{1,0:T(8,128)(2,1)} collective-permute-done((bf16[704,2048]{1,0:T(8,128)(2,1)}, bf16[704,2048]{1,0:T(8,128)(2,1)}, u32[]{:S(2)}, u32[]{:S(2)}) %collective-permute-start.42) | collective-permute-done | bytes 2883616 | tf_op jit(solution)/shard_map/ppermute | solution.py:141
  464.4 12.5 %expert_forward.4 = (bf16[640,2048]{1,0:T(8,128)(2,1)}, bf16[640,704]{1,0:T(8,128)(2,1)}, bf16[640,704]{1,0:T(8,128)(2,1)}, bf16[640,704]{1,0:T(8,128)(2,1)}, bf16[640,2048]{1,0:T(8,128)(2,1)}) custom-call(bf16[1024,2048]{1,0:T(8,128)(2,1)} %copy-done.10, s32[2,4,128]{2,1,0:T(4,128)} %bitcast.394, f32[2,4,128]{2,1,0:T(4,128)} %bitcast.398, ...), custom_call_target="tpu_custom_call" | custom-call | flops 5536481280 | bytes 19890176 | tf_op jit(solution)/shard_map/expert_forward/pallas_call | solution.py:577
  481.6 12.7 %expert_forward.6 = (bf16[640,2048]{1,0:T(8,128)(2,1)}, bf16[640,704]{1,0:T(8,128)(2,1)}, bf16[640,704]{1,0:T(8,128)(2,1)}, bf16[640,704]{1,0:T(8,128)(2,1)}, bf16[640,2048]{1,0:T(8,128)(2,1)}) custom-call(bf16[1024,2048]{1,0:T(8,128)(2,1)} %copy-done.10, s32[2,4,128]{2,1,0:T(4,128)} %bitcast.402, f32[2,4,128]{2,1,0:T(4,128)} %bitcast.404, ...), custom_call_target="tpu_custom_call" | custom-call | flops 5536481280 | bytes 19890176 | tf_op jit(solution)/shard_map/expert_forward/pallas_call | solution.py:577
  496.8 12.5 %expert_forward.5 = (bf16[640,2048]{1,0:T(8,128)(2,1)}, bf16[640,704]{1,0:T(8,128)(2,1)}, bf16[640,704]{1,0:T(8,128)(2,1)}, bf16[640,704]{1,0:T(8,128)(2,1)}, bf16[640,2048]{1,0:T(8,128)(2,1)}) custom-call(bf16[1024,2048]{1,0:T(8,128)(2,1)} %copy-done.10, s32[2,4,128]{2,1,0:T(4,128)} %bitcast.396, f32[2,4,128]{2,1,0:T(4,128)} %bitcast.400, ...), custom_call_target="tpu_custom_call" | custom-call | flops 5536481280 | bytes 19890176 | tf_op jit(solution)/shard_map/expert_forward/pallas_call | solution.py:577
  523.6 12.6 %expert_forward.7 = (bf16[640,2048]{1,0:T(8,128)(2,1)}, bf16[640,704]{1,0:T(8,128)(2,1)}, bf16[640,704]{1,0:T(8,128)(2,1)}, bf16[640,704]{1,0:T(8,128)(2,1)}, bf16[640,2048]{1,0:T(8,128)(2,1)}) custom-call(bf16[1024,2048]{1,0:T(8,128)(2,1)} %copy-done.10, s32[2,4,128]{2,1,0:T(4,128)} %bitcast.406, f32[2,4,128]{2,1,0:T(4,128)} %bitcast.408, ...), custom_call_target="tpu_custom_call" | custom-call | flops 5536481280 | bytes 19890176 | tf_op jit(solution)/shard_map/expert_forward/pallas_call | solution.py:577
  536.2 10.7 combine.2
  556.1 15.3 %expert_backward.4 = (bf16[640,2048]{1,0:T(8,128)(2,1)}, bf16[640,704]{1,0:T(8,128)(2,1)}, bf16[640,704]{1,0:T(8,128)(2,1)}, bf16[640,2048]{1,0:T(8,128)(2,1)}, f32[2,4,128]{2,1,0:T(4,128)}) custom-call(bf16[1024,2048]{1,0:T(8,128)(2,1)} %constant_dynamic-update-slice_fusion.18.cot, s32[2,4,128]{2,1,0:T(4,128)} %bitcast.407, f32[2,4,128]{2,1,0:T(4,128)} %bitcast.409, ...), custom_call_target="tpu_custom_call" | custom-call | flops 5536481280 | bytes 19890176 | tf_op jit(solution)/shard_map/expert_backward/pallas_call | solution.py:577
  579.1 15.3 %expert_backward.5 = (bf16[640,2048]{1,0:T(8,128)(2,1)}, bf16[640,704]{1,0:T(8,128)(2,1)}, bf16[640,704]{1,0:T(8,128)(2,1)}, bf16[640,2048]{1,0:T(8,128)(2,1)}, f32[2,4,128]{2,1,0:T(4,128)}) custom-call(bf16[1024,2048]{1,0:T(8,128)(2,1)} %constant_dynamic-update-slice_fusion.18.cot, s32[2,4,128]{2,1,0:T(4,128)} %bitcast.403, f32[2,4,128]{2,1,0:T(4,128)} %bitcast.405, ...), custom_call_target="tpu_custom_call" | custom-call | flops 5536481280 | bytes 19890176 | tf_op jit(solution)/shard_map/expert_backward/pallas_call | solution.py:577
  607.2 15.3 %expert_backward.6 = (bf16[640,2048]{1,0:T(8,128)(2,1)}, bf16[640,704]{1,0:T(8,128)(2,1)}, bf16[640,704]{1,0:T(8,128)(2,1)}, bf16[640,2048]{1,0:T(8,128)(2,1)}, f32[2,4,128]{2,1,0:T(4,128)}) custom-call(bf16[1024,2048]{1,0:T(8,128)(2,1)} %constant_dynamic-update-slice_fusion.18.cot, s32[2,4,128]{2,1,0:T(4,128)} %bitcast.397, f32[2,4,128]{2,1,0:T(4,128)} %bitcast.401, ...), custom_call_target="tpu_custom_call" | custom-call | flops 5536481280 | bytes 19890176 | tf_op jit(solution)/shard_map/expert_backward/pallas_call | solution.py:577
  622.5 15.3 %expert_backward.7 = (bf16[640,2048]{1,0:T(8,128)(2,1)}, bf16[640,704]{1,0:T(8,128)(2,1)}, bf16[640,704]{1,0:T(8,128)(2,1)}, bf16[640,2048]{1,0:T(8,128)(2,1)}, f32[2,4,128]{2,1,0:T(4,128)}) custom-call(bf16[1024,2048]{1,0:T(8,128)(2,1)} %constant_dynamic-update-slice_fusion.18.cot, s32[2,4,128]{2,1,0:T(4,128)} %bitcast.395, f32[2,4,128]{2,1,0:T(4,128)} %bitcast.399, ...), custom_call_target="tpu_custom_call" | custom-call | flops 5536481280 | bytes 19890176 | tf_op jit(solution)/shard_map/expert_backward/pallas_call | solution.py:577
  655.3 10.6 combine.3
  710.7 14.5 %collective-permute-done.66 = bf16[352,2048]{1,0:T(8,128)(2,1)S(1)} collective-permute-done((bf16[352,2048]{1,0:T(8,128)(2,1)}, bf16[352,2048]{1,0:T(8,128)(2,1)S(1)}, u32[]{:S(2)}, u32[]{:S(2)}) %collective-permute-start.66) | collective-permute-done | bytes 1441824 | tf_op jit(solution)/shard_map/ppermute | solution.py:141
  793.0 36.0 %collective-permute-done.88 = bf16[128,2048]{1,0:T(8,128)(2,1)S(1)} collective-permute-done((bf16[128,2048]{1,0:T(8,128)(2,1)S(1)}, bf16[128,2048]{1,0:T(8,128)(2,1)S(1)}, u32[]{:S(2)}, u32[]{:S(2)}) %collective-permute-start.88) | collective-permute-done | bytes 524320 | tf_op jit(solution)/shard_map/ppermute | solution.py:76
  829.0 14.2 %collective-permute-start.89 = (bf16[128,2048]{1,0:T(8,128)(2,1)S(1)}, bf16[128,2048]{1,0:T(8,128)(2,1)S(1)}, u32[]{:S(2)}, u32[]{:S(2)}) collective-permute-start(bf16[128,2048]{1,0:T(8,128)(2,1)S(1)} %collective-permute-done.88), channel_id=1, source_target_pairs={{0,1},{2,0},{4,2},{6,4},{7,6},{5,7},{3,5},{1,3},{8,9},{10,8},{12,1... | collective-permute-start | bytes 1572872 | tf_op jit(solution)/shard_map/ppermute | solution.py:76
  843.2 17.2 %collective-permute-start.84 = (bf16[128,2048]{1,0:T(8,128)(2,1)S(1)}, bf16[128,2048]{1,0:T(8,128)(2,1)S(1)}, u32[]{:S(2)}, u32[]{:S(2)}) collective-permute-start(bf16[128,2048]{1,0:T(8,128)(2,1)S(1)} %collective-permute-done.82), channel_id=1, source_target_pairs={{0,2},{2,4},{4,6},{6,7},{7,5},{5,3},{3,1},{1,0},{8,10},{10,12},{12... | collective-permute-start | bytes 1572872 | tf_op jit(solution)/shard_map/ppermute | solution.py:76
  906.0 41.9 %attend_back.1 = (bf16[1024,2048]{1,0:T(8,128)(2,1)}, bf16[1024,1536]{1,0:T(8,128)(2,1)}, f32[1024,4]{1,0:T(8,128)}) custom-call(s32[1,4]{1,0:T(1,128)} %bitcast.386, bf16[1024,2048]{1,0:T(8,128)(2,1)} %copy-done.42, bf16[2048,256]{1,0:T(8,128)(2,1)} %bitcast.356, bf16[2048,256]{1,0:T(8,128)(2,1)} %bitcast.360, bf16[2048,256]{1,0:T(8,128)(2,1)} %bitcast.358, ...), custom_call_target="tpu_custom_call" | custom-call | flops 21474836480 | bytes 27262976 | tf_op jit(solution)/shard_map/attend_back/pallas_call | solution.py:426
  958.0 9.8 convolution_convert_fusion
  1020.8 19.8 %collective-permute-done.118 = bf16[8,384,256]{2,1,0:T(8,128)(2,1)} collective-permute-done((bf16[8,384,256]{2,1,0:T(8,128)(2,1)}, bf16[8,384,256]{2,1,0:T(8,128)(2,1)}, u32[]{:S(2)}, u32[]{:S(2)}) %collective-permute-start.118) | collective-permute-done | bytes 1572896 | tf_op jit(solution)/shard_map/ppermute | solution.py:141
  1062.5 25.0 %collective-permute-done.98 = bf16[128,2048]{1,0:T(8,128)(2,1)S(1)} collective-permute-done((bf16[128,2048]{1,0:T(8,128)(2,1)S(1)}, bf16[128,2048]{1,0:T(8,128)(2,1)S(1)}, u32[]{:S(2)}, u32[]{:S(2)}) %collective-permute-start.98) | collective-permute-done | bytes 524320 | tf_op jit(solution)/shard_map/ppermute | solution.py:76
  1089.5 12.2 %collective-permute-start.101 = (bf16[128,2048]{1,0:T(8,128)(2,1)S(1)}, bf16[128,2048]{1,0:T(8,128)(2,1)S(1)}, u32[]{:S(2)}, u32[]{:S(2)}) collective-permute-start(bf16[128,2048]{1,0:T(8,128)(2,1)S(1)} %get-tuple-element.226), channel_id=1, source_target_pairs={{0,2},{2,4},{4,6},{6,7},{7,5},{5,3},{3,1},{1,0},{8,10},{10,12},{12... | collective-permute-start | bytes 1572872 | tf_op jit(solution)/shard_map/ppermute | solution.py:76
  (614 shorter events, 592.0 us)
Async XLA Ops:
  20.3 61.8 %all-to-all-start = ((bf16[8,384,256]{2,1,0:T(8,128)(2,1)}), bf16[8,384,256]{2,1,0:T(8,128)(2,1)S(1)}, u32[]{:S(2)}, u32[]{:S(2)}) async-start(bf16[8,384,256]{2,1,0:T(8,128)(2,1)} %pad_maximum_fusion.2), calls=%async_computation | async-start | bytes 3145728 | tf_op jit(solution)/shard_map/all_to_all | solution.py:195
  26.3 55.3 %collective-permute-start.9 = (bf16[256,2048]{1,0:T(8,128)(2,1)}, bf16[256,2048]{1,0:T(8,128)(2,1)}, u32[]{:S(2)}, u32[]{:S(2)}) collective-permute-start(bf16[256,2048]{1,0:T(8,128)(2,1)} %bitcast.420), channel_id=1, source_target_pairs={{0,16},{8,24},{16,0},{24,8},{1,17},{9,25},{17,1},{25,9},{2,18},{10... | collective-permute-start | bytes 3145736 | tf_op jit(solution)/shard_map/ppermute | solution.py:141
  70.8 87.4 %collective-permute-start.19 = (bf16[256,2048]{1,0:T(8,128)(2,1)}, bf16[256,2048]{1,0:T(8,128)(2,1)}, u32[]{:S(2)}, u32[]{:S(2)}) collective-permute-start(bf16[256,2048]{1,0:T(8,128)(2,1)} %bitcast.421), channel_id=1, source_target_pairs={{0,8},{8,0},{16,24},{24,16},{1,9},{9,1},{17,25},{25,17},{2,10},{10... | collective-permute-start | bytes 3145736 | tf_op jit(solution)/shard_map/ppermute | solution.py:135
  111.1 80.1 %all-to-all-start.1 = ((bf16[8,704,256]{2,1,0:T(8,128)(2,1)}), bf16[8,704,256]{2,1,0:T(8,128)(2,1)}, u32[]{:S(2)}, u32[]{:S(2)}) async-start(bf16[8,704,256]{2,1,0:T(8,128)(2,1)} %get-tuple-element.114), calls=%async_computation.1 | async-start | bytes 5767168 | tf_op jit(solution)/shard_map/all_to_all | solution.py:195
  140.0 64.7 %collective-permute-start.21 = (bf16[704,2048]{1,0:T(8,128)(2,1)}, bf16[704,2048]{1,0:T(8,128)(2,1)}, u32[]{:S(2)}, u32[]{:S(2)}) collective-permute-start(bf16[704,2048]{1,0:T(8,128)(2,1)} %bitcast.48.down_w), channel_id=1, source_target_pairs={{0,16},{8,24},{16,0},{24,8},{1,17},{9,25},{17,1},{25,9},{2,18},{10... | collective-permute-start | bytes 8650760 | tf_op jit(solution)/shard_map/ppermute | solution.py:141
  204.7 130.7 %all-to-all-start.2 = ((bf16[8,704,256]{2,1,0:T(8,128)(2,1)}), bf16[8,704,256]{2,1,0:T(8,128)(2,1)}, u32[]{:S(2)}, u32[]{:S(2)}) async-start(bf16[8,704,256]{2,1,0:T(8,128)(2,1)} %get-tuple-element.118), calls=%async_computation.2 | async-start | bytes 5767168 | tf_op jit(solution)/shard_map/all_to_all | solution.py:195
  212.3 38.7 %collective-permute-start.22 = (bf16[64,2048]{1,0:T(8,128)(2,1)S(1)}, bf16[64,2048]{1,0:T(8,128)(2,1)S(1)}, u32[]{:S(2)}, u32[]{:S(2)}) collective-permute-start(bf16[64,2048]{1,0:T(8,128)(2,1)S(1)} %get-tuple-element.239), channel_id=1, source_target_pairs={{0,1},{2,0},{4,2},{6,4},{7,6},{5,7},{3,5},{1,3},{8,9},{10,8},{12,1... | collective-permute-start | bytes 786440 | tf_op jit(solution)/shard_map/ppermute | solution.py:76
  252.1 40.9 %collective-permute-start.23 = (bf16[128,2048]{1,0:T(8,128)(2,1)S(1)}, bf16[128,2048]{1,0:T(8,128)(2,1)S(1)}, u32[]{:S(2)}, u32[]{:S(2)}) collective-permute-start(bf16[128,2048]{1,0:T(8,128)(2,1)S(1)} %pad_add_fusion.5), channel_id=1, source_target_pairs={{0,1},{2,0},{4,2},{6,4},{7,6},{5,7},{3,5},{1,3},{8,9},{10,8},{12,1... | collective-permute-start | bytes 1572872 | tf_op jit(solution)/shard_map/ppermute | solution.py:76
  308.3 61.7 %collective-permute-start.30 = (bf16[704,2048]{1,0:T(8,128)(2,1)}, bf16[704,2048]{1,0:T(8,128)(2,1)}, u32[]{:S(2)}, u32[]{:S(2)}) collective-permute-start(bf16[704,2048]{1,0:T(8,128)(2,1)} %bitcast.147.gate_w), channel_id=1, source_target_pairs={{0,16},{8,24},{16,0},{24,8},{1,17},{9,25},{17,1},{25,9},{2,18},{10... | collective-permute-start | bytes 8650760 | tf_op jit(solution)/shard_map/ppermute | solution.py:141
  399.1 64.8 %collective-permute-start.42 = (bf16[704,2048]{1,0:T(8,128)(2,1)}, bf16[704,2048]{1,0:T(8,128)(2,1)}, u32[]{:S(2)}, u32[]{:S(2)}) collective-permute-start(bf16[704,2048]{1,0:T(8,128)(2,1)} %bitcast.149.up_w), channel_id=1, source_target_pairs={{0,16},{8,24},{16,0},{24,8},{1,17},{9,25},{17,1},{25,9},{2,18},{10... | collective-permute-start | bytes 8650760 | tf_op jit(solution)/shard_map/ppermute | solution.py:141
  416.5 47.4 %collective-permute-start.40 = (bf16[704,2048]{1,0:T(8,128)(2,1)}, bf16[704,2048]{1,0:T(8,128)(2,1)}, u32[]{:S(2)}, u32[]{:S(2)}) collective-permute-start(bf16[704,2048]{1,0:T(8,128)(2,1)} %bitcast.149.up_w), channel_id=1, source_target_pairs={{0,8},{8,0},{16,24},{24,16},{1,9},{9,1},{17,25},{25,17},{2,10},{10... | collective-permute-start | bytes 8650760 | tf_op jit(solution)/shard_map/ppermute | solution.py:135
  425.2 51.8 %collective-permute-start.54 = (bf16[128,2048]{1,0:T(8,128)(2,1)S(1)}, bf16[128,2048]{1,0:T(8,128)(2,1)}, u32[]{:S(2)}, u32[]{:S(2)}) collective-permute-start(bf16[128,2048]{1,0:T(8,128)(2,1)S(1)} %copy-done.14), channel_id=1, source_target_pairs={{0,2},{2,4},{4,6},{6,7},{7,5},{5,3},{3,1},{1,0},{8,10},{10,12},{12... | collective-permute-start | bytes 1572872 | tf_op jit(solution)/shard_map/ppermute | solution.py:76
  429.5 50.1 %collective-permute-start.58 = (bf16[128,2048]{1,0:T(8,128)(2,1)S(1)}, bf16[128,2048]{1,0:T(8,128)(2,1)S(1)}, u32[]{:S(2)}, u32[]{:S(2)}) collective-permute-start(bf16[128,2048]{1,0:T(8,128)(2,1)S(1)} %copy-done.14), channel_id=1, source_target_pairs={{0,1},{2,0},{4,2},{6,4},{7,6},{5,7},{3,5},{1,3},{8,9},{10,8},{12,1... | collective-permute-start | bytes 1572872 | tf_op jit(solution)/shard_map/ppermute | solution.py:76
  430.4 93.2 %collective-permute-start.45 = (bf16[704,2048]{1,0:T(8,128)(2,1)}, bf16[704,2048]{1,0:T(8,128)(2,1)}, u32[]{:S(2)}, u32[]{:S(2)}) collective-permute-start(bf16[704,2048]{1,0:T(8,128)(2,1)} %collective-permute-done.21.down_w), channel_id=1, source_target_pairs={{0,8},{8,0},{16,24},{24,16},{1,9},{9,1},{17,25},{25,17},{2,10},{10... | collective-permute-start | bytes 8650760 | tf_op jit(solution)/shard_map/ppermute | solution.py:135
  463.9 59.7 %collective-permute-start.43 = (bf16[704,2048]{1,0:T(8,128)(2,1)}, bf16[704,2048]{1,0:T(8,128)(2,1)}, u32[]{:S(2)}, u32[]{:S(2)}) collective-permute-start(bf16[704,2048]{1,0:T(8,128)(2,1)} %collective-permute-done.30.gate_w), channel_id=1, source_target_pairs={{0,8},{8,0},{16,24},{24,16},{1,9},{9,1},{17,25},{25,17},{2,10},{10... | collective-permute-start | bytes 8650760 | tf_op jit(solution)/shard_map/ppermute | solution.py:135
  463.9 59.7 %collective-permute-start.44 = (bf16[704,2048]{1,0:T(8,128)(2,1)}, bf16[704,2048]{1,0:T(8,128)(2,1)}, u32[]{:S(2)}, u32[]{:S(2)}) collective-permute-start(bf16[704,2048]{1,0:T(8,128)(2,1)} %collective-permute-done.42.up_w), channel_id=1, source_target_pairs={{0,8},{8,0},{16,24},{24,16},{1,9},{9,1},{17,25},{25,17},{2,10},{10... | collective-permute-start | bytes 8650760 | tf_op jit(solution)/shard_map/ppermute | solution.py:135
  577.5 63.9 %collective-permute-start.62 = (bf16[704,2048]{1,0:T(8,128)(2,1)}, bf16[704,2048]{1,0:T(8,128)(2,1)}, u32[]{:S(2)}, u32[]{:S(2)}) collective-permute-start(bf16[704,2048]{1,0:T(8,128)(2,1)} %convolution_convert_fusion.13), channel_id=1, source_target_pairs={{0,8},{8,0},{16,24},{24,16},{1,9},{9,1},{17,25},{25,17},{2,10},{10... | collective-permute-start | bytes 8650760 | tf_op jit(solution)/shard_map/ppermute | solution.py:135
  751.5 108.9 %collective-permute-start.93 = (bf16[704,2048]{1,0:T(8,128)(2,1)}, bf16[704,2048]{1,0:T(8,128)(2,1)}, u32[]{:S(2)}, u32[]{:S(2)}) collective-permute-start(bf16[704,2048]{1,0:T(8,128)(2,1)} %convolution_convert_fusion.4), channel_id=1, source_target_pairs={{0,8},{8,0},{16,24},{24,16},{1,9},{9,1},{17,25},{25,17},{2,10},{10... | collective-permute-start | bytes 8650760 | tf_op jit(solution)/shard_map/ppermute | solution.py:135
  771.1 102.0 %collective-permute-start.92 = (bf16[704,2048]{1,0:T(8,128)(2,1)}, bf16[704,2048]{1,0:T(8,128)(2,1)}, u32[]{:S(2)}, u32[]{:S(2)}) collective-permute-start(bf16[704,2048]{1,0:T(8,128)(2,1)} %convolution_convert_fusion.6), channel_id=1, source_target_pairs={{0,8},{8,0},{16,24},{24,16},{1,9},{9,1},{17,25},{25,17},{2,10},{10... | collective-permute-start | bytes 8650760 | tf_op jit(solution)/shard_map/ppermute | solution.py:135
  779.1 118.3 %all-to-all-start.3 = ((bf16[8,704,256]{2,1,0:T(8,128)(2,1)}), bf16[8,704,256]{2,1,0:T(8,128)(2,1)}, u32[]{:S(2)}, u32[]{:S(2)}) async-start(bf16[8,704,256]{2,1,0:T(8,128)(2,1)} %bitcast.335), calls=%async_computation.3 | async-start | bytes 5767168 | tf_op jit(solution)/shard_map/all_to_all | solution.py:195
  783.9 45.1 %collective-permute-start.88 = (bf16[128,2048]{1,0:T(8,128)(2,1)S(1)}, bf16[128,2048]{1,0:T(8,128)(2,1)S(1)}, u32[]{:S(2)}, u32[]{:S(2)}) collective-permute-start(bf16[128,2048]{1,0:T(8,128)(2,1)S(1)} %fusion.57), channel_id=1, source_target_pairs={{0,1},{2,0},{4,2},{6,4},{7,6},{5,7},{3,5},{1,3},{8,9},{10,8},{12,1... | collective-permute-start | bytes 1572872 | tf_op jit(solution)/shard_map/ppermute | solution.py:76
  785.8 57.3 %collective-permute-start.82 = (bf16[128,2048]{1,0:T(8,128)(2,1)S(1)}, bf16[128,2048]{1,0:T(8,128)(2,1)S(1)}, u32[]{:S(2)}, u32[]{:S(2)}) collective-permute-start(bf16[128,2048]{1,0:T(8,128)(2,1)S(1)} %fusion.57), channel_id=1, source_target_pairs={{0,2},{2,4},{4,6},{6,7},{7,5},{5,3},{3,1},{1,0},{8,10},{10,12},{12... | collective-permute-start | bytes 1572872 | tf_op jit(solution)/shard_map/ppermute | solution.py:76
  791.4 73.3 %collective-permute-start.85 = (bf16[352,2048]{1,0:T(8,128)(2,1)S(1)}, bf16[352,2048]{1,0:T(8,128)(2,1)S(1)}, u32[]{:S(2)}, u32[]{:S(2)}) collective-permute-start(bf16[352,2048]{1,0:T(8,128)(2,1)S(1)} %copy-done.31), channel_id=1, source_target_pairs={{0,16},{8,24},{16,0},{24,8},{1,17},{9,25},{17,1},{25,9},{2,18},{10... | collective-permute-start | bytes 4325384 | tf_op jit(solution)/shard_map/ppermute | solution.py:141
  829.0 41.4 %collective-permute-start.89 = (bf16[128,2048]{1,0:T(8,128)(2,1)S(1)}, bf16[128,2048]{1,0:T(8,128)(2,1)S(1)}, u32[]{:S(2)}, u32[]{:S(2)}) collective-permute-start(bf16[128,2048]{1,0:T(8,128)(2,1)S(1)} %collective-permute-done.88), channel_id=1, source_target_pairs={{0,1},{2,0},{4,2},{6,4},{7,6},{5,7},{3,5},{1,3},{8,9},{10,8},{12,1... | collective-permute-start | bytes 1572872 | tf_op jit(solution)/shard_map/ppermute | solution.py:76
  896.8 88.2 %collective-permute-start.95 = (bf16[352,2048]{1,0:T(8,128)(2,1)}, bf16[352,2048]{1,0:T(8,128)(2,1)}, u32[]{:S(2)}, u32[]{:S(2)}) collective-permute-start(bf16[352,2048]{1,0:T(8,128)(2,1)} %get-tuple-element.191), channel_id=1, source_target_pairs={{0,16},{8,24},{16,0},{24,8},{1,17},{9,25},{17,1},{25,9},{2,18},{10... | collective-permute-start | bytes 4325384 | tf_op jit(solution)/shard_map/ppermute | solution.py:141
  900.9 114.7 %all-to-all-start.4 = ((bf16[8,704,256]{2,1,0:T(8,128)(2,1)}), bf16[8,704,256]{2,1,0:T(8,128)(2,1)}, u32[]{:S(2)}, u32[]{:S(2)}) async-start(bf16[8,704,256]{2,1,0:T(8,128)(2,1)} %bitcast.334), calls=%async_computation.4 | async-start | bytes 5767168 | tf_op jit(solution)/shard_map/all_to_all | solution.py:195
  990.7 62.0 %collective-permute-start.130 = (bf16[704,2048]{1,0:T(8,128)(2,1)}, bf16[704,2048]{1,0:T(8,128)(2,1)}, u32[]{:S(2)}, u32[]{:S(2)}) collective-permute-start(bf16[704,2048]{1,0:T(8,128)(2,1)} %convolution_convert_fusion.2), channel_id=1, source_target_pairs={{0,8},{8,0},{16,24},{24,16},{1,9},{9,1},{17,25},{25,17},{2,10},{10... | collective-permute-start | bytes 8650760 | tf_op jit(solution)/shard_map/ppermute | solution.py:135
  1020.4 81.3 %collective-permute-start.123 = (bf16[256,2048]{1,0:T(8,128)(2,1)}, bf16[256,2048]{1,0:T(8,128)(2,1)}, u32[]{:S(2)}, u32[]{:S(2)}) collective-permute-start(bf16[256,2048]{1,0:T(8,128)(2,1)} %get-tuple-element.224), channel_id=1, source_target_pairs={{0,8},{8,0},{16,24},{24,16},{1,9},{9,1},{17,25},{25,17},{2,10},{10... | collective-permute-start | bytes 3145736 | tf_op jit(solution)/shard_map/ppermute | solution.py:135
  1020.4 42.1 %collective-permute-start.100 = (bf16[64,2048]{1,0:T(8,128)(2,1)}, bf16[64,2048]{1,0:T(8,128)(2,1)}, u32[]{:S(2)}, u32[]{:S(2)}) collective-permute-start(bf16[64,2048]{1,0:T(8,128)(2,1)} %get-tuple-element.228), channel_id=1, source_target_pairs={{0,2},{2,4},{4,6},{6,7},{7,5},{5,3},{3,1},{1,0},{8,10},{10,12},{12... | collective-permute-start | bytes 786440 | tf_op jit(solution)/shard_map/ppermute | solution.py:76
  1045.7 73.2 %all-to-all-start.5 = ((bf16[8,384,256]{2,1,0:T(8,128)(2,1)}), bf16[8,384,256]{2,1,0:T(8,128)(2,1)S(1)}, u32[]{:S(2)}, u32[]{:S(2)}) async-start(bf16[8,384,256]{2,1,0:T(8,128)(2,1)} %add_convert_fusion.8), calls=%async_computation.5 | async-start | bytes 3145728 | tf_op jit(solution)/shard_map/all_to_all | solution.py:195
  1060.5 67.2 %collective-permute-start.122 = (bf16[256,2048]{1,0:T(8,128)(2,1)}, bf16[256,2048]{1,0:T(8,128)(2,1)}, u32[]{:S(2)}, u32[]{:S(2)}) collective-permute-start(bf16[256,2048]{1,0:T(8,128)(2,1)} %get-tuple-element.223), channel_id=1, source_target_pairs={{0,8},{8,0},{16,24},{24,16},{1,9},{9,1},{17,25},{25,17},{2,10},{10... | collective-permute-start | bytes 3145736 | tf_op jit(solution)/shard_map/ppermute | solution.py:135
  1060.6 57.2 %collective-permute-start.129 = (f32[5,2048]{1,0:T(8,128)S(1)}, f32[5,2048]{1,0:T(8,128)S(1)}, u32[]{:S(2)}, u32[]{:S(2)}) collective-permute-start(f32[5,2048]{1,0:T(8,128)S(1)} %add.433), channel_id=1, source_target_pairs={{0,4},{1,5},{2,6},{3,7},{4,0},{5,1},{6,2},{7,3},{8,12},{9,13},{10,... | collective-permute-start | bytes 122888 | tf_op jit(solution)/shard_map/ppermute | solution.py:203
  (172 other events, 2592.2 us)

commit v2 on v1

v2 whole, which is shorter than its diff:
```python
import functools

import jax
import jax.numpy as jnp
from jax import lax
from jax.experimental import pallas as pl
from jax.experimental.pallas import tpu as pltpu
from jax.sharding import PartitionSpec as P

HD = 128


EPS = 1e-05
THETA = 10000.0
NEG = -1e30
F32 = jnp.float32
BF16 = jnp.bfloat16
VMEM_LIMIT = 60 * 1024 * 1024


def dot(left, right, contract=((1,), (0,))):
    return lax.dot_general(left, right, (contract, ((), ())), preferred_element_type=F32)


def norm_rows(values, norm_gain):
    row_scale = lax.rsqrt(jnp.mean(values * values, axis=-1, keepdims=True) + EPS)
    return (values * row_scale * norm_gain, row_scale)


def norm_back(grad_rows, values, row_scale, norm_gain):
    gain_grad = jnp.sum(grad_rows * values * row_scale, axis=0)
    scaled_grad = grad_rows * norm_gain
    mean_term = jnp.mean(scaled_grad * values, axis=-1, keepdims=True)
    return (
        row_scale * scaled_grad - values * row_scale * row_scale * row_scale * mean_term,
        gain_grad,
    )


def seq_of(places, lengths):
    seq_ends = jnp.cumsum(lengths)
    passed = seq_ends[None, :] <= places[:, None]
    return (passed, jnp.sum(passed.astype(jnp.int32), axis=1))


def rope_tables(places, lengths):
    passed, seq_ids = seq_of(places, lengths)
    starts = jnp.sum(jnp.where(passed, lengths[None, :], 0), axis=1)
    where_in = (places - starts).astype(F32)
    frequency = THETA ** (-jnp.arange(0, HD // 2, dtype=F32) * (2.0 / HD))
    angles = where_in[:, None] * frequency[None, :]
    return (jnp.cos(angles), jnp.sin(angles), seq_ids)


def rotate(values, cosine, sine_table):
    half_width = values.shape[-1] // 2
    leading = values[..., :half_width]
    trailing = values[..., half_width:]
    return jnp.concatenate(
        [leading * cosine - trailing * sine_table, trailing * cosine + leading * sine_table],
        axis=-1,
    )


def ring_cycle(count):
    if count == 8:
        return [0, 2, 4, 6, 7, 5, 3, 1]
    if count == 16:
        return [0, 1, 2, 3, 7, 6, 5, 9, 10, 11, 15, 14, 13, 12, 8, 4]
    return list(range(count))


def ring_move(value, hops):
    cycle = ring_cycle(lax.axis_size("shard"))
    count = len(cycle)
    return lax.ppermute(
        value, "shard", [(cycle[i], cycle[(i + hops) % count]) for i in range(count)]
    )


def after(value, *others):
    return lax.optimization_barrier((value,) + others)[0] if others else value


class Transfer:
    def __init__(self, move, source, value=None):
        self.move, self.source, self.value = move, source, value

    def begin(self):
        self.value = self.move(self.value)


def tie(values, others):
    if len(values) + len(others) < 2:
        return list(values)
    held = [item.value if isinstance(item, Transfer) else item for item in others]
    tied = lax.optimization_barrier((*values, *held))
    for item, value in zip(others, tied[len(values) :]):
        if isinstance(item, Transfer):
            item.value = value
    return list(tied[: len(values)])


def begin(values, transfers):
    for item in transfers:
        item.value = item.source()
    values = tie(values, transfers)
    for item in transfers:
        item.begin()
    return values


class RingGather:
    def __init__(self, block):
        self.ahead, self.behind = [block], [block]
        self.last = []

    def tie(self, values, begins=(), ends=()):
        heads = self.last or [self.ahead[-1], self.behind[-1]]
        for item in begins:
            item.value = item.source()
        tied = tie([*heads, *values], [*begins, *ends])
        if self.last:
            self.last = tied[:2]
        else:
            self.ahead[-1], self.behind[-1] = tied[:2]
        for item in begins:
            item.begin()
        return tied[2:]

    def step(self):
        far = lax.axis_size("shard") // 2
        if len(self.ahead) < far:
            self.ahead.append(ring_move(self.ahead[-1], 1))
            self.behind.append(ring_move(self.behind[-1], -1))
        elif not self.last:
            cut = self.ahead[0].shape[0] // 2
            self.last = [ring_move(self.ahead[-1][:cut], 1), ring_move(self.behind[-1][cut:], -1)]

    def blocks(self):
        while not self.last:
            self.step()
        return self.ahead + self.last + self.behind[:0:-1]


class RingScatter:
    def __init__(self, partial):
        count = lax.axis_size("shard")
        rows = partial.shape[0] // count
        self.far, self.done = count // 2, 0
        self.part = [partial[r * rows : (r + 1) * rows] for r in range(count)]
        cut = rows // 2
        self.back, self.fore = self.part[self.far][:cut], self.part[self.far][cut:]

    def tie(self, values, begins=(), ends=()):
        for item in begins:
            item.value = item.source()
        tied = tie([self.back, self.fore, *values], [*begins, *ends])
        self.back, self.fore = tied[:2]
        for item in begins:
            item.begin()
        return tied[2:]

    def step(self):
        if self.done == self.far:
            return
        self.back, self.fore = ring_move(self.back, -1), ring_move(self.fore, 1)
        if self.done == 0:
            empty = jnp.zeros_like(self.back)
            self.back = jnp.concatenate([self.back, empty], axis=0)
            self.fore = jnp.concatenate([empty, self.fore], axis=0)
        if self.done < self.far - 1:
            self.back = self.part[self.far - 1 - self.done] + self.back
            self.fore = self.part[self.far + 1 + self.done] + self.fore
        self.done += 1

    def total(self):
        while self.done < self.far:
            self.step()
        return self.part[0].astype(F32) + self.back.astype(F32) + self.fore.astype(F32)


def ring_gather(block, plan={}):
    ring = RingGather(block)
    for step in range(lax.axis_size("shard") // 2):
        begins, ends = plan.get(step, ((), ()))
        ring.tie([], begins)
        ring.step()
        ring.tie([], (), ends)
    return ring.blocks()


def ring_scatter(partial, plan={}):
    ring = RingScatter(partial)
    for step in range(lax.axis_size("shard") // 2):
        begins, ends = plan.get(step, ((), ()))
        ring.tie([], begins)
        ring.step()
        ring.tie([], (), ends)
    return ring.total()


def direct_gather(block):
    count = lax.axis_size("shard")
    return jnp.stack([block] + [ring_move(block, r) for r in range(1, count)])


def core_swap(value):
    return lax.ppermute(value, "expert", [(i, i ^ 1) for i in range(lax.axis_size("expert"))])


def chip_shift(value, hops):
    count = lax.axis_size("expert")
    chips = count // 2
    return lax.ppermute(
        value, "expert", [(i, (i // 2 + hops) % chips * 2 + i % 2) for i in range(count)]
    )


def expert_order():
    index = lax.axis_index("expert")
    chips = lax.axis_size("expert") // 2
    return [
        (index // 2 + dx) % chips * 2 + (index % 2 + dc) % 2
        for dx in range(chips)
        for dc in range(2)
    ]


def expert_gather(value):
    chips = lax.axis_size("expert") // 2
    own = [value] + [chip_shift(value, -dx) for dx in range(1, chips)]
    return [piece for item in own for piece in (item, core_swap(item))]


def after_all(values, *others):
    return [after(item, *others) for item in values]


PARTS = 4


def part_of(value, which, parts=PARTS):
    size = value.shape[1 if value.ndim == 2 else 0] // parts
    here = slice(which * size, (which + 1) * size)
    return value[:, here] if value.ndim == 2 else value[here]


def fetch_far(source, which=0, parts=1):
    chips = lax.axis_size("expert") // 2
    take = lambda: part_of(source(), which, parts)
    return [Transfer(lambda v, dx=dx: chip_shift(v, -dx), take) for dx in range(1, chips)]


def hand_far(source, which=0, parts=1):
    chips = lax.axis_size("expert") // 2
    return [
        Transfer(
            lambda v, dx=dx: chip_shift(v, dx), lambda dx=dx: part_of(source()[dx - 1], which, parts)
        )
        for dx in range(1, chips)
    ]


def total_of(near, parts):
    came = [sum_f32([item.value for item in part]) for part in parts]
    return near + jnp.concatenate(came, axis=1)


def with_swaps(items):
    return [piece for item in items for piece in (item, core_swap(item))]


def expert_sums(pieces, firsts):
    return [
        (pieces[k].astype(F32) + core_swap(pieces[k + 1]).astype(F32)).astype(BF16) for k in firsts
    ]


def far_exchange(sums):
    return [chip_shift(item, dx + 1) for dx, item in enumerate(sums)]


def sum_f32(parts):
    return sum(item.astype(F32) for item in parts)


def expert_reduce(pieces):
    sums = expert_sums(pieces, range(0, len(pieces), 2))
    return sum_f32(sums[:1] + far_exchange(sums[1:]))


def shard_exchange(pieces):
    return lax.all_to_all(pieces, "shard", split_axis=0, concat_axis=0, tiled=True)


def sum_pairs(value, axis, step):
    count = lax.axis_size(axis)
    return value + lax.ppermute(value, axis, [(i, i ^ step) for i in range(count)])


def powers(count):
    return [1 << i for i in range(count.bit_length() - 1)]


def turn(values, cosine, sine_table):
    return values * cosine + pltpu.roll(values, HD // 2, 1) * sine_table


def whole(shape):
    zeros = (0,) * len(shape)
    return pl.BlockSpec(shape, lambda *_: zeros, pipeline_mode=pl.Buffered(1))


def tiles(shape):
    return pl.BlockSpec(shape, lambda i: (i,) + (0,) * (len(shape) - 1))


def named_by(routes, order, slot, k):
    return (routes[:, slot : slot + 1] == order[0, k]).astype(F32)


def columns(parts):
    lane = lax.broadcasted_iota(jnp.int32, (parts[0].shape[0], len(parts)), 1)
    total = jnp.zeros(lane.shape, F32)
    for k, part in enumerate(parts):
        total = jnp.where(lane == k, part, total)
    return total


def lay(blocks, target):
    start = 0
    for block in blocks:
        target[start : start + block.shape[0], :] = block[...]
        start += block.shape[0]


def cost(microseconds):
    return pl.CostEstimate(flops=microseconds * 115 * 10**6, bytes_accessed=1 << 16, transcendentals=0)


def attend_kernel(layout, count, chunk, order, *refs):
    blocks, refs = refs[:count], refs[count:]
    (first_w,), refs = regroup(refs, [layout])
    experts = len(layout)
    out_w, refs = refs[:experts], refs[experts:]
    router, routes_ref, bounds, place_row, cosine, sine_table = refs[:6]
    mixed, query_out, keys, values, wide, gates_out, hidden, kv_w = refs[6:]
    step = pl.program_id(0)
    tile = mixed.shape[0]
    total_rows, span = keys.shape
    width = hidden.shape[1]
    shards = sum(piece.shape[0] for piece in first_w[0])
    depth = width // shards

    @pl.when(step == 0)
    def _():
        lay(blocks, hidden)
        for k in range(experts):
            for s, block in enumerate([piece.at[i] for piece in first_w[k] for i in range(piece.shape[0])]):
                to = pl.ds(pl.multiple_of(s * depth + order[0, k] * chunk, chunk), chunk)
                for half in range(2):
                    kv_w[half, to, :] = block[depth + half * chunk : depth + (half + 1) * chunk, :]

        @pl.loop(0, total_rows // tile)
        def _(i):
            here = pl.ds(pl.multiple_of(i * tile, tile), tile)
            raw = dot(hidden[here, :], kv_w[0])
            for h in range(span // HD):
                cols = slice(h * HD, (h + 1) * HD)
                keys[here, cols] = turn(raw[:, cols], cosine[here, :], sine_table[here, :]).astype(BF16)
            values[here, :] = dot(hidden[here, :], kv_w[1]).astype(BF16)

    here = pl.ds(pl.multiple_of(step * tile, tile), tile)
    rows_in = hidden[here, :]
    routes = routes_ref[...]
    hot = [[named_by(routes, order, j, k) for k in range(experts)] for j in range(2)]
    logits = dot(rows_in, router[...])
    picked = [sum(hot[j][k] * logits[:, k : k + 1] for k in range(experts)) for j in range(2)]
    top = jnp.maximum(picked[0], picked[1])
    raised = [jnp.exp(value - top) for value in picked]
    gates = [value / (raised[0] + raised[1]) for value in raised]
    gates_out[...] = columns([hot[0][k] * gates[0] + hot[1][k] * gates[1] for k in range(experts)])
    query_all = []
    for pieces in first_w:
        at, total = 0, 0.0
        for piece in pieces:
            size = piece.shape[0] * depth
            total = total + dot(rows_in[:, at : at + size], piece[:, :depth, :].reshape(size, span))
            at += size
        query_all.append(total)
    allowed = (place_row[...] >= bounds[:, 0:1]) & (place_row[...] <= bounds[:, 1:2])
    cos_here, sin_here = cosine[here, :], sine_table[here, :]
    vectors = []
    for j in range(2):
        raw = sum(hot[j][k] * query_all[k] for k in range(experts))
        heads = []
        for h in range(span // HD):
            cols = slice(h * HD, (h + 1) * HD)
            query = turn(raw[:, cols], cos_here, sin_here).astype(BF16)
            query_out[:, j * span + h * HD : j * span + (h + 1) * HD] = query
            scores = dot(query, keys[:, cols], ((1,), (1,))) * HD**-0.5
            scores = jnp.where(allowed, scores, NEG)
            row_top = jnp.max(scores, axis=1, keepdims=True)
            exp_scores = jnp.exp(scores - row_top)
            row_total = jnp.sum(exp_scores, axis=1, keepdims=True)
            heads.append(dot(exp_scores.astype(BF16), values[:, cols]) / row_total)
        vectors.append((jnp.concatenate(heads, axis=1) if len(heads) > 1 else heads[0]) * gates[j])
    total = 0.0
    for k in range(experts):
        part = (hot[0][k] * vectors[0] + hot[1][k] * vectors[1]).astype(BF16)
        wide[:, k * span : (k + 1) * span] = part
        total = total + dot(part, out_w[k][...])
    mixed[...] = total.astype(BF16)


def attend(blocks, first_w, out_w, router, routes, order, bounds, place_row, cosine, sine_table, chunk):
    total_rows, width = routes.shape[0], blocks[0].shape[1]
    experts = len(first_w)
    span = first_w[0][0].shape[2]
    layout = [len(pieces) for pieces in first_w]
    first_w = [piece for pieces in first_w for piece in pieces]
    tile = 256

    def struct(*shape):
        return jax.ShapeDtypeStruct(shape, BF16)

    return pl.pallas_call(
        functools.partial(attend_kernel, layout, len(blocks), chunk),
        grid=(total_rows // tile,),
        in_specs=[pl.BlockSpec(memory_space=pltpu.SMEM)]
        + [whole(w.shape) for w in [*blocks, *first_w, *out_w, router]]
        + [
            tiles((tile, 2)),
            tiles((tile, 2)),
            whole(place_row.shape),
            whole(cosine.shape),
            whole(sine_table.shape),
        ],
        out_specs=[
            tiles((tile, width)),
            tiles((tile, 2 * span)),
            whole((total_rows, span)),
            whole((total_rows, span)),
            tiles((tile, experts * span)),
            tiles((tile, experts)),
            whole((total_rows, width)),
            whole((2, width, span)),
        ],
        out_shape=[
            struct(total_rows, width),
            struct(total_rows, 2 * span),
            struct(total_rows, span),
            struct(total_rows, span),
            struct(total_rows, experts * span),
            jax.ShapeDtypeStruct((total_rows, experts), F32),
            struct(total_rows, width),
            struct(2, width, span),
        ],
        compiler_params=pltpu.CompilerParams(vmem_limit_bytes=VMEM_LIMIT),
        cost_estimate=cost(35),
        name="attend",
    )(order, *blocks, *first_w, *out_w, router, routes, bounds, place_row, cosine, sine_table)


def attend_back_kernel(layout, steps, count, order, *refs):
    blocks, refs = refs[:count], refs[count:]
    (first_w,), refs = regroup(refs, [layout])
    experts = len(layout)
    kv_w, refs = refs[0], refs[1:]
    out_w, refs = refs[:experts], refs[experts:]
    router, hidden, refs = refs[0], refs[1], refs[2:]
    routes_ref, gates_ref, bounds_row, place_col, cosine, sine_table, query_ref, keys, values, wide = refs[:10]
    grad_rows, grad_first, small, grad_mid, key_sum, value_sum, logit_grads = refs[10:]
    step = pl.program_id(0)
    tile = grad_rows.shape[0]
    total_rows, span = keys.shape

    @pl.when(step == 0)
    def _():
        lay(blocks, grad_mid)
        small[...] = jnp.zeros_like(small)
        key_sum[...] = jnp.zeros_like(key_sum)
        value_sum[...] = jnp.zeros_like(value_sum)

    @pl.when(step < steps)
    def _():
        here = pl.ds(pl.multiple_of(step * tile, tile), tile)
        routes = routes_ref[here, :]
        gates = gates_ref[here, :]
        hot = [[named_by(routes, order, j, k) for k in range(experts)] for j in range(2)]
        allowed = (place_col[...] >= bounds_row[0:1, here]) & (place_col[...] <= bounds_row[1:2, here])
        rows_in = grad_mid[here, :]
        slot_grads = [0.0, 0.0]
        sums = []
        for k in range(experts):
            grad = dot(rows_in, out_w[k][...], ((1,), (1,)))
            part = wide[:, k * span : (k + 1) * span].astype(F32)
            sums.append(jnp.sum(part * grad, axis=1, keepdims=True))
            for j in range(2):
                slot_grads[j] = slot_grads[j] + (hot[j][k] * gates[:, k : k + 1]) * grad
        sums = columns(sums)
        wide_grads = sums - gates * jnp.sum(sums, axis=1, keepdims=True)
        wide_grads = jnp.concatenate([wide_grads, jnp.zeros((tile, HD - experts), F32)], axis=1)
        logit_grads[here, :] = wide_grads.astype(BF16)
        cos_here, sin_here = cosine[here, :], sine_table[here, :]
        slot_queries = []
        for j in range(2):
            heads = []
            for h in range(span // HD):
                cols = slice(h * HD, (h + 1) * HD)
                query = query_ref[:, j * span + h * HD : j * span + (h + 1) * HD]
                grad = slot_grads[j][:, cols].astype(BF16)
                scores = dot(keys[:, cols], query, ((1,), (1,))) * HD**-0.5
                scores = jnp.where(allowed, scores, NEG)
                exp_scores = jnp.exp(scores - jnp.max(scores, axis=0, keepdims=True))
                probs = exp_scores * (1.0 / jnp.sum(exp_scores, axis=0, keepdims=True))
                value_sum[:, cols] += dot(probs.astype(BF16), grad)
                grad_probs = dot(values[:, cols], grad, ((1,), (1,)))
                mean = jnp.sum(probs * grad_probs, axis=0, keepdims=True)
                grad_scores = (probs * (grad_probs - mean)).astype(BF16)
                key_sum[:, cols] += dot(grad_scores, query)
                grad_query = dot(grad_scores, keys[:, cols], ((0,), (0,))) * HD**-0.5
                heads.append(turn(grad_query, cos_here, -sin_here))
            slot_queries.append(jnp.concatenate(heads, axis=1) if len(heads) > 1 else heads[0])
        for k in range(experts):
            grad_first[here, k * span : (k + 1) * span] = (
                hot[0][k] * slot_queries[0] + hot[1][k] * slot_queries[1]
            ).astype(BF16)

    @pl.when(step == steps - 1)
    def _():
        for h in range(span // HD):
            cols = slice(h * HD, (h + 1) * HD)
            grad_first[:, experts * span + h * HD : experts * span + (h + 1) * HD] = turn(
                key_sum[:, cols] * HD**-0.5, cosine[...], -sine_table[...]
            ).astype(BF16)
        grad_first[:, (experts + 1) * span :] = value_sum[...].astype(BF16)

    @pl.when(step >= steps)
    def _():
        here = pl.ds(pl.multiple_of((step - steps) * tile, tile), tile)
        total = dot(grad_first[here, experts * span : (experts + 1) * span], kv_w[0], ((1,), (1,)))
        total = total + dot(grad_first[here, (experts + 1) * span :], kv_w[1], ((1,), (1,)))
        total = total + dot(logit_grads[here, :], router[...], ((1,), (1,)))
        width = total.shape[1]
        depth = width // sum(piece.shape[0] for piece in first_w[0])
        for k, pieces in enumerate(first_w):
            grad = grad_first[here, k * span : (k + 1) * span]
            back = [
                dot(grad, piece[:, :depth, :].reshape(piece.shape[0] * depth, span), ((1,), (1,)))
                for piece in pieces
            ]
            total = total + (jnp.concatenate(back, axis=1) if len(back) > 1 else back[0])
        grad_rows[...] = total.astype(BF16)
        rows_in = hidden[...]
        small[:-8, :] += dot(logit_grads[here, :], rows_in, ((0,), (0,)))[: small.shape[0] - 8, :]
        small[-8:, :] += jnp.sum((total * rows_in.astype(F32)).reshape(-1, 8, total.shape[1]), axis=0)


def attend_back(
    blocks, first_w, kv_w, out_w, router, hidden, routes, order, gates, bounds_row, place_col, cosine,
    sine_table, query, keys, values, wide,
):
    small_rows = -(-len(first_w) // 8) * 8 + 8
    total_rows, width = routes.shape[0], blocks[0].shape[1]
    experts = len(first_w)
    span = first_w[0][0].shape[2]
    layout = [len(pieces) for pieces in first_w]
    first_w = [piece for pieces in first_w for piece in pieces]
    tile = 256 if total_rows <= 1024 else 128
    steps = total_rows // tile

    def early(shape):
        return pl.BlockSpec(shape, lambda i: (jnp.minimum(i, steps - 1), 0))

    return pl.pallas_call(
        functools.partial(attend_back_kernel, layout, steps, len(blocks)),
        grid=(2 * steps,),
        in_specs=[pl.BlockSpec(memory_space=pltpu.SMEM)]
        + [whole(w.shape) for w in [*blocks, *first_w, kv_w, *out_w, router]]
        + [pl.BlockSpec((tile, width), lambda i: (jnp.maximum(i - steps, 0), 0))]
        + [
            whole(routes.shape),
            whole(gates.shape),
            whole(bounds_row.shape),
            whole(place_col.shape),
            whole(cosine.shape),
            whole(sine_table.shape),
            early((tile, 2 * span)),
            whole(keys.shape),
            whole(values.shape),
            early((tile, experts * span)),
        ],
        out_specs=[
            pl.BlockSpec((tile, width), lambda i: (jnp.maximum(i - steps, 0), 0)),
            whole((total_rows, (experts + 2) * span)),
            whole((small_rows, width)),
            whole((total_rows, width)),
        ],
        out_shape=[
            jax.ShapeDtypeStruct((total_rows, width), BF16),
            jax.ShapeDtypeStruct((total_rows, (experts + 2) * span), BF16),
            jax.ShapeDtypeStruct((small_rows, width), F32),
            jax.ShapeDtypeStruct((total_rows, width), BF16),
        ],
        scratch_shapes=[
            pltpu.VMEM((total_rows, span), F32),
            pltpu.VMEM((total_rows, span), F32),
            pltpu.VMEM((total_rows, HD), BF16),
        ],
        compiler_params=pltpu.CompilerParams(vmem_limit_bytes=VMEM_LIMIT),
        cost_estimate=cost(45),
        name="attend_back",
    )(
        order, *blocks, *first_w, kv_w, *out_w, router, hidden, routes, gates, bounds_row, place_col, cosine,
        sine_table, query, keys, values, wide,
    )


def split_kernel(block, gate, up):
    half = block.shape[1] // 2
    gate[...] = block[:, :half].T.reshape(gate.shape)
    up[...] = block[:, half:].T.reshape(up.shape)


def split_columns(weight, shards):
    depth, both = weight.shape
    inner = both // (2 * shards)
    tile = 128
    out = jax.ShapeDtypeStruct((shards, inner, depth), BF16)
    spec = pl.BlockSpec((shards, inner, tile), lambda i: (0, 0, i))
    return pl.pallas_call(
        split_kernel,
        grid=(depth // tile,),
        in_specs=[tiles((tile, both))],
        out_specs=[spec, spec],
        out_shape=[out, out],
        compiler_params=pltpu.CompilerParams(vmem_limit_bytes=VMEM_LIMIT),
        cost_estimate=cost(5),
        name="split_columns",
    )(weight)


def join_kernel(gate, up, out):
    shards, inner, tile = gate.shape
    half = shards * inner
    out[:, :half] = gate[...].reshape(half, tile).T.astype(F32)
    out[:, half:] = up[...].reshape(half, tile).T.astype(F32)


def join_columns(gate, up):
    shards, inner, depth = gate.shape
    tile = 128
    spec = pl.BlockSpec((shards, inner, tile), lambda i: (0, 0, i))
    return pl.pallas_call(
        join_kernel,
        grid=(depth // tile,),
        in_specs=[spec, spec],
        out_specs=tiles((tile, 2 * shards * inner)),
        out_shape=jax.ShapeDtypeStruct((depth, 2 * shards * inner), F32),
        compiler_params=pltpu.CompilerParams(vmem_limit_bytes=VMEM_LIMIT),
        cost_estimate=cost(7),
        name="join_columns",
    )(gate, up)


def dispatch_kernel(capacity, count, gated, rank, *refs):
    blocks, refs = refs[:count], refs[count:]
    if gated:
        router, out, gates_out, hidden = refs
    else:
        out, hidden = refs
    step = pl.program_id(0)
    _, experts, rows = rank.shape

    @pl.when(step == 0)
    def _():
        lay(blocks, hidden)

    rows_in = hidden[pl.ds(pl.multiple_of(step * rows, rows), rows), :]
    ranks = rank[0]
    slot = lax.broadcasted_iota(jnp.int32, (capacity, rows), 0)
    pick = jnp.concatenate([(slot == ranks[k : k + 1, :]).astype(BF16) for k in range(experts)], axis=0)
    picked = dot(pick, rows_in).astype(BF16)
    for k in range(experts):
        out[k] = picked[k * capacity : (k + 1) * capacity, :]
    if gated:
        logits = dot(router[...], rows_in, ((1,), (1,)))[:experts, :]
        logits = jnp.where(ranks >= 0, logits, NEG)
        raised = jnp.where(ranks >= 0, jnp.exp(logits - jnp.max(logits, axis=0, keepdims=True)), 0.0)
        gates_out[0] = raised / jnp.sum(raised, axis=0, keepdims=True)


def dispatch(blocks, rank, capacity, router=None):
    shards, experts, rows = rank.shape
    width = blocks[0].shape[1]
    out_specs = [pl.BlockSpec((experts, capacity, width), lambda i: (0, i, 0))]
    out_shape = [jax.ShapeDtypeStruct((experts, shards * capacity, width), BF16)]
    extra = []
    if router is not None:
        extra = [router]
        out_specs += [tiles((1, experts, rows)), whole((shards * rows, width))]
        out_shape += [
            jax.ShapeDtypeStruct((shards, experts, rows), F32),
            jax.ShapeDtypeStruct((shards * rows, width), BF16),
        ]
    return pl.pallas_call(
        functools.partial(dispatch_kernel, capacity, len(blocks), router is not None),
        grid=(shards,),
        in_specs=[tiles((1, experts, rows))] + [whole(item.shape) for item in [*blocks, *extra]],
        out_specs=out_specs,
        out_shape=out_shape,
        scratch_shapes=[] if router is not None else [pltpu.VMEM((shards * rows, width), BF16)],
        compiler_params=pltpu.CompilerParams(vmem_limit_bytes=VMEM_LIMIT),
        cost_estimate=cost(10),
        name="dispatch",
    )(rank, *blocks, *extra)


def fetch(step, count, weights, store, sems):
    def copies(index):
        made = []
        for i, pieces in enumerate(weights[index]):
            at = 0
            for piece in pieces:
                parts = [piece] if len(piece.shape) == 2 else [piece.at[s] for s in range(piece.shape[0])]
                for part in parts:
                    span = part.shape[1]
                    target = store.at[index % 2, i, :, at : at + span]
                    made.append(pltpu.make_async_copy(part, target, sems.at[index % 2, len(made)]))
                    at += span
        return made

    for index in range(count):

        @pl.when(step == index)
        def _():
            if index == 0:
                for copy in copies(0):
                    copy.start()
            if index + 1 < count:
                for copy in copies(index + 1):
                    copy.start()
            for copy in copies(index):
                copy.wait()


def regroup(refs, layout):
    groups, at = [], 0
    for expert in layout:
        groups.append([])
        for pieces in expert:
            groups[-1].append(refs[at : at + pieces])
            at += pieces
    return groups, refs[at:]


def row_scale(capacity, rank, gates):
    blocks, rows = rank.shape
    slot = lax.broadcasted_iota(jnp.int32, (capacity, rows), 0)
    return jnp.concatenate(
        [
            jnp.sum(jnp.where(slot == rank[b : b + 1, :], gates[b : b + 1, :], 0.0), axis=1, keepdims=True)
            for b in range(blocks)
        ],
        axis=0,
    )


def forward_kernel(capacity, layout, rank, gates, rows_in, *refs):
    weights, refs = regroup(refs, layout)
    count = len(layout)
    gate_out, up_out, act_out, result, store, sems = refs
    step = pl.program_id(0)
    fetch(step, count, weights, store, sems)
    gate_w, up_w, down_w = [store.at[step % 2, i] for i in range(3)]
    scale = row_scale(capacity, rank[0], gates[0])
    slots = rows_in.shape[1]
    part = slots // 2
    for at in range(0, slots, part):
        here = slice(at, at + part)
        data = rows_in[0, here, :]
        gate = dot(data, gate_w[...], ((1,), (1,)))
        up = dot(data, up_w[...], ((1,), (1,)))
        act = (gate * jax.nn.sigmoid(gate) * up * scale[here, :]).astype(BF16)
        gate_out[0, here, :] = gate.astype(BF16)
        up_out[0, here, :] = up.astype(BF16)
        act_out[0, here, :] = act
        result[0, here, :] = dot(act, down_w[...]).astype(BF16)


def backward_kernel(capacity, layout, rank, gates, cot, gate_ref, up_ref, act, *refs):
    weights, refs = regroup(refs, layout)
    count = len(layout)
    grad_gate_out, grad_up_out, grad_rows, gate_sums, store, sems = refs
    step = pl.program_id(0)
    fetch(step, count, weights, store, sems)
    gate_w, up_w, down_w = [store.at[step % 2, i] for i in range(3)]
    scale = row_scale(capacity, rank[0], gates[0])
    slots = cot.shape[1]
    part = slots // 2
    blocks, rows = rank.shape[1:]
    slot = lax.broadcasted_iota(jnp.int32, (capacity, rows), 0)
    for at in range(0, slots, part):
        here = slice(at, at + part)
        back = dot(cot[0, here, :], down_w[...], ((1,), (1,)))
        sums = jnp.sum(act[0, here, :].astype(F32) * back, axis=1, keepdims=True)
        for b in range(at // capacity, (at + part) // capacity):
            hit = slot == rank[0, b : b + 1, :]
            piece = sums[b * capacity - at : (b + 1) * capacity - at, :]
            gate_sums[0, b : b + 1, :] = jnp.sum(jnp.where(hit, piece, 0.0), axis=0, keepdims=True)
        gate = gate_ref[0, here, :].astype(F32)
        sigmoid_gate = jax.nn.sigmoid(gate)
        grad_act = back * scale[here, :]
        grad_up = (grad_act * gate * sigmoid_gate).astype(BF16)
        grad_gate = (
            grad_act * up_ref[0, here, :].astype(F32) * sigmoid_gate * (1.0 + gate * (1.0 - sigmoid_gate))
        ).astype(BF16)
        grad_up_out[0, here, :] = grad_up
        grad_gate_out[0, here, :] = grad_gate
        grad_rows[0, here, :] = (dot(grad_gate, gate_w[...]) + dot(grad_up, up_w[...])).astype(BF16)


def expert_call(
    kernel, name, first, rows_in, parts, weights, out_cols, sums, rank, gates, capacity, skip=0
):
    _, shards, rows = rank.shape
    width, inner = rows_in.shape[2], weights[0][0][0].shape[-2]
    count = len(weights)
    slots = shards * capacity
    layout = [[len(pieces) for pieces in group] for group in weights]
    flat = [piece for group in weights for pieces in group for piece in pieces]
    copies = 2 * shards + PARTS

    def of_all(shape):
        return pl.BlockSpec((1,) + shape, lambda i: (first + i, 0, 0))

    def of_these(shape):
        return pl.BlockSpec((1,) + shape, lambda i: (i, 0, 0))

    def of_parts(shape):
        return pl.BlockSpec((1,) + shape, lambda i: (skip + i, 0, 0))

    return pl.pallas_call(
        functools.partial(kernel, capacity, layout),
        grid=(count,),
        in_specs=[of_all((shards, rows)), of_all((shards, rows)), of_all((slots, width))]
        + [of_parts((slots, inner)) for _ in parts]
        + [pl.BlockSpec(memory_space=pl.ANY)] * len(flat),
        out_specs=[of_these((slots, cols)) for cols in out_cols] + [of_these((shards, rows))] * sums,
        out_shape=[jax.ShapeDtypeStruct((count, slots, cols), BF16) for cols in out_cols]
        + [jax.ShapeDtypeStruct((count, shards, rows), F32)] * sums,
        scratch_shapes=[pltpu.VMEM((2, 3, inner, width), BF16), pltpu.SemaphoreType.DMA((2, copies))],
        compiler_params=pltpu.CompilerParams(vmem_limit_bytes=VMEM_LIMIT),
        cost_estimate=cost(10 * count),
        name=name,
    )(rank, gates, rows_in, *parts, *flat)


def combine_kernel(capacity, extra, rank, *refs):
    rows, experts = rank.shape
    if extra:
        sums, gates, router, hidden, refs = refs[0], refs[1], refs[2], refs[3], refs[4:]
        *parts, out, small = refs
    else:
        *parts, out = refs
    slot = lax.broadcasted_iota(jnp.int32, (rows, experts * capacity), 1)
    pick = jnp.zeros(slot.shape, F32)
    for k in range(experts):
        at = jnp.where(rank[:, k : k + 1] >= 0, rank[:, k : k + 1] + k * capacity, -1)
        pick = pick + (slot == at).astype(F32)
    data = jnp.concatenate([part[i] for part in parts for i in range(part.shape[0])], axis=0)
    total = dot(pick.astype(BF16), data)
    if extra:
        grads = sums[0] - gates[0] * jnp.sum(sums[0], axis=0, keepdims=True)
        pad = router.shape[0] - experts
        grads = jnp.concatenate([grads, jnp.zeros((pad, rows), F32)], axis=0).astype(BF16)
        total = total + dot(grads, router[...], ((0,), (0,)))

        @pl.when(pl.program_id(0) == 0)
        def _():
            small[...] = jnp.zeros_like(small)

        small[...] += dot(grads, hidden[...])
    out[...] = total.astype(BF16)


def combine(rank_cols, parts, rows, capacity, extra=()):
    total_rows, experts = rank_cols.shape
    width = parts[0].shape[2]
    out_specs = [tiles((rows, width))]
    out_shape = [jax.ShapeDtypeStruct((total_rows, width), BF16)]
    in_specs = [tiles((rows, experts))]
    if extra:
        router = extra[2]
        in_specs += [
            tiles((1, experts, rows)), tiles((1, experts, rows)), whole(router.shape), tiles((rows, width)),
        ]
        out_specs.append(whole(router.shape))
        out_shape.append(jax.ShapeDtypeStruct(router.shape, F32))
    return pl.pallas_call(
        functools.partial(combine_kernel, capacity, bool(extra)),
        grid=(total_rows // rows,),
        in_specs=in_specs
        + [pl.BlockSpec((part.shape[0], capacity, width), lambda i: (0, i, 0)) for part in parts],
        out_specs=out_specs,
        out_shape=out_shape,
        compiler_params=pltpu.CompilerParams(vmem_limit_bytes=VMEM_LIMIT),
        cost_estimate=cost(10),
        name="combine",
    )(rank_cols, *extra, *parts)


def body(
    tokens_in,
    cotangent,
    norm1_gain,
    kv_weight,
    query_weight,
    attn_out_weight,
    attn_router,
    norm2_gain,
    in_weight,
    out_weight,
    mlp_router,
    attn_routes,
    mlp_routes,
    place_order,
    seq_lengths,
):
    experts = lax.axis_size("expert")
    shards = lax.axis_size("shard")
    rows, width = tokens_in.shape
    total_rows = rows * shards
    chips = experts // 2
    capacity = -(-5 * rows // (2 * experts) // 16) * 16
    span = query_weight.shape[2] // shards
    inner = out_weight.shape[1]
    depth = in_weight.shape[1]
    order = jnp.stack(expert_order())
    own_expert = order[0]

    chunk = depth // experts
    kv_chunk = lax.dynamic_slice_in_dim(kv_weight, own_expert * chunk, chunk, axis=0)
    kv_chunk = kv_chunk.reshape(chunk, 2, shards, span).transpose(2, 1, 0, 3)
    query_blocks = query_weight[0].reshape(depth, shards, span).transpose(1, 0, 2)
    first_blocks = jnp.concatenate([query_blocks, kv_chunk.reshape(shards, 2 * chunk, span)], axis=1)

    info = jnp.concatenate(
        [place_order, attn_routes.T, mlp_routes.T, jnp.zeros((3, rows), jnp.int32)], axis=0
    )
    info = Transfer(direct_gather, lambda info=info: info)
    inverse = jnp.argsort(order)

    stream = tokens_in.astype(F32)
    normed1, row_scale1 = norm_rows(stream, norm1_gain)
    hidden1_own = normed1.astype(BF16)
    first = Transfer(shard_exchange, lambda: first_blocks)
    out_far = fetch_far(lambda: attn_out_weight[0])
    first_far = [fetch_far(lambda: first.value, i, 2) for i in range(2)]
    (hidden1_own,) = begin([hidden1_own], [first])
    gate_blocks, up_blocks = split_columns(in_weight[0], shards)
    down_far = [fetch_far(lambda: out_weight[0], i, PARTS) for i in range(PARTS)]
    ring = RingGather(hidden1_own)
    ring.tie([], out_far + [info])
    ring.step()
    ring.tie([], (), [first, gate_blocks, info] + out_far)
    ring.tie([], first_far[0])
    ring.step()
    ring.tie([], (), first_far[0])
    ring.tie([], first_far[1])
    ring.step()
    info = info.value
    lengths = seq_lengths[0]
    places = info[:, 0].reshape(total_rows)
    cosine, sine_table, seq_ids = rope_tables(places, lengths)
    starts = jnp.sum(
        jnp.where(jnp.arange(lengths.shape[0])[None, :] < seq_ids[:, None], lengths[None, :], 0), axis=1
    )
    cosine = jnp.concatenate([cosine, cosine], axis=1)
    sine_table = jnp.concatenate([-sine_table, sine_table], axis=1)
    bounds = jnp.stack([starts, places])

    def routes_of(first):
        return info[:, first : first + 2].transpose(0, 2, 1).reshape(total_rows, 2)

    routes_attn = routes_of(1)
    named = jnp.any(info[:, 3:5, None, :] == order[None, None, :, None], axis=1)
    earlier = (jnp.arange(rows)[:, None] < jnp.arange(rows)[None, :]).astype(BF16)
    rank = jnp.einsum("bku,ut->bkt", named.astype(BF16), earlier, preferred_element_type=F32)
    rank = jnp.where(named, rank, -1.0).astype(jnp.int32)
    rank_cols = rank.transpose(0, 2, 1).reshape(total_rows, experts)
    rank_rows = rank.transpose(1, 0, 2)
    attn_router_rel = jnp.take(attn_router, order, axis=1)
    mlp_router_rel = jnp.take(mlp_router, order, axis=1)

    router_wide = jnp.pad(attn_router_rel, ((0, 0), (0, 128 - experts)))
    tables = [cosine, sine_table, bounds, routes_attn, rank, router_wide]
    ring.tie([], (), tables + first_far[1])
    ring.step()
    ring.tie([])
    hidden1_blocks = ring.blocks()
    gate_own = Transfer(shard_exchange, lambda: gate_blocks)
    hidden1_blocks = begin(hidden1_blocks, [gate_own])
    hidden1_blocks = begin(hidden1_blocks, down_far[1] + down_far[2])
    first_all = []
    for pieces in [[first.value]] + [[a.value, b.value] for a, b in zip(*first_far)]:
        first_all += [pieces, [core_swap(piece) for piece in pieces]]
    attn_out_w = with_swaps([attn_out_weight[0]] + [item.value for item in out_far])
    up_own = Transfer(shard_exchange, lambda: up_blocks)
    gate_far = [fetch_far(lambda: gate_own.value, i, PARTS) for i in range(PARTS)]
    up_far = [fetch_far(lambda: up_own.value, i, PARTS) for i in range(PARTS)]

    def first_parts(grad):
        key_grad, value_grad = [
            grad[:, (experts + i) * span : (experts + i + 1) * span].reshape(shards, experts, chunk, span)
            for i in range(2)
        ]
        parts = []
        for k in range(experts):
            query_grad = grad[:, k * span : (k + 1) * span].reshape(shards, depth, span)
            own = [
                lax.dynamic_index_in_dim(item, order[k], axis=1, keepdims=False)
                for item in (key_grad, value_grad)
            ]
            parts.append(jnp.concatenate([query_grad, *own], axis=1))
        return expert_sums(parts, range(0, experts, 2))

    mixed, query, keys, values, vec_wide, gates_attn, hidden1, kv_w = attend(
        hidden1_blocks, first_all, attn_out_w, router_wide, routes_attn, order[None], bounds.T,
        places[None], cosine, sine_table, chunk,
    )
    (mixed,) = tie([mixed], [gate_own] + down_far[1] + down_far[2])
    middle = stream + ring_scatter(
        mixed,
        {
            0: ([up_own] + down_far[3] + gate_far[0] + gate_far[1], down_far[3] + gate_far[0] + gate_far[1]),
            1: (gate_far[2] + gate_far[3], gate_far[2] + gate_far[3]),
            2: (down_far[0], [up_own] + down_far[0]),
            3: (up_far[0], up_far[0]),
        },
    )

    normed2, row_scale2 = norm_rows(middle, norm2_gain)
    hidden2_own = normed2.astype(BF16)
    cot_steps = RingGather(cotangent)
    ring = RingGather(hidden2_own)
    for part in up_far[1:]:
        ring.tie([], part)
        ring.step()
        ring.tie([], (), part)
    ring.step()
    cot_steps.ahead[0], *ring.last = tie([cotangent, *ring.last], [])
    cot_steps.behind[0] = cot_steps.ahead[0]
    hidden2_blocks = ring.blocks()
    cot_steps.step()
    router_rows = jnp.pad(mlp_router_rel.T, ((0, 16 - experts), (0, 0)))
    rows_in, gates_mlp, hidden2 = dispatch(hidden2_blocks, rank, capacity, router_rows)
    gate_rows = gates_mlp.transpose(1, 0, 2)
    down_own = Transfer(None, None, out_weight[0])
    halves = []
    forwards = []
    rows_now = rows_in
    for first in range(0, experts, 2):
        (rows_now,) = cot_steps.tie([rows_now])
        cot_steps.step()
        at = first // 2 - 1
        these = [
            [[own.value]] if first == 0 else [[part[at].value for part in far]]
            for own, far in ((gate_own, gate_far), (up_own, up_far), (down_own, down_far))
        ]
        these = [(near[0], [core_swap(piece) for piece in near[0]]) for near in these]
        these = list(zip(*these))
        halves.append((first, these))
        forwards.append(
            list(
                expert_call(
                forward_kernel, "expert_forward", first, rows_now, [], these,
                [inner, inner, inner, width], 0, rank_rows, gate_rows, capacity,
                )
            )
        )
        (forwards[-1][3],) = cot_steps.tie([forwards[-1][3]])
        rows_now = after(rows_now, forwards[-1][3])
    gates_low, ups_low, acts, results = zip(*forwards)
    cot_steps.step()
    combined = combine(rank_cols, results, rows, capacity)[0]
    (combined,) = cot_steps.tie([combined])
    cot_blocks = cot_steps.blocks()
    cot_blocks[0] = after(cot_blocks[0], combined)
    result_steps = RingScatter(combined)
    result_steps.step()
    rows_cot = dispatch(cot_blocks, rank, capacity)[0]
    rows_cot = dispatch(cot_blocks, rank, capacity)[0]
    backs, gate_w_grads = {}, {}
    cot_now = rows_cot
    calls = halves[:0:-1] + [(1, halves[0][1][1:]), (0, halves[0][1][:1])]
    for first, these in calls:
        at = first // 2
        (cot_now,) = result_steps.tie([cot_now], gate_hand[1 - first] if first < 2 else ())
        result_steps.step()
        back = [*expert_call(
            backward_kernel, "expert_backward", first, cot_now, [gates_low[at], ups_low[at], acts[at]],
            these, [inner, inner, width], 1, rank_rows, gate_rows, capacity, first % 2,
        )]
        (back[2],) = result_steps.tie([back[2]], (), gate_hand[1 - first] if first < 2 else ())
        cot_now = after(cot_now, back[2])
        for k in range(len(these)):
            backs[first + k] = [back[0][k], back[1][k], back[2], back[3]]
        if first >= 2:
            for k in (first + 1, first):
                gate_w_grads[k] = dot(backs[k][0], rows_in[k], ((0,), (0,))).astype(BF16)
                cot_now = after(cot_now, gate_w_grads[k])
            gate_sums_far = expert_sums(gate_w_grads, range(2, experts, 2)) if first == 2 else None
            gate_hand = [hand_far(lambda: gate_sums_far, i, PARTS) for i in range(PARTS)]
    grad_gates, grad_ups = [[backs[k][i] for k in range(experts)] for i in range(2)]
    groups = [0, 1] + list(range(2, experts, 2))
    grads, gate_sums = [[backs[k][i] for k in groups] for i in (2, 3)]
    acts = [item[i] for item in acts for i in range(2)]
    gate_sums = jnp.concatenate(gate_sums, axis=0).transpose(1, 0, 2)
    grads = begin(grads[:1], gate_hand[2]) + grads[1:]
    combined, mlp_part = combine(
        rank_cols, grads, rows, capacity, (gate_sums, gates_mlp, router_rows, hidden2)
    )
    result_rows = result_steps.total()
    output = (middle + result_rows).astype(BF16)
    up_w_grads, down_w_grads = {}, {}

    def weight_grad(into, left, right, k, late):
        into[k] = dot(after(left[k], late), right[k], ((0,), (0,))).astype(BF16)
        return into[k]

    gate_back = Transfer(
        lambda v: shard_exchange(v.reshape(inner, shards, depth).transpose(1, 0, 2)),
        lambda: gate_total,
    )
    up_back = Transfer(shard_exchange, lambda: up_total)
    ring = RingScatter(combined)
    (late,) = ring.tie([after(rank, result_rows)], (), gate_hand[2])
    (late,) = ring.tie([late], gate_hand[3])
    for k in range(experts - 1, 3, -1):
        weight_grad(up_w_grads, grad_ups, rows_in, k, late)
    ring.step()
    weight_grad(up_w_grads, grad_ups, rows_in, 3, late)
    (late,) = ring.tie([late], (), [up_w_grads[3]] + gate_hand[3])
    ring.step()
    weight_grad(up_w_grads, grad_ups, rows_in, 2, late)
    (late,) = ring.tie([late], (), [up_w_grads[2]])
    ring.step()
    up_sums_far = expert_sums(up_w_grads, range(2, experts, 2))
    up_hand = [hand_far(lambda: up_sums_far, i, PARTS) for i in range(PARTS)]
    weight_grad(gate_w_grads, grad_gates, rows_in, 1, late)
    (late,) = ring.tie([late], (), [gate_w_grads[1], *up_sums_far])
    ring.step()
    weight_grad(gate_w_grads, grad_gates, rows_in, 0, late)
    gate_near = expert_sums(gate_w_grads, [0])[0].astype(F32)
    (late,) = ring.tie([late], (), [gate_w_grads[0]])
    back_rows = ring.total()
    grad_hidden2 = back_rows
    grad_middle, grad_gain2 = norm_back(grad_hidden2, middle, row_scale2, norm2_gain)
    grad_middle = grad_middle + cotangent.astype(F32)

    gate_total = total_of(gate_near, gate_hand).astype(BF16)
    gate_total = total_of(gate_near, gate_hand).astype(BF16)
    ring = RingGather(grad_middle.astype(BF16))
    (late,) = ring.tie([late], [gate_back] + up_hand[0] + up_hand[1])
    ring.step()
    weight_grad(up_w_grads, grad_ups, rows_in, 1, late)
    (late,) = ring.tie([late], (), [up_w_grads[1]] + up_hand[0] + up_hand[1])
    (late,) = ring.tie([late], up_hand[2] + up_hand[3])
    ring.step()
    weight_grad(up_w_grads, grad_ups, rows_in, 0, late)
    up_near = expert_sums(up_w_grads, [0])[0].astype(F32)
    for k in range(experts - 1, 1, -1):
        weight_grad(down_w_grads, acts, rows_cot, k, late)
    down_sums_far = expert_sums(down_w_grads, range(2, experts, 2))
    down_hand = [hand_far(lambda: down_sums_far, i, PARTS) for i in range(PARTS)]
    (late,) = ring.tie([late], (), [up_w_grads[0], *down_sums_far, gate_back] + up_hand[2] + up_hand[3])
    (late,) = ring.tie([late], down_hand[0])
    ring.step()
    up_total = total_of(up_near, up_hand).astype(BF16)
    up_total = up_total.reshape(inner, shards, depth).transpose(1, 0, 2)
    for k in (1, 0):
        weight_grad(down_w_grads, acts, rows_cot, k, late)
    (late,) = ring.tie([late], (), [up_total] + down_hand[0])
    ring.step()
    (late,) = ring.tie([late], (), [down_w_grads[0], down_w_grads[1]])
    mid_blocks = ring.blocks()
    mid_blocks = begin(mid_blocks, [up_back] + down_hand[1] + down_hand[2] + down_hand[3])
    grad_rows1, grad_first, attn_part, grad_mid = attend_back(
        mid_blocks, first_all, kv_w, attn_out_w, router_wide, hidden1, routes_attn, order[None], gates_attn, bounds,
        places[:, None], cosine, sine_table, query, keys, values, vec_wide,
    )
    grad_rows1, grad_first, attn_part, late = tie(
        [grad_rows1, grad_first, attn_part, late], down_hand[1] + down_hand[2] + down_hand[3]
    )
    grad_first_w = dot(hidden1, grad_first, ((0,), (0,))).astype(BF16)
    sums = jnp.concatenate(
        [
            jnp.sum(attn_part[-8:], axis=0, keepdims=True) / norm1_gain,
            grad_gain2[None],
            jnp.take(attn_part, inverse, axis=0),
            jnp.take(mlp_part, inverse, axis=0),
        ],
        axis=0,
    )
    rounds = [("expert", step) for step in powers(experts)] + [("shard", step) for step in powers(shards)]
    small = []
    for i, (axis, step) in enumerate(rounds):
        source = (lambda: sums) if i == 0 else (lambda i=i: small[i - 1].value)
        small.append(Transfer(lambda v, axis=axis, step=step: sum_pairs(v, axis, step), source))
    (late,) = begin([late], small[:1])
    grad_rows1, late = tie([grad_rows1, late], [up_back, grad_first_w] + small[:1])
    first_sums = first_parts(grad_first_w)
    first_hand = [hand_far(lambda: first_sums[1:], i, 2) for i in range(2)]
    ring = RingScatter(grad_rows1)
    (late,) = ring.tie([late], small[1:2])
    ring.step()
    (late,) = ring.tie([late], (), first_sums + small[1:2])
    (late,) = ring.tie([late], first_hand[0] + small[2:3])
    ring.step()
    (late,) = ring.tie([late], (), first_hand[0] + small[2:3])
    (late,) = ring.tie([late], first_hand[1] + small[3:4])
    ring.step()
    grad_second_w = dot(after(vec_wide, late), grad_mid, ((0,), (0,))).astype(BF16)
    (late,) = ring.tie([late], (), first_hand[1] + small[3:4] + [grad_second_w])
    came = [jnp.concatenate([a.value, b.value], axis=0) for a, b in zip(*first_hand)]
    first_grad = sum_f32(first_sums[:1] + came).astype(BF16)
    first_back = Transfer(shard_exchange, lambda: first_grad)
    second_sums = expert_sums(jnp.split(grad_second_w, experts, axis=0), range(0, experts, 2))
    second_hand = hand_far(lambda: second_sums[1:])
    (late,) = ring.tie([late], [first_back])
    ring.step()
    (late,) = begin([late], second_hand)
    for item in small[4:]:
        (late,) = tie(begin([late], [item]), [item])
    back_rows1 = ring.total()
    late = after(late, back_rows1)
    in_grad = join_columns(after(gate_back.value, late), up_back.value)[None]
    attn_grad = sum_f32(second_sums[:1] + [item.value for item in second_hand])[None]
    out_grad = total_of(after(expert_sums(down_w_grads, [0])[0], late).astype(F32), down_hand)[None]
    first_grad = first_back.value
    sums = small[-1].value
    grad_hidden1 = back_rows1
    grad_stream, _ = norm_back(grad_hidden1, stream, row_scale1, norm1_gain)
    grad_input = grad_stream + grad_middle

    query_grad = first_grad[:, :depth].transpose(1, 0, 2).reshape(1, depth, shards * span).astype(F32)
    kv_grad = first_grad[:, depth:].reshape(shards, 2, chunk, span)
    kv_grad = kv_grad.transpose(2, 1, 0, 3).reshape(chunk, 2 * shards * span)
    pieces = expert_gather(kv_grad.astype(BF16))
    kv_grad = jnp.zeros((depth, 2 * shards * span), F32)
    for k, piece in enumerate(pieces):
        kv_grad = lax.dynamic_update_slice_in_dim(kv_grad, piece.astype(F32), order[k] * chunk, axis=0)

    return (
        output,
        grad_input,
        sums[0],
        kv_grad,
        query_grad,
        attn_grad,
        sums[2 : 2 + experts].T,
        sums[1],
        in_grad,
        out_grad,
        sums[2 + experts :].T,
    )


def solution(mesh):
    return jax.shard_map(
        body,
        mesh=mesh,
        in_specs=(
            P(("expert", "shard"), None),
            P(("expert", "shard"), None),
            P(),
            P("shard", None),
            P("expert", "shard", None),
            P("expert", "shard", None),
            P(),
            P(),
            P("expert", "shard", None),
            P("expert", "shard", None),
            P(),
            P(("expert", "shard"), None),
            P(("expert", "shard"), None),
            P("expert", "shard"),
            P("expert", None),
        ),
        out_specs=(
            P(("expert", "shard"), None),
            P(("expert", "shard"), None),
            P(),
            P("shard", None),
            P("expert", "shard", None),
            P("expert", "shard", None),
            P(),
            P(),
            P("expert", "shard", None),
            P("expert", "shard", None),
            P(),
        ),
        check_vma=False,
    )
```

time: 1180 us -> 1030 us (0.87)
  local copies, waits for them, and re-layouts: 115 us -> 61.1 us
  starting transfers between devices: 239 us -> 193 us
  other arithmetic: 98.6 us -> 60.5 us
  waiting for transfers between devices: 422 us -> 402 us
  Pallas kernels: 220 us -> 234 us
    ppermute x85 -> x71, starting transfers between devices: 180 us -> 116 us  [ring_move(): lax.ppermute(value, 'shard', [(cycle[i], cycle[(i + hops) % count]) for i...]
    ppermute x14 -> x31, waiting for transfers between devices: 120 us -> 71.2 us  [chip_shift(): lax.ppermute(value, 'expert', [(i, (i // 2 + hops) % chips * 2 + i % 2) f...]
    all_to_all x6, waiting for transfers between devices: 0.02 us -> 31.1 us  [shard_exchange(): lax.all_to_all(pieces, 'shard', split_axis=0, concat_axis=0, tiled=True)]
    unnamed x172 -> x221, local copies, waits for them, and re-layouts: 32.1 us -> 9.73 us
    ppermute x85 -> x71, waiting for transfers between devices: 295 us -> 275 us  [ring_move(): lax.ppermute(value, 'shard', [(cycle[i], cycle[(i + hops) % count]) for i...]
    ppermute x14 -> x31, starting transfers between devices: 18.9 us -> 37.8 us  [chip_shift(): lax.ppermute(value, 'expert', [(i, (i // 2 + hops) % chips * 2 + i % 2) f...]
    ppermute x10 -> x5, waiting for transfers between devices: 6.82 us -> 22 us  [sum_pairs(): lax.ppermute(value, axis, [(i, i ^ step) for i in range(count)])]
    pallas_call x12 -> x11, Pallas kernels: 208 us -> 222 us  [the longest x5 97 us: expert_call(): pl.pallas_call(functools.partial(kernel, capacity, layout), grid=(count,)...]
  transfers between devices with their start and end apart: 137 -> 145, of which waited for: 56 -> 72; matrix products, arithmetic and copies ran while one was open for 24% -> 14% of each run, Pallas kernels for 17% -> 20%
where the time goes in v2:
time: 1030 us; the launch traced here: 1020 us
  waiting for transfers between devices  402 us (39%)
  Pallas kernels  234 us (23%)
  starting transfers between devices  193 us (19%)
  matrix products  70.8 us (7%)
  local copies, waits for them, and re-layouts  61.1 us (6%)
  other arithmetic  60.5 us (6%)
    ppermute x71, waiting for transfers between devices, ring_move(): lax.ppermute(value, 'shard', [(cycle[i], cycle[(i + hops) % count]) for i...  275 us
    ppermute x71, starting transfers between devices, ring_move(): lax.ppermute(value, 'shard', [(cycle[i], cycle[(i + hops) % count]) for i...  116 us
    pallas_call x5, Pallas kernels, expert_call(): pl.pallas_call(functools.partial(kernel, capacity, layout), grid=(count,)...  97 us
    ppermute x31, waiting for transfers between devices, chip_shift(): lax.ppermute(value, 'expert', [(i, (i // 2 + hops) % chips * 2 + i % 2) f...  71.2 us
    dot_general x14, matrix products, dot(): lax.dot_general(left, right, (contract, ((), ())), preferred_element_type...  70.7 us
    pallas_call x1, Pallas kernels, attend_back(): pl.pallas_call(functools.partial(attend_back_kernel, layout, steps, len(b...  47.5 us
    ppermute x31, starting transfers between devices, chip_shift(): lax.ppermute(value, 'expert', [(i, (i // 2 + hops) % chips * 2 + i % 2) f...  37.8 us
    pallas_call x1, Pallas kernels, attend(): pl.pallas_call(functools.partial(attend_kernel, layout, len(blocks), chun...  35.1 us
  transfers between devices with their start and end apart: 145, of which 72 were waited for; matrix products, arithmetic and copies ran while one was open for 14% of the time, Pallas kernels for 20%

profile of v2, /device:TPU:0, one launch (start us, length us, event | category | flops | bytes accessed | tf_op | source)
XLA Modules:
  0.0 1024.2 jit_solution(880948516405387849)
XLA Ops:
  24.9 18.1 %collective-permute-done.2 = s32[8,128]{1,0:T(8,128)S(1)} collective-permute-done((s32[8,128]{1,0:T(8,128)S(1)}, s32[8,128]{1,0:T(8,128)S(1)}, u32[]{:S(2)}, u32[]{:S(2)}) %collective-permute-start.2) | collective-permute-done | bytes 4128 | tf_op jit(solution)/shard_map/ppermute | solution.py:76
  57.8 9.7 collective-permute-start.7
  137.0 35.1 %attend.1 = (bf16[1024,2048]{1,0:T(8,128)(2,1)}, bf16[1024,512]{1,0:T(8,128)(2,1)}, bf16[1024,256]{1,0:T(8,128)(2,1)}, bf16[1024,256]{1,0:T(8,128)(2,1)}, bf16[1...) custom-call(s32[1,4]{1,0:T(1,128)} %bitcast.259, ...), custom_call_target="tpu_custom_call" | custom-call | flops 4024999936 | bytes 65536 | tf_op jit(solution)/shard_map/attend/pallas_call | solution.py:428
  172.1 14.4 %all-to-all-done.1.refs_0_ = bf16[8,704,256]{2,1,0:T(8,128)(2,1)} async-done(((bf16[8,704,256]{2,1,0:T(8,128)(2,1)}), bf16[8,704,256]{2,1,0:T(8,128)(2,1)}, u32[]{:S(2)}, u32[]{:S(2)}) %all-to-all-start.1) | async-done | bytes 2883616 | tf_op jit(solution)/shard_map/all_to_all | solution.py:294
  201.8 46.6 %collective-permute-done.26 = bf16[64,2048]{1,0:T(8,128)(2,1)S(1)} collective-permute-done((bf16[64,2048]{1,0:T(8,128)(2,1)}, bf16[64,2048]{1,0:T(8,128)(2,1)S(1)}, u32[]{:S(2)}, u32[]{:S(2)}) %collective-permute-start.26) | collective-permute-done | bytes 262176 | tf_op jit(solution)/shard_map/ppermute | solution.py:76
  249.8 18.3 %collective-permute-start.31 = (bf16[128,2048]{1,0:T(8,128)(2,1)S(1)}, bf16[128,2048]{1,0:T(8,128)(2,1)S(1)}, u32[]{:S(2)}, u32[]{:S(2)}) collective-permute-start(bf16[128,2048]{1,0:T(8,128)(2,1)S(1)} %get-tuple-element.393), channel_id=1, source_target_pairs={{0,2},{2,4},{4,6},{6,7},{7,5},{5,3},{3,1},{1,0},{8,10},{10,12},{12... | collective-permute-start | bytes 1572872 | tf_op jit(solution)/shard_map/ppermute | solution.py:76
  270.2 8.3 collective-permute-done.31
  287.6 13.1 %collective-permute-done.33.refs_3_ = bf16[2,704,256]{2,1,0:T(8,128)(2,1)} collective-permute-done((bf16[2,704,256]{2,1,0:T(8,128)(2,1)}, bf16[2,704,256]{2,1,0:T(8,128)(2,1)}, u32[]{:S(2)}, u32[]{:S(2)}) %collective-permute-start.33) | collective-permute-done | bytes 720928 | tf_op jit(solution)/shard_map/ppermute | solution.py:215
  304.6 8.0 collective-permute-done.35
  324.9 8.8 collective-permute-done.37
  399.2 11.5 %collective-permute-done.51.refs_1_ = bf16[128,2048]{1,0:T(8,128)(2,1)S(1)} collective-permute-done((bf16[128,2048]{1,0:T(8,128)(2,1)S(1)}, bf16[128,2048]{1,0:T(8,128)(2,1)S(1)}, u32[]{:S(2)}, u32[]{:S(2)}) %collective-permute-start.51) | collective-permute-done | bytes 524320 | tf_op jit(solution)/shard_map/ppermute | solution.py:76
  414.3 11.3 %dispatch.2 = (bf16[4,640,2048]{2,1,0:T(8,128)(2,1)}, f32[8,4,128]{2,1,0:T(4,128)}, bf16[1024,2048]{1,0:T(8,128)(2,1)}) custom-call(s32[8,4,128]{2,1,0:T(4,128)} %copy.116.rank, bf16[128,2048]{1,0:T(8,128)(2,1)} %copy-done.35, bf16[128,2048]{1,0:T(8,128)(2,1)} %copy-done.70, bf16[128,2048]{1,0:T(8,128)(2,1)} %copy-done.72, bf16[128,2048]{1,0:T(8,128)(2,1)} %copy-done.41, ...), custom_call_target="tpu_custom_call" | custom-call | flops 1150000000 | bytes 65536 | tf_op jit(solution)/shard_map/dispatch/pallas_call | solution.py:708
  428.4 11.7 %collective-permute-done.53.refs_2_ = bf16[128,2048]{1,0:T(8,128)(2,1)} collective-permute-done((bf16[128,2048]{1,0:T(8,128)(2,1)S(1)}, bf16[128,2048]{1,0:T(8,128)(2,1)}, u32[]{:S(2)}, u32[]{:S(2)}) %collective-permute-start.53) | collective-permute-done | bytes 524320 | tf_op jit(solution)/shard_map/ppermute | solution.py:76
  443.1 20.2 %expert_forward.2 = (bf16[2,640,704]{2,1,0:T(8,128)(2,1)}, bf16[2,640,704]{2,1,0:T(8,128)(2,1)}, bf16[2,640,704]{2,1,0:T(8,128)(2,1)}, bf16[2,640,2048]{2,1,0:T(8,128)(2,1)}) custom-call(s32[4,8,128]{2,1,0:T(8,128)} %bitcast.241, f32[4,8,128]{2,1,0:T(8,128)} %bitcast.247, bf16[4,640,2048]{2,1,0:T(8,128)(2,1)} %get-tuple-element.440.rows_in, ...), custom_call_target="tpu_custom_call" | custom-call | flops 2300000000 | bytes 65536 | tf_op jit(solution)/shard_map/expert_forward/pallas_call | solution.py:845
  465.4 20.2 %expert_forward.3 = (bf16[2,640,704]{2,1,0:T(8,128)(2,1)}, bf16[2,640,704]{2,1,0:T(8,128)(2,1)}, bf16[2,640,704]{2,1,0:T(8,128)(2,1)}, bf16[2,640,2048]{2,1,0:T(8,128)(2,1)}) custom-call(s32[4,8,128]{2,1,0:T(8,128)} %bitcast.242, f32[4,8,128]{2,1,0:T(8,128)} %bitcast.248, bf16[4,640,2048]{2,1,0:T(8,128)(2,1)} %get-tuple-element.440.rows_in, ...), custom_call_target="tpu_custom_call" | custom-call | flops 2300000000 | bytes 65536 | tf_op jit(solution)/shard_map/expert_forward/pallas_call | solution.py:845
  488.9 9.8 combine.2
  502.3 9.7 dispatch.3.cot
  513.4 24.7 %expert_backward.3 = (bf16[2,640,704]{2,1,0:T(8,128)(2,1)}, bf16[2,640,704]{2,1,0:T(8,128)(2,1)}, bf16[2,640,2048]{2,1,0:T(8,128)(2,1)}, f32[2,8,128]{2,1,0:T(8,128)}) custom-call(s32[4,8,128]{2,1,0:T(8,128)} %bitcast.243, f32[4,8,128]{2,1,0:T(8,128)} %bitcast.249, bf16[4,640,2048]{2,1,0:T(8,128)(2,1)} %dispatch.3.cot, ...), custom_call_target="tpu_custom_call" | custom-call | flops 2300000000 | bytes 65536 | tf_op jit(solution)/shard_map/expert_backward/pallas_call | solution.py:845
  549.2 7.9 collective-permute-done.77
  566.0 16.0 %expert_backward.4 = (bf16[1,640,704]{2,1,0:T(8,128)(2,1)}, bf16[1,640,704]{2,1,0:T(8,128)(2,1)}, bf16[1,640,2048]{2,1,0:T(8,128)(2,1)}, f32[1,8,128]{2,1,0:T(8,128)}) custom-call(s32[4,8,128]{2,1,0:T(8,128)} %bitcast.244, f32[4,8,128]{2,1,0:T(8,128)} %bitcast.250, bf16[4,640,2048]{2,1,0:T(8,128)(2,1)} %dispatch.3.cot, ...), custom_call_target="tpu_custom_call" | custom-call | flops 1150000000 | bytes 65536 | tf_op jit(solution)/shard_map/expert_backward/pallas_call | solution.py:845
  587.8 16.0 %expert_backward.5 = (bf16[1,640,704]{2,1,0:T(8,128)(2,1)}, bf16[1,640,704]{2,1,0:T(8,128)(2,1)}, bf16[1,640,2048]{2,1,0:T(8,128)(2,1)}, f32[1,8,128]{2,1,0:T(8,128)}) custom-call(s32[4,8,128]{2,1,0:T(8,128)} %bitcast.245, f32[4,8,128]{2,1,0:T(8,128)} %bitcast.251, bf16[4,640,2048]{2,1,0:T(8,128)(2,1)} %dispatch.3.cot, ...), custom_call_target="tpu_custom_call" | custom-call | flops 1150000000 | bytes 65536 | tf_op jit(solution)/shard_map/expert_backward/pallas_call | solution.py:845
  609.1 11.7 %combine.3 = (bf16[1024,2048]{1,0:T(8,128)(2,1)}, f32[16,2048]{1,0:T(8,128)}) custom-call(s32[1024,4]{1,0:T(8,128)} %bitcast.218, f32[8,4,128]{2,1,0:T(4,128)} %maximum_bitcast_fusion.refs_0_, f32[8,4,128]{2,1,0:T(4,128)} %get-tuple-element.431.refs_1_, bf16[16,2048]{1,0:T(8,128)(2,1)} %pad.17.refs_9_.refs_2_, ...), custom_call_target="tpu_custom_call" | custom-call | flops 1150000000 | bytes 65536 | tf_op jit(solution)/shard_map/combine/pallas_call | solution.py:902
  635.6 10.8 %collective-permute-done.88 = bf16[704,512]{1,0:T(8,128)(2,1)S(1)} collective-permute-done((bf16[704,512]{1,0:T(8,128)(2,1)S(1)}, bf16[704,512]{1,0:T(8,128)(2,1)S(1)}, u32[]{:S(2)}, u32[]{:S(2)}) %collective-permute-start.88) | collective-permute-done | bytes 720928 | tf_op jit(solution)/shard_map/ppermute | solution.py:215
  648.5 10.7 %collective-permute-done.90 = bf16[128,2048]{1,0:T(8,128)(2,1)S(1)} collective-permute-done((bf16[128,2048]{1,0:T(8,128)(2,1)S(1)}, bf16[128,2048]{1,0:T(8,128)(2,1)S(1)}, u32[]{:S(2)}, u32[]{:S(2)}) %collective-permute-start.90) | collective-permute-done | bytes 524320 | tf_op jit(solution)/shard_map/ppermute | solution.py:76
  671.1 10.5 %collective-permute-done.92 = bf16[128,2048]{1,0:T(8,128)(2,1)S(1)} collective-permute-done((bf16[128,2048]{1,0:T(8,128)(2,1)S(1)}, bf16[128,2048]{1,0:T(8,128)(2,1)S(1)}, u32[]{:S(2)}, u32[]{:S(2)}) %collective-permute-start.92) | collective-permute-done | bytes 524320 | tf_op jit(solution)/shard_map/ppermute | solution.py:76
  716.1 10.5 %collective-permute-done.98.refs_8_ = bf16[128,2048]{1,0:T(8,128)(2,1)} collective-permute-done((bf16[128,2048]{1,0:T(8,128)(2,1)S(1)}, bf16[128,2048]{1,0:T(8,128)(2,1)}, u32[]{:S(2)}, u32[]{:S(2)}) %collective-permute-start.98) | collective-permute-done | bytes 524320 | tf_op jit(solution)/shard_map/ppermute | solution.py:76
  753.7 13.4 %collective-permute-done.101.refs_2_ = bf16[128,2048]{1,0:T(8,128)(2,1)S(1)} collective-permute-done((bf16[128,2048]{1,0:T(8,128)(2,1)}, bf16[128,2048]{1,0:T(8,128)(2,1)S(1)}, u32[]{:S(2)}, u32[]{:S(2)}) %collective-permute-start.101) | collective-permute-done | bytes 524320 | tf_op jit(solution)/shard_map/ppermute | solution.py:76
  780.9 11.3 %collective-permute-start.106 = (bf16[128,2048]{1,0:T(8,128)(2,1)S(1)}, bf16[128,2048]{1,0:T(8,128)(2,1)S(1)}, u32[]{:S(2)}, u32[]{:S(2)}) collective-permute-start(bf16[128,2048]{1,0:T(8,128)(2,1)S(1)} %copy-done.62), channel_id=1, source_target_pairs={{0,2},{2,4},{4,6},{6,7},{7,5},{5,3},{3,1},{1,0},{8,10},{10,12},{12... | collective-permute-start | bytes 1572872 | tf_op jit(solution)/shard_map/ppermute | solution.py:76
  826.2 47.5 %attend_back.1 = (bf16[1024,2048]{1,0:T(8,128)(2,1)}, bf16[1024,1536]{1,0:T(8,128)(2,1)}, f32[16,2048]{1,0:T(8,128)}, bf16[1024,2048]{1,0:T(8,128)(2,1)}) custom-call(s32[1,4]{1,0:T(1,128)} %bitcast.260, bf16[128,2048]{1,0:T(8,128)(2,1)} %copy-done.34, bf16[128,2048]{1,0:T(8,128)(2,1)} %collective-permute-done.97.refs_1_, bf16[128,2048]{1,0:T(8,128)(2,1)} %copy-done.61, ...), custom_call_target="tpu_custom_call" | custom-call | flops 5175000064 | bytes 65536 | tf_op jit(solution)/shard_map/attend_back/pallas_call | solution.py:577
  875.1 9.9 convolution_convert_fusion
  915.1 12.0 %collective-permute-done.124 = f32[10,2048]{1,0:T(8,128)S(1)} collective-permute-done((f32[10,2048]{1,0:T(8,128)S(1)}, f32[10,2048]{1,0:T(8,128)S(1)}, u32[]{:S(2)}, u32[]{:S(2)}) %collective-permute-start.124) | collective-permute-done | bytes 81952 | tf_op jit(solution)/shard_map/ppermute | solution.py:299
  990.9 14.1 %all-to-all-done.5 = bf16[8,384,256]{2,1,0:T(8,128)(2,1)S(1)} async-done(((bf16[8,384,256]{2,1,0:T(8,128)(2,1)}), bf16[8,384,256]{2,1,0:T(8,128)(2,1)S(1)}, u32[]{:S(2)}, u32[]{:S(2)}) %all-to-all-start.5) | async-done | bytes 1572896 | tf_op jit(solution)/shard_map/all_to_all | solution.py:294
  (636 shorter events, 519.5 us)
Async XLA Ops:
  8.3 66.5 %all-to-all-start = ((bf16[8,384,256]{2,1,0:T(8,128)(2,1)}), bf16[8,384,256]{2,1,0:T(8,128)(2,1)S(1)}, u32[]{:S(2)}, u32[]{:S(2)}) async-start(bf16[8,384,256]{2,1,0:T(8,128)(2,1)} %pad_maximum_fusion), calls=%async_computation | async-start | bytes 3145728 | tf_op jit(solution)/shard_map/all_to_all | solution.py:294
  20.1 34.8 %collective-permute-start.4 = (s32[8,128]{1,0:T(8,128)S(1)}, s32[8,128]{1,0:T(8,128)S(1)}, u32[]{:S(2)}, u32[]{:S(2)}) collective-permute-start(s32[8,128]{1,0:T(8,128)S(1)} %add_add_fusion), channel_id=1, source_target_pairs={{0,6},{2,7},{4,5},{6,3},{7,1},{5,0},{3,2},{1,4},{8,14},{10,15},{12... | collective-permute-start | bytes 12296 | tf_op jit(solution)/shard_map/ppermute | solution.py:76
  21.6 53.2 %collective-permute-start = (bf16[128,2048]{1,0:T(8,128)(2,1)S(1)}, bf16[128,2048]{1,0:T(8,128)(2,1)}, u32[]{:S(2)}, u32[]{:S(2)}) collective-permute-start(bf16[128,2048]{1,0:T(8,128)(2,1)S(1)} %fusion.19.refs_0_), channel_id=1, source_target_pairs={{0,2},{2,4},{4,6},{6,7},{7,5},{5,3},{3,1},{1,0},{8,10},{10,12},{12... | collective-permute-start | bytes 1572872 | tf_op jit(solution)/shard_map/ppermute | solution.py:76
  22.2 52.7 %collective-permute-start.9 = (bf16[256,2048]{1,0:T(8,128)(2,1)}, bf16[256,2048]{1,0:T(8,128)(2,1)}, u32[]{:S(2)}, u32[]{:S(2)}) collective-permute-start(bf16[256,2048]{1,0:T(8,128)(2,1)} %bitcast.219), channel_id=1, source_target_pairs={{0,16},{8,24},{16,0},{24,8},{1,17},{9,25},{17,1},{25,9},{2,18},{10... | collective-permute-start | bytes 3145736 | tf_op jit(solution)/shard_map/ppermute | solution.py:215
  43.1 31.7 %collective-permute-start.1 = (bf16[128,2048]{1,0:T(8,128)(2,1)S(1)}, bf16[128,2048]{1,0:T(8,128)(2,1)}, u32[]{:S(2)}, u32[]{:S(2)}) collective-permute-start(bf16[128,2048]{1,0:T(8,128)(2,1)S(1)} %fusion.19.refs_0_), channel_id=1, source_target_pairs={{0,1},{2,0},{4,2},{6,4},{7,6},{5,7},{3,5},{1,3},{8,9},{10,8},{12,1... | collective-permute-start | bytes 1572872 | tf_op jit(solution)/shard_map/ppermute | solution.py:76
  121.9 64.6 %all-to-all-start.1 = ((bf16[8,704,256]{2,1,0:T(8,128)(2,1)}), bf16[8,704,256]{2,1,0:T(8,128)(2,1)}, u32[]{:S(2)}, u32[]{:S(2)}) async-start(bf16[8,704,256]{2,1,0:T(8,128)(2,1)} %get-tuple-element.379), calls=%async_computation.1 | async-start | bytes 5767168 | tf_op jit(solution)/shard_map/all_to_all | solution.py:294
  132.6 39.5 %collective-permute-start.23 = (bf16[704,512]{1,0:T(8,128)(2,1)}, bf16[704,512]{1,0:T(8,128)(2,1)}, u32[]{:S(2)}, u32[]{:S(2)}) collective-permute-start(bf16[704,512]{1,0:T(8,128)(2,1)} %get-tuple-element.380), channel_id=1, source_target_pairs={{0,16},{8,24},{16,0},{24,8},{1,17},{9,25},{17,1},{25,9},{2,18},{10... | collective-permute-start | bytes 2162696 | tf_op jit(solution)/shard_map/ppermute | solution.py:215
  134.5 37.7 %collective-permute-start.24 = (bf16[704,512]{1,0:T(8,128)(2,1)}, bf16[704,512]{1,0:T(8,128)(2,1)}, u32[]{:S(2)}, u32[]{:S(2)}) collective-permute-start(bf16[704,512]{1,0:T(8,128)(2,1)} %get-tuple-element.381), channel_id=1, source_target_pairs={{0,16},{8,24},{16,0},{24,8},{1,17},{9,25},{17,1},{25,9},{2,18},{10... | collective-permute-start | bytes 2162696 | tf_op jit(solution)/shard_map/ppermute | solution.py:215
  191.8 127.4 %all-to-all-start.2 = ((bf16[8,704,256]{2,1,0:T(8,128)(2,1)}), bf16[8,704,256]{2,1,0:T(8,128)(2,1)}, u32[]{:S(2)}, u32[]{:S(2)}) async-start(bf16[8,704,256]{2,1,0:T(8,128)(2,1)} %get-tuple-element.400), calls=%async_computation.2 | async-start | bytes 5767168 | tf_op jit(solution)/shard_map/all_to_all | solution.py:294
  196.2 52.2 %collective-permute-start.26 = (bf16[64,2048]{1,0:T(8,128)(2,1)}, bf16[64,2048]{1,0:T(8,128)(2,1)S(1)}, u32[]{:S(2)}, u32[]{:S(2)}) collective-permute-start(bf16[64,2048]{1,0:T(8,128)(2,1)} %get-tuple-element.386), channel_id=1, source_target_pairs={{0,2},{2,4},{4,6},{6,7},{7,5},{5,3},{3,1},{1,0},{8,10},{10,12},{12... | collective-permute-start | bytes 786440 | tf_op jit(solution)/shard_map/ppermute | solution.py:76
  198.1 50.3 %collective-permute-start.25 = (bf16[64,2048]{1,0:T(8,128)(2,1)}, bf16[64,2048]{1,0:T(8,128)(2,1)S(1)}, u32[]{:S(2)}, u32[]{:S(2)}) collective-permute-start(bf16[64,2048]{1,0:T(8,128)(2,1)} %get-tuple-element.385), channel_id=1, source_target_pairs={{0,1},{2,0},{4,2},{6,4},{7,6},{5,7},{3,5},{1,3},{8,9},{10,8},{12,1... | collective-permute-start | bytes 786440 | tf_op jit(solution)/shard_map/ppermute | solution.py:76
  198.3 51.5 %collective-permute-start.27 = (bf16[704,512]{1,0:T(8,128)(2,1)}, bf16[704,512]{1,0:T(8,128)(2,1)S(1)}, u32[]{:S(2)}, u32[]{:S(2)}) collective-permute-start(bf16[704,512]{1,0:T(8,128)(2,1)} %get-tuple-element.387), channel_id=1, source_target_pairs={{0,16},{8,24},{16,0},{24,8},{1,17},{9,25},{17,1},{25,9},{2,18},{10... | collective-permute-start | bytes 2162696 | tf_op jit(solution)/shard_map/ppermute | solution.py:215
  199.8 50.0 %collective-permute-start.28 = (bf16[2,704,256]{2,1,0:T(8,128)(2,1)}, bf16[2,704,256]{2,1,0:T(8,128)(2,1)S(1)}, u32[]{:S(2)}, u32[]{:S(2)}) collective-permute-start(bf16[2,704,256]{2,1,0:T(8,128)(2,1)} %get-tuple-element.388), channel_id=1, source_target_pairs={{0,16},{8,24},{16,0},{24,8},{1,17},{9,25},{17,1},{25,9},{2,18},{10... | collective-permute-start | bytes 2162696 | tf_op jit(solution)/shard_map/ppermute | solution.py:215
  200.3 49.5 %collective-permute-start.29 = (bf16[2,704,256]{2,1,0:T(8,128)(2,1)}, bf16[2,704,256]{2,1,0:T(8,128)(2,1)S(1)}, u32[]{:S(2)}, u32[]{:S(2)}) collective-permute-start(bf16[2,704,256]{2,1,0:T(8,128)(2,1)} %get-tuple-element.389), channel_id=1, source_target_pairs={{0,16},{8,24},{16,0},{24,8},{1,17},{9,25},{17,1},{25,9},{2,18},{10... | collective-permute-start | bytes 2162696 | tf_op jit(solution)/shard_map/ppermute | solution.py:215
  269.7 31.1 %collective-permute-start.33 = (bf16[2,704,256]{2,1,0:T(8,128)(2,1)}, bf16[2,704,256]{2,1,0:T(8,128)(2,1)}, u32[]{:S(2)}, u32[]{:S(2)}) collective-permute-start(bf16[2,704,256]{2,1,0:T(8,128)(2,1)} %get-tuple-element.395), channel_id=1, source_target_pairs={{0,16},{8,24},{16,0},{24,8},{1,17},{9,25},{17,1},{25,9},{2,18},{10... | collective-permute-start | bytes 2162696 | tf_op jit(solution)/shard_map/ppermute | solution.py:215
  324.9 60.6 %collective-permute-start.57 = (bf16[704,2048]{1,0:T(8,128)(2,1)}, bf16[704,2048]{1,0:T(8,128)(2,1)}, u32[]{:S(2)}, u32[]{:S(2)}) collective-permute-start(bf16[704,2048]{1,0:T(8,128)(2,1)} %bitcast.207), channel_id=1, source_target_pairs={{0,8},{8,0},{16,24},{24,16},{1,9},{9,1},{17,25},{25,17},{2,10},{10... | collective-permute-start | bytes 8650760 | tf_op jit(solution)/shard_map/ppermute | solution.py:209
  372.9 54.9 %collective-permute-start.55 = (bf16[8,704,256]{2,1,0:T(8,128)(2,1)}, bf16[8,704,256]{2,1,0:T(8,128)(2,1)}, u32[]{:S(2)}, u32[]{:S(2)}) collective-permute-start(bf16[8,704,256]{2,1,0:T(8,128)(2,1)} %all-to-all-done.1.refs_0_), channel_id=1, source_target_pairs={{0,8},{8,0},{16,24},{24,16},{1,9},{9,1},{17,25},{25,17},{2,10},{10... | collective-permute-start | bytes 8650760 | tf_op jit(solution)/shard_map/ppermute | solution.py:209
  380.6 47.7 %collective-permute-start.56 = (bf16[8,704,256]{2,1,0:T(8,128)(2,1)}, bf16[8,704,256]{2,1,0:T(8,128)(2,1)}, u32[]{:S(2)}, u32[]{:S(2)}) collective-permute-start(bf16[8,704,256]{2,1,0:T(8,128)(2,1)} %all-to-all-done.2.refs_1_), channel_id=1, source_target_pairs={{0,8},{8,0},{16,24},{24,16},{1,9},{9,1},{17,25},{25,17},{2,10},{10... | collective-permute-start | bytes 8650760 | tf_op jit(solution)/shard_map/ppermute | solution.py:209
  427.8 35.5 %collective-permute-start.68 = (bf16[704,512]{1,0:T(8,128)(2,1)}, bf16[704,512]{1,0:T(8,128)(2,1)S(1)}, u32[]{:S(2)}, u32[]{:S(2)}) collective-permute-start(bf16[704,512]{1,0:T(8,128)(2,1)} %collective-permute-done.36.refs_8_), channel_id=1, source_target_pairs={{0,8},{8,0},{16,24},{24,16},{1,9},{9,1},{17,25},{25,17},{2,10},{10... | collective-permute-start | bytes 2162696 | tf_op jit(solution)/shard_map/ppermute | solution.py:209
  427.8 36.8 %collective-permute-start.64 = (bf16[2,704,256]{2,1,0:T(8,128)(2,1)}, bf16[2,704,256]{2,1,0:T(8,128)(2,1)}, u32[]{:S(2)}, u32[]{:S(2)}) collective-permute-start(bf16[2,704,256]{2,1,0:T(8,128)(2,1)} %collective-permute-done.39.refs_4_), channel_id=1, source_target_pairs={{0,8},{8,0},{16,24},{24,16},{1,9},{9,1},{17,25},{25,17},{2,10},{10... | collective-permute-start | bytes 2162696 | tf_op jit(solution)/shard_map/ppermute | solution.py:209
  428.3 37.1 %collective-permute-start.65 = (bf16[2,704,256]{2,1,0:T(8,128)(2,1)S(1)}, bf16[2,704,256]{2,1,0:T(8,128)(2,1)}, u32[]{:S(2)}, u32[]{:S(2)}) collective-permute-start(bf16[2,704,256]{2,1,0:T(8,128)(2,1)S(1)} %collective-permute-done.42.refs_5_), channel_id=1, source_target_pairs={{0,8},{8,0},{16,24},{24,16},{1,9},{9,1},{17,25},{25,17},{2,10},{10... | collective-permute-start | bytes 2162696 | tf_op jit(solution)/shard_map/ppermute | solution.py:209
  626.2 33.6 %collective-permute-start.93 = (bf16[704,2048]{1,0:T(8,128)(2,1)S(1)}, bf16[704,2048]{1,0:T(8,128)(2,1)S(1)}, u32[]{:S(2)}, u32[]{:S(2)}) collective-permute-start(bf16[704,2048]{1,0:T(8,128)(2,1)S(1)} %convolution_convert_fusion.11), channel_id=1, source_target_pairs={{0,8},{8,0},{16,24},{24,16},{1,9},{9,1},{17,25},{25,17},{2,10},{10... | collective-permute-start | bytes 8650760 | tf_op jit(solution)/shard_map/ppermute | solution.py:209
  701.3 30.6 %collective-permute-start.100 = (bf16[704,512]{1,0:T(8,128)(2,1)}, bf16[704,512]{1,0:T(8,128)(2,1)}, u32[]{:S(2)}, u32[]{:S(2)}) collective-permute-start(bf16[704,512]{1,0:T(8,128)(2,1)} %get-tuple-element.539), channel_id=1, source_target_pairs={{0,16},{8,24},{16,0},{24,8},{1,17},{9,25},{17,1},{25,9},{2,18},{10... | collective-permute-start | bytes 2162696 | tf_op jit(solution)/shard_map/ppermute | solution.py:215
  704.3 71.3 %all-to-all-start.3 = ((bf16[8,704,256]{2,1,0:T(8,128)(2,1)}), bf16[8,704,256]{2,1,0:T(8,128)(2,1)}, u32[]{:S(2)}, u32[]{:S(2)}) async-start(bf16[8,704,256]{2,1,0:T(8,128)(2,1)} %bitcast.212), calls=%async_computation.3 | async-start | bytes 5767168 | tf_op jit(solution)/shard_map/all_to_all | solution.py:294
  737.4 54.7 %collective-permute-start.108 = (bf16[704,2048]{1,0:T(8,128)(2,1)}, bf16[704,2048]{1,0:T(8,128)(2,1)}, u32[]{:S(2)}, u32[]{:S(2)}) collective-permute-start(bf16[704,2048]{1,0:T(8,128)(2,1)} %convolution_convert_fusion.7), channel_id=1, source_target_pairs={{0,8},{8,0},{16,24},{24,16},{1,9},{9,1},{17,25},{25,17},{2,10},{10... | collective-permute-start | bytes 8650760 | tf_op jit(solution)/shard_map/ppermute | solution.py:209
  780.0 29.6 %collective-permute-start.138 = (bf16[704,2048]{1,0:T(8,128)(2,1)S(1)}, bf16[704,2048]{1,0:T(8,128)(2,1)S(1)}, u32[]{:S(2)}, u32[]{:S(2)}) collective-permute-start(bf16[704,2048]{1,0:T(8,128)(2,1)S(1)} %convolution_convert_fusion.2), channel_id=1, source_target_pairs={{0,8},{8,0},{16,24},{24,16},{1,9},{9,1},{17,25},{25,17},{2,10},{10... | collective-permute-start | bytes 8650760 | tf_op jit(solution)/shard_map/ppermute | solution.py:209
  817.1 56.6 %collective-permute-start.112 = (bf16[704,512]{1,0:T(8,128)(2,1)}, bf16[704,512]{1,0:T(8,128)(2,1)S(1)}, u32[]{:S(2)}, u32[]{:S(2)}) collective-permute-start(bf16[704,512]{1,0:T(8,128)(2,1)} %get-tuple-element.591), channel_id=1, source_target_pairs={{0,16},{8,24},{16,0},{24,8},{1,17},{9,25},{17,1},{25,9},{2,18},{10... | collective-permute-start | bytes 2162696 | tf_op jit(solution)/shard_map/ppermute | solution.py:215
  817.9 55.9 %collective-permute-start.113 = (bf16[704,512]{1,0:T(8,128)(2,1)}, bf16[704,512]{1,0:T(8,128)(2,1)S(1)}, u32[]{:S(2)}, u32[]{:S(2)}) collective-permute-start(bf16[704,512]{1,0:T(8,128)(2,1)} %get-tuple-element.592), channel_id=1, source_target_pairs={{0,16},{8,24},{16,0},{24,8},{1,17},{9,25},{17,1},{25,9},{2,18},{10... | collective-permute-start | bytes 2162696 | tf_op jit(solution)/shard_map/ppermute | solution.py:215
  819.1 54.6 %collective-permute-start.114 = (bf16[704,512]{1,0:T(8,128)(2,1)}, bf16[704,512]{1,0:T(8,128)(2,1)S(1)}, u32[]{:S(2)}, u32[]{:S(2)}) collective-permute-start(bf16[704,512]{1,0:T(8,128)(2,1)} %get-tuple-element.593), channel_id=1, source_target_pairs={{0,16},{8,24},{16,0},{24,8},{1,17},{9,25},{17,1},{25,9},{2,18},{10... | collective-permute-start | bytes 2162696 | tf_op jit(solution)/shard_map/ppermute | solution.py:215
  821.7 78.3 %all-to-all-start.4 = ((bf16[8,704,256]{2,1,0:T(8,128)(2,1)}), bf16[8,704,256]{2,1,0:T(8,128)(2,1)}, u32[]{:S(2)}, u32[]{:S(2)}) async-start(bf16[8,704,256]{2,1,0:T(8,128)(2,1)} %bitcast.211), calls=%async_computation.4 | async-start | bytes 5767168 | tf_op jit(solution)/shard_map/all_to_all | solution.py:294
  955.2 32.0 %collective-permute-start.136 = (bf16[256,2048]{1,0:T(8,128)(2,1)}, bf16[256,2048]{1,0:T(8,128)(2,1)}, u32[]{:S(2)}, u32[]{:S(2)}) collective-permute-start(bf16[256,2048]{1,0:T(8,128)(2,1)} %get-tuple-element.675), channel_id=1, source_target_pairs={{0,8},{8,0},{16,24},{24,16},{1,9},{9,1},{17,25},{25,17},{2,10},{10... | collective-permute-start | bytes 3145736 | tf_op jit(solution)/shard_map/ppermute | solution.py:209
  957.2 47.8 %all-to-all-start.5 = ((bf16[8,384,256]{2,1,0:T(8,128)(2,1)}), bf16[8,384,256]{2,1,0:T(8,128)(2,1)S(1)}, u32[]{:S(2)}, u32[]{:S(2)}) async-start(bf16[8,384,256]{2,1,0:T(8,128)(2,1)} %add_convert_fusion.8), calls=%async_computation.5 | async-start | bytes 3145728 | tf_op jit(solution)/shard_map/all_to_all | solution.py:294
  (222 other events, 4063.7 us)

commit v3 on v2

--- a/solution.py
+++ b/solution.py
@@ -200,9 +200,16 @@
     return ring.total()
 
 
-def direct_gather(block):
+def doubled(value, step):
     count = lax.axis_size("shard")
-    return jnp.stack([block] + [ring_move(block, r) for r in range(1, count)])
+    return jnp.concatenate([value, lax.ppermute(value, "shard", [(i, i ^ step) for i in range(count)])])
+
+
+def ring_sorted(blocks):
+    cycle = ring_cycle(lax.axis_size("shard"))
+    own = lax.axis_index("shard")
+    spot = jnp.array([cycle.index(s) for s in range(len(cycle))])[own]
+    return jnp.take(blocks, own ^ jnp.array(cycle)[(spot - jnp.arange(len(cycle))) % len(cycle)], axis=0)
 
 
 def core_swap(value):
@@ -718,32 +725,44 @@
     )(rank, *blocks, *extra)
 
 
-def fetch(step, count, weights, store, sems):
-    def copies(index):
-        made = []
-        for i, pieces in enumerate(weights[index]):
+class Fetch:
+    def __init__(self, step, weights, store, sems):
+        self.step, self.weights, self.store, self.sems = step, weights, store, sems
+
+    def copies(self, index, which):
+        made, slot = [], 0
+        for i, pieces in enumerate(self.weights[index]):
             at = 0
             for piece in pieces:
                 parts = [piece] if len(piece.shape) == 2 else [piece.at[s] for s in range(piece.shape[0])]
                 for part in parts:
                     span = part.shape[1]
-                    target = store.at[index % 2, i, :, at : at + span]
-                    made.append(pltpu.make_async_copy(part, target, sems.at[index % 2, len(made)]))
+                    if i == which:
+                        target = self.store.at[index % 2, i, :, at : at + span]
+                        made.append(pltpu.make_async_copy(part, target, self.sems.at[index % 2, slot]))
                     at += span
+                    slot += 1
         return made
 
-    for index in range(count):
-
-        @pl.when(step == index)
-        def _():
-            if index == 0:
-                for copy in copies(0):
-                    copy.start()
-            if index + 1 < count:
-                for copy in copies(index + 1):
-                    copy.start()
-            for copy in copies(index):
-                copy.wait()
+    def start(self, sequence):
+        count = len(self.weights)
+        for index in range(count):
+
+            @pl.when(self.step == index)
+            def _():
+                for ahead in [0, 1] if index == 0 else [index + 1]:
+                    if ahead < count:
+                        for i in sequence:
+                            for copy in self.copies(ahead, i):
+                                copy.start()
+
+    def wait(self, i):
+        for index in range(len(self.weights)):
+
+            @pl.when(self.step == index)
+            def _():
+                for copy in self.copies(index, i):
+                    copy.wait()
 
 
 def regroup(refs, layout):
@@ -773,7 +792,8 @@
     count = len(layout)
     gate_out, up_out, act_out, result, store, sems = refs
     step = pl.program_id(0)
-    fetch(step, count, weights, store, sems)
+    fetch = Fetch(step, weights, store, sems)
+    fetch.start((0, 1, 2))
     gate_w, up_w, down_w = [store.at[step % 2, i] for i in range(3)]
     scale = row_scale(capacity, rank[0], gates[0])
     slots = rows_in.shape[1]
@@ -781,12 +801,18 @@
     for at in range(0, slots, part):
         here = slice(at, at + part)
         data = rows_in[0, here, :]
+        if at == 0:
+            fetch.wait(0)
         gate = dot(data, gate_w[...], ((1,), (1,)))
+        if at == 0:
+            fetch.wait(1)
         up = dot(data, up_w[...], ((1,), (1,)))
         act = (gate * jax.nn.sigmoid(gate) * up * scale[here, :]).astype(BF16)
         gate_out[0, here, :] = gate.astype(BF16)
         up_out[0, here, :] = up.astype(BF16)
         act_out[0, here, :] = act
+        if at == 0:
+            fetch.wait(2)
         result[0, here, :] = dot(act, down_w[...]).astype(BF16)
 
 
@@ -795,7 +821,8 @@
     count = len(layout)
     grad_gate_out, grad_up_out, grad_rows, gate_sums, store, sems = refs
     step = pl.program_id(0)
-    fetch(step, count, weights, store, sems)
+    fetch = Fetch(step, weights, store, sems)
+    fetch.start((2, 0, 1))
     gate_w, up_w, down_w = [store.at[step % 2, i] for i in range(3)]
     scale = row_scale(capacity, rank[0], gates[0])
     slots = cot.shape[1]
@@ -804,6 +831,8 @@
     slot = lax.broadcasted_iota(jnp.int32, (capacity, rows), 0)
     for at in range(0, slots, part):
         here = slice(at, at + part)
+        if at == 0:
+            fetch.wait(2)
         back = dot(cot[0, here, :], down_w[...], ((1,), (1,)))
         sums = jnp.sum(act[0, here, :].astype(F32) * back, axis=1, keepdims=True)
         for b in range(at // capacity, (at + part) // capacity):
@@ -819,6 +848,9 @@
         ).astype(BF16)
         grad_up_out[0, here, :] = grad_up
         grad_gate_out[0, here, :] = grad_gate
+        if at == 0:
+            fetch.wait(0)
+            fetch.wait(1)
         grad_rows[0, here, :] = (dot(grad_gate, gate_w[...]) + dot(grad_up, up_w[...])).astype(BF16)
 
 
@@ -950,7 +982,10 @@
     info = jnp.concatenate(
         [place_order, attn_routes.T, mlp_routes.T, jnp.zeros((3, rows), jnp.int32)], axis=0
     )
-    info = Transfer(direct_gather, lambda info=info: info)
+    rounds = []
+    for i, step in enumerate(powers(shards)):
+        source = (lambda info=info: info[None]) if i == 0 else (lambda i=i: rounds[i - 1].value)
+        rounds.append(Transfer(lambda v, step=step: doubled(v, step), source))
     inverse = jnp.argsort(order)
 
     stream = tokens_in.astype(F32)
@@ -961,17 +996,22 @@
     first_far = [fetch_far(lambda: first.value, i, 2) for i in range(2)]
     (hidden1_own,) = begin([hidden1_own], [first])
     gate_blocks, up_blocks = split_columns(in_weight[0], shards)
-    down_far = [fetch_far(lambda: out_weight[0], i, PARTS) for i in range(PARTS)]
+    down_parts = [part_of(out_weight[0], i) for i in range(PARTS)]
+    down_far = [fetch_far(lambda i=i: down_parts[i]) for i in range(PARTS)]
     ring = RingGather(hidden1_own)
-    ring.tie([], out_far + [info])
-    ring.step()
-    ring.tie([], (), [first, gate_blocks, info] + out_far)
-    ring.tie([], first_far[0])
-    ring.step()
-    ring.tie([], (), first_far[0])
-    ring.tie([], first_far[1])
-    ring.step()
-    info = info.value
+    ring.tie([], out_far + rounds[:1])
+    ring.step()
+    ring.tie([], (), [first, gate_blocks, *down_parts] + out_far + rounds[:1])
+    ring.tie([], first_far[0] + rounds[1:2])
+    ring.step()
+    ring.tie([], (), first_far[0] + rounds[1:2])
+    ring.tie([], first_far[1] + rounds[2:3])
+    ring.step()
+    ring.tie([], (), rounds[2:3])
+    for item in rounds[3:]:
+        item.value = item.source()
+        item.begin()
+    info = ring_sorted(rounds[-1].value)
     lengths = seq_lengths[0]
     places = info[:, 0].reshape(total_rows)
     cosine, sine_table, seq_ids = rope_tables(places, lengths)
@@ -997,17 +1037,16 @@
 
     router_wide = jnp.pad(attn_router_rel, ((0, 0), (0, 128 - experts)))
     tables = [cosine, sine_table, bounds, routes_attn, rank, router_wide]
+    ring.step()
     ring.tie([], (), tables + first_far[1])
-    ring.step()
-    ring.tie([])
     hidden1_blocks = ring.blocks()
     gate_own = Transfer(shard_exchange, lambda: gate_blocks)
     hidden1_blocks = begin(hidden1_blocks, [gate_own])
-    hidden1_blocks = begin(hidden1_blocks, down_far[1] + down_far[2])
     first_all = []
     for pieces in [[first.value]] + [[a.value, b.value] for a, b in zip(*first_far)]:
         first_all += [pieces, [core_swap(piece) for piece in pieces]]
     attn_out_w = with_swaps([attn_out_weight[0]] + [item.value for item in out_far])
+    hidden1_blocks = begin(hidden1_blocks, down_far[1] + down_far[2])
     up_own = Transfer(shard_exchange, lambda: up_blocks)
     gate_far = [fetch_far(lambda: gate_own.value, i, PARTS) for i in range(PARTS)]
     up_far = [fetch_far(lambda: up_own.value, i, PARTS) for i in range(PARTS)]
@@ -1035,10 +1074,10 @@
     middle = stream + ring_scatter(
         mixed,
         {
-            0: ([up_own] + down_far[3] + gate_far[0] + gate_far[1], down_far[3] + gate_far[0] + gate_far[1]),
-            1: (gate_far[2] + gate_far[3], gate_far[2] + gate_far[3]),
-            2: (down_far[0], [up_own] + down_far[0]),
-            3: (up_far[0], up_far[0]),
+            0: ([up_own] + gate_far[0] + gate_far[1] + gate_far[2], gate_far[0] + gate_far[1] + gate_far[2]),
+            1: (gate_far[3], [up_own] + gate_far[3]),
+            2: (up_far[0], up_far[0]),
+            3: (up_far[1], up_far[1]),
         },
     )
 
@@ -1046,7 +1085,7 @@
     hidden2_own = normed2.astype(BF16)
     cot_steps = RingGather(cotangent)
     ring = RingGather(hidden2_own)
-    for part in up_far[1:]:
+    for part in (up_far[2], up_far[3], down_far[3]):
         ring.tie([], part)
         ring.step()
         ring.tie([], (), part)
@@ -1063,7 +1102,7 @@
     forwards = []
     rows_now = rows_in
     for first in range(0, experts, 2):
-        (rows_now,) = cot_steps.tie([rows_now])
+        (rows_now,) = cot_steps.tie([rows_now], () if first else down_far[0])
         cot_steps.step()
         at = first // 2 - 1
         these = [
@@ -1081,7 +1120,7 @@
                 )
             )
         )
-        (forwards[-1][3],) = cot_steps.tie([forwards[-1][3]])
+        (forwards[-1][3],) = cot_steps.tie([forwards[-1][3]], (), () if first else down_far[0])
         rows_now = after(rows_now, forwards[-1][3])
     gates_low, ups_low, acts, results = zip(*forwards)
     cot_steps.step()
@@ -1143,10 +1182,10 @@
         weight_grad(up_w_grads, grad_ups, rows_in, k, late)
     ring.step()
     weight_grad(up_w_grads, grad_ups, rows_in, 3, late)
-    (late,) = ring.tie([late], (), [up_w_grads[3]] + gate_hand[3])
+    (late,) = ring.tie([late], (), [up_w_grads[3]])
     ring.step()
     weight_grad(up_w_grads, grad_ups, rows_in, 2, late)
-    (late,) = ring.tie([late], (), [up_w_grads[2]])
+    (late,) = ring.tie([late], (), [up_w_grads[2]] + gate_hand[3])
     ring.step()
     up_sums_far = expert_sums(up_w_grads, range(2, experts, 2))
     up_hand = [hand_far(lambda: up_sums_far, i, PARTS) for i in range(PARTS)]
@@ -1167,25 +1206,24 @@
     (late,) = ring.tie([late], [gate_back] + up_hand[0] + up_hand[1])
     ring.step()
     weight_grad(up_w_grads, grad_ups, rows_in, 1, late)
-    (late,) = ring.tie([late], (), [up_w_grads[1]] + up_hand[0] + up_hand[1])
+    weight_grad(down_w_grads, acts, rows_cot, 1, late)
+    (late,) = ring.tie([late], (), [up_w_grads[1], down_w_grads[1]] + up_hand[0] + up_hand[1])
     (late,) = ring.tie([late], up_hand[2] + up_hand[3])
     ring.step()
     weight_grad(up_w_grads, grad_ups, rows_in, 0, late)
     up_near = expert_sums(up_w_grads, [0])[0].astype(F32)
-    for k in range(experts - 1, 1, -1):
+    for k in [*range(experts - 1, 1, -1), 0]:
         weight_grad(down_w_grads, acts, rows_cot, k, late)
     down_sums_far = expert_sums(down_w_grads, range(2, experts, 2))
     down_hand = [hand_far(lambda: down_sums_far, i, PARTS) for i in range(PARTS)]
-    (late,) = ring.tie([late], (), [up_w_grads[0], *down_sums_far, gate_back] + up_hand[2] + up_hand[3])
+    (late,) = ring.tie([late], (), [up_w_grads[0], down_w_grads[0], *down_sums_far, gate_back] + up_hand[2] + up_hand[3])
     (late,) = ring.tie([late], down_hand[0])
     ring.step()
     up_total = total_of(up_near, up_hand).astype(BF16)
     up_total = up_total.reshape(inner, shards, depth).transpose(1, 0, 2)
-    for k in (1, 0):
-        weight_grad(down_w_grads, acts, rows_cot, k, late)
     (late,) = ring.tie([late], (), [up_total] + down_hand[0])
     ring.step()
-    (late,) = ring.tie([late], (), [down_w_grads[0], down_w_grads[1]])
+    (late,) = ring.tie([late])
     mid_blocks = ring.blocks()
     mid_blocks = begin(mid_blocks, [up_back] + down_hand[1] + down_hand[2] + down_hand[3])
     grad_rows1, grad_first, attn_part, grad_mid = attend_back(
@@ -1195,7 +1233,6 @@
     grad_rows1, grad_first, attn_part, late = tie(
         [grad_rows1, grad_first, attn_part, late], down_hand[1] + down_hand[2] + down_hand[3]
     )
-    grad_first_w = dot(hidden1, grad_first, ((0,), (0,))).astype(BF16)
     sums = jnp.concatenate(
         [
             jnp.sum(attn_part[-8:], axis=0, keepdims=True) / norm1_gain,
@@ -1210,14 +1247,15 @@
     for i, (axis, step) in enumerate(rounds):
         source = (lambda: sums) if i == 0 else (lambda i=i: small[i - 1].value)
         small.append(Transfer(lambda v, axis=axis, step=step: sum_pairs(v, axis, step), source))
-    (late,) = begin([late], small[:1])
-    grad_rows1, late = tie([grad_rows1, late], [up_back, grad_first_w] + small[:1])
+    ring = RingScatter(grad_rows1)
+    late, grad_first = ring.tie([late, grad_first], small[:1])
+    ring.step()
+    grad_first_w = dot(hidden1, grad_first, ((0,), (0,))).astype(BF16)
     first_sums = first_parts(grad_first_w)
     first_hand = [hand_far(lambda: first_sums[1:], i, 2) for i in range(2)]
-    ring = RingScatter(grad_rows1)
-    (late,) = ring.tie([late], small[1:2])
-    ring.step()
-    (late,) = ring.tie([late], (), first_sums + small[1:2])
+    (late,) = tie([late], [grad_first_w] + small[:1])
+    (late,) = begin([late], small[1:2])
+    (late,) = ring.tie([late], (), [up_back] + first_sums + small[1:2])
     (late,) = ring.tie([late], first_hand[0] + small[2:3])
     ring.step()
     (late,) = ring.tie([late], (), first_hand[0] + small[2:3])
@@ -1239,13 +1277,13 @@
     late = after(late, back_rows1)
     in_grad = join_columns(after(gate_back.value, late), up_back.value)[None]
     attn_grad = sum_f32(second_sums[:1] + [item.value for item in second_hand])[None]
-    out_grad = total_of(after(expert_sums(down_w_grads, [0])[0], late).astype(F32), down_hand)[None]
-    first_grad = first_back.value
+    out_grad = total_of(expert_sums(down_w_grads, [0])[0].astype(F32), down_hand)[None]
     sums = small[-1].value
     grad_hidden1 = back_rows1
     grad_stream, _ = norm_back(grad_hidden1, stream, row_scale1, norm1_gain)
     grad_input = grad_stream + grad_middle
 
+    first_grad = first_back.value
     query_grad = first_grad[:, :depth].transpose(1, 0, 2).reshape(1, depth, shards * span).astype(F32)
     kv_grad = first_grad[:, depth:].reshape(shards, 2, chunk, span)
     kv_grad = kv_grad.transpose(2, 1, 0, 3).reshape(chunk, 2 * shards * span)

time: 1030 us -> 1010 us (0.981)
  waiting for transfers between devices: 402 us -> 362 us
    ppermute x0 -> x3, waiting for transfers between devices: none -> 32.8 us  [doubled(): lax.ppermute(value, 'shard', [(i, i ^ step) for i in range(count)])]
    ppermute x31, waiting for transfers between devices: 71.2 us -> 38.5 us  [chip_shift(): lax.ppermute(value, 'expert', [(i, (i // 2 + hops) % chips * 2 + i % 2) f...]
    ppermute x71 -> x64, waiting for transfers between devices: 275 us -> 243 us  [ring_move(): lax.ppermute(value, 'shard', [(cycle[i], cycle[(i + hops) % count]) for i...]
    ppermute x5, waiting for transfers between devices: 22 us -> 5.51 us  [sum_pairs(): lax.ppermute(value, axis, [(i, i ^ step) for i in range(count)])]
    ppermute x71 -> x64, starting transfers between devices: 116 us -> 107 us  [ring_move(): lax.ppermute(value, 'shard', [(cycle[i], cycle[(i + hops) % count]) for i...]
  transfers between devices with their start and end apart: 145 -> 141, of which waited for: 72 -> 68; matrix products, arithmetic and copies ran while one was open for 14% -> 16% of each run, Pallas kernels for 20% -> 21%
where the time goes in v3:
time: 1010 us; the launch traced here: 1000 us
  waiting for transfers between devices  362 us (36%)
  Pallas kernels  232 us (23%)
  starting transfers between devices  195 us (19%)
  local copies, waits for them, and re-layouts  71.2 us (7%)
  matrix products  69.5 us (7%)
  other arithmetic  68.1 us (7%)
    ppermute x64, waiting for transfers between devices, ring_move(): lax.ppermute(value, 'shard', [(cycle[i], cycle[(i + hops) % count]) for i...  243 us
    ppermute x64, starting transfers between devices, ring_move(): lax.ppermute(value, 'shard', [(cycle[i], cycle[(i + hops) % count]) for i...  107 us
    pallas_call x5, Pallas kernels, expert_call(): pl.pallas_call(functools.partial(kernel, capacity, layout), grid=(count,)...  95 us
    dot_general x14, matrix products, dot(): lax.dot_general(left, right, (contract, ((), ())), preferred_element_type...  69.4 us
    pallas_call x1, Pallas kernels, attend_back(): pl.pallas_call(functools.partial(attend_back_kernel, layout, steps, len(b...  47.5 us
    ppermute x31, waiting for transfers between devices, chip_shift(): lax.ppermute(value, 'expert', [(i, (i // 2 + hops) % chips * 2 + i % 2) f...  38.5 us
    ppermute x31, starting transfers between devices, chip_shift(): lax.ppermute(value, 'expert', [(i, (i // 2 + hops) % chips * 2 + i % 2) f...  38.5 us
    pallas_call x1, Pallas kernels, attend(): pl.pallas_call(functools.partial(attend_kernel, layout, len(blocks), chun...  35.1 us
  transfers between devices with their start and end apart: 141, of which 68 were waited for; matrix products, arithmetic and copies ran while one was open for 16% of the time, Pallas kernels for 21%

profile of v3, /device:TPU:0, one launch (start us, length us, event | category | flops | bytes accessed | tf_op | source)
XLA Modules:
  0.0 1000.5 jit_solution(12912834704552178895)
XLA Ops:
  31.6 14.6 %collective-permute-done.3 = s32[1,8,128]{2,1,0:T(8,128)S(1)} collective-permute-done((s32[1,8,128]{2,1,0:T(8,128)S(1)}, s32[1,8,128]{2,1,0:T(8,128)S(1)}, u32[]{:S(2)}, u32[]{:S(2)}) %collective-permute-start.3) | collective-permute-done | bytes 4128 | tf_op jit(solution)/shard_map/ppermute | solution.py:205
  57.5 10.0 collective-permute-start.4
  70.9 9.7 collective-permute-done.7
  91.2 8.6 collective-permute-done.10
  126.3 35.1 %attend.1 = (bf16[1024,2048]{1,0:T(8,128)(2,1)}, bf16[1024,512]{1,0:T(8,128)(2,1)}, bf16[1024,256]{1,0:T(8,128)(2,1)}, bf16[1024,256]{1,0:T(8,128)(2,1)}, bf16[1...) custom-call(s32[1,4]{1,0:T(1,128)} %bitcast.244, ...), custom_call_target="tpu_custom_call" | custom-call | flops 4024999936 | bytes 65536 | tf_op jit(solution)/shard_map/attend/pallas_call | solution.py:435
  161.4 16.9 %all-to-all-done.1.refs_0_ = bf16[8,704,256]{2,1,0:T(8,128)(2,1)} async-done(((bf16[8,704,256]{2,1,0:T(8,128)(2,1)}), bf16[8,704,256]{2,1,0:T(8,128)(2,1)}, u32[]{:S(2)}, u32[]{:S(2)}) %all-to-all-start.1) | async-done | bytes 2883616 | tf_op jit(solution)/shard_map/all_to_all | solution.py:301
  193.6 46.7 %collective-permute-done.22 = bf16[64,2048]{1,0:T(8,128)(2,1)S(1)} collective-permute-done((bf16[64,2048]{1,0:T(8,128)(2,1)}, bf16[64,2048]{1,0:T(8,128)(2,1)S(1)}, u32[]{:S(2)}, u32[]{:S(2)}) %collective-permute-start.22) | collective-permute-done | bytes 262176 | tf_op jit(solution)/shard_map/ppermute | solution.py:76
  241.8 18.3 %collective-permute-start.27 = (bf16[128,2048]{1,0:T(8,128)(2,1)S(1)}, bf16[128,2048]{1,0:T(8,128)(2,1)S(1)}, u32[]{:S(2)}, u32[]{:S(2)}) collective-permute-start(bf16[128,2048]{1,0:T(8,128)(2,1)S(1)} %get-tuple-element.390), channel_id=1, source_target_pairs={{0,2},{2,4},{4,6},{6,7},{7,5},{5,3},{3,1},{1,0},{8,10},{10,12},{12... | collective-permute-start | bytes 1572872 | tf_op jit(solution)/shard_map/ppermute | solution.py:76
  261.6 8.9 collective-permute-done.27
  283.2 8.0 collective-permute-done.30
  301.5 8.6 collective-permute-done.32
  318.5 7.5 collective-permute-done.35.refs_1_
  354.4 8.6 collective-permute-done.42.refs_6_
  395.5 11.4 %dispatch.2 = (bf16[4,640,2048]{2,1,0:T(8,128)(2,1)}, f32[8,4,128]{2,1,0:T(4,128)}, bf16[1024,2048]{1,0:T(8,128)(2,1)}) custom-call(s32[8,4,128]{2,1,0:T(4,128)} %copy.91.rank, bf16[128,2048]{1,0:T(8,128)(2,1)} %copy-done.37, bf16[128,2048]{1,0:T(8,128)(2,1)} %copy-done.68, bf16[128,2048]{1,0:T(8,128)(2,1)} %copy-done.70, bf16[128,2048]{1,0:T(8,128)(2,1)} %copy-done.42, ...), custom_call_target="tpu_custom_call" | custom-call | flops 1150000000 | bytes 65536 | tf_op jit(solution)/shard_map/dispatch/pallas_call | solution.py:715
  411.0 10.3 %collective-permute-done.48.refs_2_ = bf16[128,2048]{1,0:T(8,128)(2,1)S(1)} collective-permute-done((bf16[128,2048]{1,0:T(8,128)(2,1)}, bf16[128,2048]{1,0:T(8,128)(2,1)S(1)}, u32[]{:S(2)}, u32[]{:S(2)}) %collective-permute-start.48) | collective-permute-done | bytes 524320 | tf_op jit(solution)/shard_map/ppermute | solution.py:76
  427.6 20.9 %expert_forward.2 = (bf16[2,640,704]{2,1,0:T(8,128)(2,1)}, bf16[2,640,704]{2,1,0:T(8,128)(2,1)}, bf16[2,640,704]{2,1,0:T(8,128)(2,1)}, bf16[2,640,2048]{2,1,0:T(8,128)(2,1)}) custom-call(s32[4,8,128]{2,1,0:T(8,128)} %bitcast.228, f32[4,8,128]{2,1,0:T(8,128)} %bitcast.234, bf16[4,640,2048]{2,1,0:T(8,128)(2,1)} %get-tuple-element.437.rows_in, ...), custom_call_target="tpu_custom_call" | custom-call | flops 2300000000 | bytes 65536 | tf_op jit(solution)/shard_map/expert_forward/pallas_call | solution.py:877
  453.9 20.6 %expert_forward.3 = (bf16[2,640,704]{2,1,0:T(8,128)(2,1)}, bf16[2,640,704]{2,1,0:T(8,128)(2,1)}, bf16[2,640,704]{2,1,0:T(8,128)(2,1)}, bf16[2,640,2048]{2,1,0:T(8,128)(2,1)}) custom-call(s32[4,8,128]{2,1,0:T(8,128)} %bitcast.229, f32[4,8,128]{2,1,0:T(8,128)} %bitcast.235, bf16[4,640,2048]{2,1,0:T(8,128)(2,1)} %get-tuple-element.437.rows_in, ...), custom_call_target="tpu_custom_call" | custom-call | flops 2300000000 | bytes 65536 | tf_op jit(solution)/shard_map/expert_forward/pallas_call | solution.py:877
  478.7 9.8 combine.2
  492.0 9.4 dispatch.3.cot
  502.9 24.2 %expert_backward.3 = (bf16[2,640,704]{2,1,0:T(8,128)(2,1)}, bf16[2,640,704]{2,1,0:T(8,128)(2,1)}, bf16[2,640,2048]{2,1,0:T(8,128)(2,1)}, f32[2,8,128]{2,1,0:T(8,128)}) custom-call(s32[4,8,128]{2,1,0:T(8,128)} %bitcast.230, f32[4,8,128]{2,1,0:T(8,128)} %bitcast.236, bf16[4,640,2048]{2,1,0:T(8,128)(2,1)} %dispatch.3.cot, ...), custom_call_target="tpu_custom_call" | custom-call | flops 2300000000 | bytes 65536 | tf_op jit(solution)/shard_map/expert_backward/pallas_call | solution.py:877
  538.3 7.9 collective-permute-done.73
  554.3 14.6 %expert_backward.4 = (bf16[1,640,704]{2,1,0:T(8,128)(2,1)}, bf16[1,640,704]{2,1,0:T(8,128)(2,1)}, bf16[1,640,2048]{2,1,0:T(8,128)(2,1)}, f32[1,8,128]{2,1,0:T(8,128)}) custom-call(s32[4,8,128]{2,1,0:T(8,128)} %bitcast.231, f32[4,8,128]{2,1,0:T(8,128)} %bitcast.237, bf16[4,640,2048]{2,1,0:T(8,128)(2,1)} %dispatch.3.cot, ...), custom_call_target="tpu_custom_call" | custom-call | flops 1150000000 | bytes 65536 | tf_op jit(solution)/shard_map/expert_backward/pallas_call | solution.py:877
  574.9 14.6 %expert_backward.5 = (bf16[1,640,704]{2,1,0:T(8,128)(2,1)}, bf16[1,640,704]{2,1,0:T(8,128)(2,1)}, bf16[1,640,2048]{2,1,0:T(8,128)(2,1)}, f32[1,8,128]{2,1,0:T(8,128)}) custom-call(s32[4,8,128]{2,1,0:T(8,128)} %bitcast.232, f32[4,8,128]{2,1,0:T(8,128)} %bitcast.238, bf16[4,640,2048]{2,1,0:T(8,128)(2,1)} %dispatch.3.cot, ...), custom_call_target="tpu_custom_call" | custom-call | flops 1150000000 | bytes 65536 | tf_op jit(solution)/shard_map/expert_backward/pallas_call | solution.py:877
  594.8 11.8 %combine.3 = (bf16[1024,2048]{1,0:T(8,128)(2,1)}, f32[16,2048]{1,0:T(8,128)}) custom-call(s32[1024,4]{1,0:T(8,128)} %bitcast.205, f32[8,4,128]{2,1,0:T(4,128)} %maximum_bitcast_fusion.refs_0_, f32[8,4,128]{2,1,0:T(4,128)} %get-tuple-element.427.refs_1_, bf16[16,2048]{1,0:T(8,128)(2,1)} %pad.17.refs_9_.refs_2_, ...), custom_call_target="tpu_custom_call" | custom-call | flops 1150000000 | bytes 65536 | tf_op jit(solution)/shard_map/combine/pallas_call | solution.py:934
  624.8 10.3 %collective-permute-done.85 = bf16[128,2048]{1,0:T(8,128)(2,1)S(1)} collective-permute-done((bf16[128,2048]{1,0:T(8,128)(2,1)S(1)}, bf16[128,2048]{1,0:T(8,128)(2,1)S(1)}, u32[]{:S(2)}, u32[]{:S(2)}) %collective-permute-start.85) | collective-permute-done | bytes 524320 | tf_op jit(solution)/shard_map/ppermute | solution.py:76
  650.1 9.2 collective-permute-done.88
  730.1 13.7 %collective-permute-done.97.refs_2_ = bf16[128,2048]{1,0:T(8,128)(2,1)S(1)} collective-permute-done((bf16[128,2048]{1,0:T(8,128)(2,1)}, bf16[128,2048]{1,0:T(8,128)(2,1)S(1)}, u32[]{:S(2)}, u32[]{:S(2)}) %collective-permute-start.97) | collective-permute-done | bytes 524320 | tf_op jit(solution)/shard_map/ppermute | solution.py:76
  753.1 11.6 %collective-permute-start.102 = (bf16[128,2048]{1,0:T(8,128)(2,1)}, bf16[128,2048]{1,0:T(8,128)(2,1)S(1)}, u32[]{:S(2)}, u32[]{:S(2)}) collective-permute-start(bf16[128,2048]{1,0:T(8,128)(2,1)} %copy-done.60), channel_id=1, source_target_pairs={{0,2},{2,4},{4,6},{6,7},{7,5},{5,3},{3,1},{1,0},{8,10},{10,12},{12... | collective-permute-start | bytes 1572872 | tf_op jit(solution)/shard_map/ppermute | solution.py:76
  798.2 47.5 %attend_back.1 = (bf16[1024,2048]{1,0:T(8,128)(2,1)}, bf16[1024,1536]{1,0:T(8,128)(2,1)}, f32[16,2048]{1,0:T(8,128)}, bf16[1024,2048]{1,0:T(8,128)(2,1)}) custom-call(s32[1,4]{1,0:T(1,128)} %bitcast.245, bf16[128,2048]{1,0:T(8,128)(2,1)} %copy-done.36, bf16[128,2048]{1,0:T(8,128)(2,1)} %collective-permute-done.93.refs_1_, bf16[128,2048]{1,0:T(8,128)(2,1)} %copy-done.60, ...), custom_call_target="tpu_custom_call" | custom-call | flops 5175000064 | bytes 65536 | tf_op jit(solution)/shard_map/attend_back/pallas_call | solution.py:584
  850.1 9.9 convolution_convert_fusion
  957.0 8.2 collective-permute-done.133
  968.6 12.7 %all-to-all-done.5 = bf16[8,384,256]{2,1,0:T(8,128)(2,1)S(1)} async-done(((bf16[8,384,256]{2,1,0:T(8,128)(2,1)}), bf16[8,384,256]{2,1,0:T(8,128)(2,1)S(1)}, u32[]{:S(2)}, u32[]{:S(2)}) %all-to-all-start.5) | async-done | bytes 1572896 | tf_op jit(solution)/shard_map/all_to_all | solution.py:301
  (629 shorter events, 517.8 us)
Async XLA Ops:
  8.3 46.3 %all-to-all-start = ((bf16[8,384,256]{2,1,0:T(8,128)(2,1)}), bf16[8,384,256]{2,1,0:T(8,128)(2,1)S(1)}, u32[]{:S(2)}, u32[]{:S(2)}) async-start(bf16[8,384,256]{2,1,0:T(8,128)(2,1)} %pad_maximum_fusion), calls=%async_computation | async-start | bytes 3145728 | tf_op jit(solution)/shard_map/all_to_all | solution.py:301
  15.7 38.9 %collective-permute-start.2 = (bf16[256,2048]{1,0:T(8,128)(2,1)}, bf16[256,2048]{1,0:T(8,128)(2,1)}, u32[]{:S(2)}, u32[]{:S(2)}) collective-permute-start(bf16[256,2048]{1,0:T(8,128)(2,1)} %bitcast.206), channel_id=1, source_target_pairs={{0,16},{8,24},{16,0},{24,8},{1,17},{9,25},{17,1},{25,9},{2,18},{10... | collective-permute-start | bytes 3145736 | tf_op jit(solution)/shard_map/ppermute | solution.py:222
  17.2 35.8 %collective-permute-start = (bf16[128,2048]{1,0:T(8,128)(2,1)S(1)}, bf16[128,2048]{1,0:T(8,128)(2,1)}, u32[]{:S(2)}, u32[]{:S(2)}) collective-permute-start(bf16[128,2048]{1,0:T(8,128)(2,1)S(1)} %fusion.19.refs_0_), channel_id=1, source_target_pairs={{0,2},{2,4},{4,6},{6,7},{7,5},{5,3},{3,1},{1,0},{8,10},{10,12},{12... | collective-permute-start | bytes 1572872 | tf_op jit(solution)/shard_map/ppermute | solution.py:76
  19.3 35.3 %collective-permute-start.1 = (bf16[128,2048]{1,0:T(8,128)(2,1)S(1)}, bf16[128,2048]{1,0:T(8,128)(2,1)}, u32[]{:S(2)}, u32[]{:S(2)}) collective-permute-start(bf16[128,2048]{1,0:T(8,128)(2,1)S(1)} %fusion.19.refs_0_), channel_id=1, source_target_pairs={{0,1},{2,0},{4,2},{6,4},{7,6},{5,7},{3,5},{1,3},{8,9},{10,8},{12,1... | collective-permute-start | bytes 1572872 | tf_op jit(solution)/shard_map/ppermute | solution.py:76
  111.2 67.1 %all-to-all-start.1 = ((bf16[8,704,256]{2,1,0:T(8,128)(2,1)}), bf16[8,704,256]{2,1,0:T(8,128)(2,1)}, u32[]{:S(2)}, u32[]{:S(2)}) async-start(bf16[8,704,256]{2,1,0:T(8,128)(2,1)} %get-tuple-element.376), calls=%async_computation.1 | async-start | bytes 5767168 | tf_op jit(solution)/shard_map/all_to_all | solution.py:301
  121.9 39.5 %collective-permute-start.19 = (bf16[704,512]{1,0:T(8,128)(2,1)}, bf16[704,512]{1,0:T(8,128)(2,1)}, u32[]{:S(2)}, u32[]{:S(2)}) collective-permute-start(bf16[704,512]{1,0:T(8,128)(2,1)} %get-tuple-element.377), channel_id=1, source_target_pairs={{0,16},{8,24},{16,0},{24,8},{1,17},{9,25},{17,1},{25,9},{2,18},{10... | collective-permute-start | bytes 2162696 | tf_op jit(solution)/shard_map/ppermute | solution.py:222
  123.8 37.7 %collective-permute-start.20 = (bf16[704,512]{1,0:T(8,128)(2,1)}, bf16[704,512]{1,0:T(8,128)(2,1)}, u32[]{:S(2)}, u32[]{:S(2)}) collective-permute-start(bf16[704,512]{1,0:T(8,128)(2,1)} %get-tuple-element.378), channel_id=1, source_target_pairs={{0,16},{8,24},{16,0},{24,8},{1,17},{9,25},{17,1},{25,9},{2,18},{10... | collective-permute-start | bytes 2162696 | tf_op jit(solution)/shard_map/ppermute | solution.py:222
  183.6 93.6 %all-to-all-start.2 = ((bf16[8,704,256]{2,1,0:T(8,128)(2,1)}), bf16[8,704,256]{2,1,0:T(8,128)(2,1)}, u32[]{:S(2)}, u32[]{:S(2)}) async-start(bf16[8,704,256]{2,1,0:T(8,128)(2,1)} %get-tuple-element.391), calls=%async_computation.2 | async-start | bytes 5767168 | tf_op jit(solution)/shard_map/all_to_all | solution.py:301
  188.0 52.3 %collective-permute-start.22 = (bf16[64,2048]{1,0:T(8,128)(2,1)}, bf16[64,2048]{1,0:T(8,128)(2,1)S(1)}, u32[]{:S(2)}, u32[]{:S(2)}) collective-permute-start(bf16[64,2048]{1,0:T(8,128)(2,1)} %get-tuple-element.383), channel_id=1, source_target_pairs={{0,2},{2,4},{4,6},{6,7},{7,5},{5,3},{3,1},{1,0},{8,10},{10,12},{12... | collective-permute-start | bytes 786440 | tf_op jit(solution)/shard_map/ppermute | solution.py:76
  189.9 50.4 %collective-permute-start.21 = (bf16[64,2048]{1,0:T(8,128)(2,1)}, bf16[64,2048]{1,0:T(8,128)(2,1)S(1)}, u32[]{:S(2)}, u32[]{:S(2)}) collective-permute-start(bf16[64,2048]{1,0:T(8,128)(2,1)} %get-tuple-element.382), channel_id=1, source_target_pairs={{0,1},{2,0},{4,2},{6,4},{7,6},{5,7},{3,5},{1,3},{8,9},{10,8},{12,1... | collective-permute-start | bytes 786440 | tf_op jit(solution)/shard_map/ppermute | solution.py:76
  190.1 51.6 %collective-permute-start.23 = (bf16[2,704,256]{2,1,0:T(8,128)(2,1)}, bf16[2,704,256]{2,1,0:T(8,128)(2,1)S(1)}, u32[]{:S(2)}, u32[]{:S(2)}) collective-permute-start(bf16[2,704,256]{2,1,0:T(8,128)(2,1)} %get-tuple-element.384), channel_id=1, source_target_pairs={{0,16},{8,24},{16,0},{24,8},{1,17},{9,25},{17,1},{25,9},{2,18},{10... | collective-permute-start | bytes 2162696 | tf_op jit(solution)/shard_map/ppermute | solution.py:222
  191.6 50.1 %collective-permute-start.24 = (bf16[2,704,256]{2,1,0:T(8,128)(2,1)}, bf16[2,704,256]{2,1,0:T(8,128)(2,1)S(1)}, u32[]{:S(2)}, u32[]{:S(2)}) collective-permute-start(bf16[2,704,256]{2,1,0:T(8,128)(2,1)} %get-tuple-element.385), channel_id=1, source_target_pairs={{0,16},{8,24},{16,0},{24,8},{1,17},{9,25},{17,1},{25,9},{2,18},{10... | collective-permute-start | bytes 2162696 | tf_op jit(solution)/shard_map/ppermute | solution.py:222
  192.1 49.6 %collective-permute-start.25 = (bf16[2,704,256]{2,1,0:T(8,128)(2,1)}, bf16[2,704,256]{2,1,0:T(8,128)(2,1)S(1)}, u32[]{:S(2)}, u32[]{:S(2)}) collective-permute-start(bf16[2,704,256]{2,1,0:T(8,128)(2,1)} %get-tuple-element.386), channel_id=1, source_target_pairs={{0,16},{8,24},{16,0},{24,8},{1,17},{9,25},{17,1},{25,9},{2,18},{10... | collective-permute-start | bytes 2162696 | tf_op jit(solution)/shard_map/ppermute | solution.py:222
  241.8 28.7 %collective-permute-start.27 = (bf16[128,2048]{1,0:T(8,128)(2,1)S(1)}, bf16[128,2048]{1,0:T(8,128)(2,1)S(1)}, u32[]{:S(2)}, u32[]{:S(2)}) collective-permute-start(bf16[128,2048]{1,0:T(8,128)(2,1)S(1)} %get-tuple-element.390), channel_id=1, source_target_pairs={{0,2},{2,4},{4,6},{6,7},{7,5},{5,3},{3,1},{1,0},{8,10},{10,12},{12... | collective-permute-start | bytes 1572872 | tf_op jit(solution)/shard_map/ppermute | solution.py:76
  318.5 62.6 %collective-permute-start.52 = (bf16[704,2048]{1,0:T(8,128)(2,1)S(1)}, bf16[704,2048]{1,0:T(8,128)(2,1)S(1)}, u32[]{:S(2)}, u32[]{:S(2)}) collective-permute-start(bf16[704,2048]{1,0:T(8,128)(2,1)S(1)} %bitcast.196), channel_id=1, source_target_pairs={{0,8},{8,0},{16,24},{24,16},{1,9},{9,1},{17,25},{25,17},{2,10},{10... | collective-permute-start | bytes 8650760 | tf_op jit(solution)/shard_map/ppermute | solution.py:216
  346.7 63.8 %collective-permute-start.50 = (bf16[8,704,256]{2,1,0:T(8,128)(2,1)}, bf16[8,704,256]{2,1,0:T(8,128)(2,1)}, u32[]{:S(2)}, u32[]{:S(2)}) collective-permute-start(bf16[8,704,256]{2,1,0:T(8,128)(2,1)} %all-to-all-done.1.refs_0_), channel_id=1, source_target_pairs={{0,8},{8,0},{16,24},{24,16},{1,9},{9,1},{17,25},{25,17},{2,10},{10... | collective-permute-start | bytes 8650760 | tf_op jit(solution)/shard_map/ppermute | solution.py:216
  346.7 63.8 %collective-permute-start.51 = (bf16[8,704,256]{2,1,0:T(8,128)(2,1)}, bf16[8,704,256]{2,1,0:T(8,128)(2,1)}, u32[]{:S(2)}, u32[]{:S(2)}) collective-permute-start(bf16[8,704,256]{2,1,0:T(8,128)(2,1)} %all-to-all-done.2.refs_1_), channel_id=1, source_target_pairs={{0,8},{8,0},{16,24},{24,16},{1,9},{9,1},{17,25},{25,17},{2,10},{10... | collective-permute-start | bytes 8650760 | tf_op jit(solution)/shard_map/ppermute | solution.py:216
  410.5 38.1 %collective-permute-start.58 = (bf16[2,704,256]{2,1,0:T(8,128)(2,1)S(1)}, bf16[2,704,256]{2,1,0:T(8,128)(2,1)}, u32[]{:S(2)}, u32[]{:S(2)}) collective-permute-start(bf16[2,704,256]{2,1,0:T(8,128)(2,1)S(1)} %copy-done.21), channel_id=1, source_target_pairs={{0,8},{8,0},{16,24},{24,16},{1,9},{9,1},{17,25},{25,17},{2,10},{10... | collective-permute-start | bytes 2162696 | tf_op jit(solution)/shard_map/ppermute | solution.py:216
  410.5 38.6 %collective-permute-start.59 = (bf16[2,704,256]{2,1,0:T(8,128)(2,1)}, bf16[2,704,256]{2,1,0:T(8,128)(2,1)}, u32[]{:S(2)}, u32[]{:S(2)}) collective-permute-start(bf16[2,704,256]{2,1,0:T(8,128)(2,1)} %collective-permute-done.28.refs_3_), channel_id=1, source_target_pairs={{0,8},{8,0},{16,24},{24,16},{1,9},{9,1},{17,25},{25,17},{2,10},{10... | collective-permute-start | bytes 2162696 | tf_op jit(solution)/shard_map/ppermute | solution.py:216
  678.0 30.7 %collective-permute-start.96 = (bf16[704,512]{1,0:T(8,128)(2,1)}, bf16[704,512]{1,0:T(8,128)(2,1)}, u32[]{:S(2)}, u32[]{:S(2)}) collective-permute-start(bf16[704,512]{1,0:T(8,128)(2,1)} %get-tuple-element.537), channel_id=1, source_target_pairs={{0,16},{8,24},{16,0},{24,8},{1,17},{9,25},{17,1},{25,9},{2,18},{10... | collective-permute-start | bytes 2162696 | tf_op jit(solution)/shard_map/ppermute | solution.py:222
  681.1 71.3 %all-to-all-start.3 = ((bf16[8,704,256]{2,1,0:T(8,128)(2,1)}), bf16[8,704,256]{2,1,0:T(8,128)(2,1)}, u32[]{:S(2)}, u32[]{:S(2)}) async-start(bf16[8,704,256]{2,1,0:T(8,128)(2,1)} %bitcast.199), calls=%async_computation.3 | async-start | bytes 5767168 | tf_op jit(solution)/shard_map/all_to_all | solution.py:301
  711.3 53.4 %collective-permute-start.104 = (bf16[704,2048]{1,0:T(8,128)(2,1)}, bf16[704,2048]{1,0:T(8,128)(2,1)}, u32[]{:S(2)}, u32[]{:S(2)}) collective-permute-start(bf16[704,2048]{1,0:T(8,128)(2,1)} %convolution_convert_fusion.7), channel_id=1, source_target_pairs={{0,8},{8,0},{16,24},{24,16},{1,9},{9,1},{17,25},{25,17},{2,10},{10... | collective-permute-start | bytes 8650760 | tf_op jit(solution)/shard_map/ppermute | solution.py:216
  711.8 32.0 %collective-permute-start.97 = (bf16[128,2048]{1,0:T(8,128)(2,1)}, bf16[128,2048]{1,0:T(8,128)(2,1)S(1)}, u32[]{:S(2)}, u32[]{:S(2)}) collective-permute-start(bf16[128,2048]{1,0:T(8,128)(2,1)} %collective-permute-done.93.refs_1_), channel_id=1, source_target_pairs={{0,2},{2,4},{4,6},{6,7},{7,5},{5,3},{3,1},{1,0},{8,10},{10,12},{12... | collective-permute-start | bytes 1572872 | tf_op jit(solution)/shard_map/ppermute | solution.py:76
  712.4 31.4 %collective-permute-start.98 = (bf16[128,2048]{1,0:T(8,128)(2,1)}, bf16[128,2048]{1,0:T(8,128)(2,1)S(1)}, u32[]{:S(2)}, u32[]{:S(2)}) collective-permute-start(bf16[128,2048]{1,0:T(8,128)(2,1)} %collective-permute-done.94.refs_8_), channel_id=1, source_target_pairs={{0,1},{2,0},{4,2},{6,4},{7,6},{5,7},{3,5},{1,3},{8,9},{10,8},{12,1... | collective-permute-start | bytes 1572872 | tf_op jit(solution)/shard_map/ppermute | solution.py:76
  714.0 29.7 %collective-permute-start.100 = (bf16[704,512]{1,0:T(8,128)(2,1)S(1)}, bf16[704,512]{1,0:T(8,128)(2,1)S(1)}, u32[]{:S(2)}, u32[]{:S(2)}) collective-permute-start(bf16[704,512]{1,0:T(8,128)(2,1)S(1)} %copy-done.56), channel_id=1, source_target_pairs={{0,16},{8,24},{16,0},{24,8},{1,17},{9,25},{17,1},{25,9},{2,18},{10... | collective-permute-start | bytes 2162696 | tf_op jit(solution)/shard_map/ppermute | solution.py:222
  788.5 57.1 %collective-permute-start.108 = (bf16[704,512]{1,0:T(8,128)(2,1)}, bf16[704,512]{1,0:T(8,128)(2,1)}, u32[]{:S(2)}, u32[]{:S(2)}) collective-permute-start(bf16[704,512]{1,0:T(8,128)(2,1)} %get-tuple-element.588), channel_id=1, source_target_pairs={{0,16},{8,24},{16,0},{24,8},{1,17},{9,25},{17,1},{25,9},{2,18},{10... | collective-permute-start | bytes 2162696 | tf_op jit(solution)/shard_map/ppermute | solution.py:222
  789.3 56.4 %collective-permute-start.109 = (bf16[704,512]{1,0:T(8,128)(2,1)}, bf16[704,512]{1,0:T(8,128)(2,1)}, u32[]{:S(2)}, u32[]{:S(2)}) collective-permute-start(bf16[704,512]{1,0:T(8,128)(2,1)} %get-tuple-element.589), channel_id=1, source_target_pairs={{0,16},{8,24},{16,0},{24,8},{1,17},{9,25},{17,1},{25,9},{2,18},{10... | collective-permute-start | bytes 2162696 | tf_op jit(solution)/shard_map/ppermute | solution.py:222
  790.6 55.1 %collective-permute-start.110 = (bf16[704,512]{1,0:T(8,128)(2,1)}, bf16[704,512]{1,0:T(8,128)(2,1)}, u32[]{:S(2)}, u32[]{:S(2)}) collective-permute-start(bf16[704,512]{1,0:T(8,128)(2,1)} %get-tuple-element.590), channel_id=1, source_target_pairs={{0,16},{8,24},{16,0},{24,8},{1,17},{9,25},{17,1},{25,9},{2,18},{10... | collective-permute-start | bytes 2162696 | tf_op jit(solution)/shard_map/ppermute | solution.py:222
  792.9 102.1 %collective-permute-start.134 = (bf16[704,2048]{1,0:T(8,128)(2,1)}, bf16[704,2048]{1,0:T(8,128)(2,1)}, u32[]{:S(2)}, u32[]{:S(2)}) collective-permute-start(bf16[704,2048]{1,0:T(8,128)(2,1)} %convolution_convert_fusion.6), channel_id=1, source_target_pairs={{0,8},{8,0},{16,24},{24,16},{1,9},{9,1},{17,25},{25,17},{2,10},{10... | collective-permute-start | bytes 8650760 | tf_op jit(solution)/shard_map/ppermute | solution.py:216
  793.0 96.9 %all-to-all-start.4 = ((bf16[8,704,256]{2,1,0:T(8,128)(2,1)}), bf16[8,704,256]{2,1,0:T(8,128)(2,1)}, u32[]{:S(2)}, u32[]{:S(2)}) async-start(bf16[8,704,256]{2,1,0:T(8,128)(2,1)} %bitcast.198), calls=%async_computation.4 | async-start | bytes 5767168 | tf_op jit(solution)/shard_map/all_to_all | solution.py:301
  924.7 32.3 %collective-permute-start.131 = (bf16[256,2048]{1,0:T(8,128)(2,1)}, bf16[256,2048]{1,0:T(8,128)(2,1)}, u32[]{:S(2)}, u32[]{:S(2)}) collective-permute-start(bf16[256,2048]{1,0:T(8,128)(2,1)} %get-tuple-element.659), channel_id=1, source_target_pairs={{0,8},{8,0},{16,24},{24,16},{1,9},{9,1},{17,25},{25,17},{2,10},{10... | collective-permute-start | bytes 3145736 | tf_op jit(solution)/shard_map/ppermute | solution.py:216
  934.8 46.6 %all-to-all-start.5 = ((bf16[8,384,256]{2,1,0:T(8,128)(2,1)}), bf16[8,384,256]{2,1,0:T(8,128)(2,1)S(1)}, u32[]{:S(2)}, u32[]{:S(2)}) async-start(bf16[8,384,256]{2,1,0:T(8,128)(2,1)} %add_convert_fusion.8), calls=%async_computation.5 | async-start | bytes 3145728 | tf_op jit(solution)/shard_map/all_to_all | solution.py:301
  (212 other events, 3806.8 us)

commit v4 on v3

--- a/solution.py
+++ b/solution.py
@@ -1261,6 +1261,7 @@
     (late,) = ring.tie([late], (), first_hand[0] + small[2:3])
     (late,) = ring.tie([late], first_hand[1] + small[3:4])
     ring.step()
+    ring.step()
     grad_second_w = dot(after(vec_wide, late), grad_mid, ((0,), (0,))).astype(BF16)
     (late,) = ring.tie([late], (), first_hand[1] + small[3:4] + [grad_second_w])
     came = [jnp.concatenate([a.value, b.value], axis=0) for a, b in zip(*first_hand)]
@@ -1268,14 +1269,14 @@
     first_back = Transfer(shard_exchange, lambda: first_grad)
     second_sums = expert_sums(jnp.split(grad_second_w, experts, axis=0), range(0, experts, 2))
     second_hand = hand_far(lambda: second_sums[1:])
-    (late,) = ring.tie([late], [first_back])
-    ring.step()
-    (late,) = begin([late], second_hand)
+    ring.tie([], [first_back])
+    came_back = [gate_back, up_back] + [item for part in down_hand for item in part]
+    for item, value in zip(came_back, begin([item.value for item in came_back], second_hand)):
+        item.value = value
     for item in small[4:]:
         (late,) = tie(begin([late], [item]), [item])
     back_rows1 = ring.total()
-    late = after(late, back_rows1)
-    in_grad = join_columns(after(gate_back.value, late), up_back.value)[None]
+    in_grad = join_columns(gate_back.value, up_back.value)[None]
     attn_grad = sum_f32(second_sums[:1] + [item.value for item in second_hand])[None]
     out_grad = total_of(expert_sums(down_w_grads, [0])[0].astype(F32), down_hand)[None]
     sums = small[-1].value

time: 1010 us -> 1000 us (0.990)
    ppermute x5, waiting for transfers between devices: 5.51 us -> 18.4 us  [sum_pairs(): lax.ppermute(value, axis, [(i, i ^ step) for i in range(count)])]
  transfers between devices with their start and end apart: 141 -> 141, of which waited for: 68 -> 67; matrix products, arithmetic and copies ran while one was open for 16% -> 16% of each run, Pallas kernels for 21% -> 21%
where the time goes in v4:
time: 1000 us; the launch traced here: 993 us
  waiting for transfers between devices  365 us (36%)
  Pallas kernels  232 us (23%)
  starting transfers between devices  194 us (19%)
  matrix products  69.6 us (7%)
  local copies, waits for them, and re-layouts  67.4 us (7%)
  other arithmetic  62.8 us (6%)
    ppermute x64, waiting for transfers between devices, ring_move(): lax.ppermute(value, 'shard', [(cycle[i], cycle[(i + hops) % count]) for i...  241 us
    ppermute x64, starting transfers between devices, ring_move(): lax.ppermute(value, 'shard', [(cycle[i], cycle[(i + hops) % count]) for i...  105 us
    pallas_call x5, Pallas kernels, expert_call(): pl.pallas_call(functools.partial(kernel, capacity, layout), grid=(count,)...  95.1 us
    dot_general x14, matrix products, dot(): lax.dot_general(left, right, (contract, ((), ())), preferred_element_type...  69.5 us
    pallas_call x1, Pallas kernels, attend_back(): pl.pallas_call(functools.partial(attend_back_kernel, layout, steps, len(b...  47.5 us
    ppermute x31, starting transfers between devices, chip_shift(): lax.ppermute(value, 'expert', [(i, (i // 2 + hops) % chips * 2 + i % 2) f...  38.2 us
    ppermute x31, waiting for transfers between devices, chip_shift(): lax.ppermute(value, 'expert', [(i, (i // 2 + hops) % chips * 2 + i % 2) f...  37.3 us
    pallas_call x1, Pallas kernels, attend(): pl.pallas_call(functools.partial(attend_kernel, layout, len(blocks), chun...  35.1 us
  transfers between devices with their start and end apart: 141, of which 67 were waited for; matrix products, arithmetic and copies ran while one was open for 16% of the time, Pallas kernels for 21%

profile of v4, /device:TPU:0, one launch (start us, length us, event | category | flops | bytes accessed | tf_op | source)
XLA Modules:
  0.0 992.7 jit_solution(16352907964157937004)
XLA Ops:
  31.6 14.6 %collective-permute-done.3 = s32[1,8,128]{2,1,0:T(8,128)S(1)} collective-permute-done((s32[1,8,128]{2,1,0:T(8,128)S(1)}, s32[1,8,128]{2,1,0:T(8,128)S(1)}, u32[]{:S(2)}, u32[]{:S(2)}) %collective-permute-start.3) | collective-permute-done | bytes 4128 | tf_op jit(solution)/shard_map/ppermute | solution.py:205
  57.5 10.0 %collective-permute-start.4 = (bf16[128,2048]{1,0:T(8,128)(2,1)}, bf16[128,2048]{1,0:T(8,128)(2,1)}, u32[]{:S(2)}, u32[]{:S(2)}) collective-permute-start(bf16[128,2048]{1,0:T(8,128)(2,1)} %collective-permute-done.refs_1_), channel_id=1, source_target_pairs={{0,2},{2,4},{4,6},{6,7},{7,5},{5,3},{3,1},{1,0},{8,10},{10,12},{12... | collective-permute-start | bytes 1572872 | tf_op jit(solution)/shard_map/ppermute | solution.py:76
  70.9 9.7 collective-permute-done.7
  91.2 8.6 collective-permute-done.10
  126.3 35.1 %attend.1 = (bf16[1024,2048]{1,0:T(8,128)(2,1)}, bf16[1024,512]{1,0:T(8,128)(2,1)}, bf16[1024,256]{1,0:T(8,128)(2,1)}, bf16[1024,256]{1,0:T(8,128)(2,1)}, bf16[1...) custom-call(s32[1,4]{1,0:T(1,128)} %bitcast.244, ...), custom_call_target="tpu_custom_call" | custom-call | flops 4024999936 | bytes 65536 | tf_op jit(solution)/shard_map/attend/pallas_call | solution.py:435
  161.4 16.9 %all-to-all-done.1.refs_0_ = bf16[8,704,256]{2,1,0:T(8,128)(2,1)} async-done(((bf16[8,704,256]{2,1,0:T(8,128)(2,1)}), bf16[8,704,256]{2,1,0:T(8,128)(2,1)}, u32[]{:S(2)}, u32[]{:S(2)}) %all-to-all-start.1) | async-done | bytes 2883616 | tf_op jit(solution)/shard_map/all_to_all | solution.py:301
  193.6 46.7 %collective-permute-done.22 = bf16[64,2048]{1,0:T(8,128)(2,1)S(1)} collective-permute-done((bf16[64,2048]{1,0:T(8,128)(2,1)}, bf16[64,2048]{1,0:T(8,128)(2,1)S(1)}, u32[]{:S(2)}, u32[]{:S(2)}) %collective-permute-start.22) | collective-permute-done | bytes 262176 | tf_op jit(solution)/shard_map/ppermute | solution.py:76
  241.7 18.3 %collective-permute-start.27 = (bf16[128,2048]{1,0:T(8,128)(2,1)S(1)}, bf16[128,2048]{1,0:T(8,128)(2,1)S(1)}, u32[]{:S(2)}, u32[]{:S(2)}) collective-permute-start(bf16[128,2048]{1,0:T(8,128)(2,1)S(1)} %get-tuple-element.397), channel_id=1, source_target_pairs={{0,2},{2,4},{4,6},{6,7},{7,5},{5,3},{3,1},{1,0},{8,10},{10,12},{12... | collective-permute-start | bytes 1572872 | tf_op jit(solution)/shard_map/ppermute | solution.py:76
  261.5 8.9 collective-permute-done.27
  283.1 8.0 collective-permute-done.30
  301.4 8.6 collective-permute-done.32
  318.4 7.5 collective-permute-done.35.refs_1_
  354.4 8.6 collective-permute-done.42.refs_6_
  395.4 11.4 %dispatch.2 = (bf16[4,640,2048]{2,1,0:T(8,128)(2,1)}, f32[8,4,128]{2,1,0:T(4,128)}, bf16[1024,2048]{1,0:T(8,128)(2,1)}) custom-call(s32[8,4,128]{2,1,0:T(4,128)} %copy.91.rank, bf16[128,2048]{1,0:T(8,128)(2,1)} %copy-done.39, bf16[128,2048]{1,0:T(8,128)(2,1)} %copy-done.69, bf16[128,2048]{1,0:T(8,128)(2,1)} %copy-done.71, bf16[128,2048]{1,0:T(8,128)(2,1)} %copy-done.44, ...), custom_call_target="tpu_custom_call" | custom-call | flops 1150000000 | bytes 65536 | tf_op jit(solution)/shard_map/dispatch/pallas_call | solution.py:715
  411.0 10.3 %collective-permute-done.48.refs_2_ = bf16[128,2048]{1,0:T(8,128)(2,1)S(1)} collective-permute-done((bf16[128,2048]{1,0:T(8,128)(2,1)}, bf16[128,2048]{1,0:T(8,128)(2,1)S(1)}, u32[]{:S(2)}, u32[]{:S(2)}) %collective-permute-start.48) | collective-permute-done | bytes 524320 | tf_op jit(solution)/shard_map/ppermute | solution.py:76
  427.5 20.9 %expert_forward.2 = (bf16[2,640,704]{2,1,0:T(8,128)(2,1)}, bf16[2,640,704]{2,1,0:T(8,128)(2,1)}, bf16[2,640,704]{2,1,0:T(8,128)(2,1)}, bf16[2,640,2048]{2,1,0:T(8,128)(2,1)}) custom-call(s32[4,8,128]{2,1,0:T(8,128)} %bitcast.228, f32[4,8,128]{2,1,0:T(8,128)} %bitcast.234, bf16[4,640,2048]{2,1,0:T(8,128)(2,1)} %get-tuple-element.444.rows_in, ...), custom_call_target="tpu_custom_call" | custom-call | flops 2300000000 | bytes 65536 | tf_op jit(solution)/shard_map/expert_forward/pallas_call | solution.py:877
  453.8 20.6 %expert_forward.3 = (bf16[2,640,704]{2,1,0:T(8,128)(2,1)}, bf16[2,640,704]{2,1,0:T(8,128)(2,1)}, bf16[2,640,704]{2,1,0:T(8,128)(2,1)}, bf16[2,640,2048]{2,1,0:T(8,128)(2,1)}) custom-call(s32[4,8,128]{2,1,0:T(8,128)} %bitcast.229, f32[4,8,128]{2,1,0:T(8,128)} %bitcast.235, bf16[4,640,2048]{2,1,0:T(8,128)(2,1)} %get-tuple-element.444.rows_in, ...), custom_call_target="tpu_custom_call" | custom-call | flops 2300000000 | bytes 65536 | tf_op jit(solution)/shard_map/expert_forward/pallas_call | solution.py:877
  478.7 9.8 combine.2
  492.0 9.4 dispatch.3.cot
  502.8 24.2 %expert_backward.3 = (bf16[2,640,704]{2,1,0:T(8,128)(2,1)}, bf16[2,640,704]{2,1,0:T(8,128)(2,1)}, bf16[2,640,2048]{2,1,0:T(8,128)(2,1)}, f32[2,8,128]{2,1,0:T(8,128)}) custom-call(s32[4,8,128]{2,1,0:T(8,128)} %bitcast.230, f32[4,8,128]{2,1,0:T(8,128)} %bitcast.236, bf16[4,640,2048]{2,1,0:T(8,128)(2,1)} %dispatch.3.cot, ...), custom_call_target="tpu_custom_call" | custom-call | flops 2300000000 | bytes 65536 | tf_op jit(solution)/shard_map/expert_backward/pallas_call | solution.py:877
  538.2 7.9 collective-permute-done.73
  554.3 14.6 %expert_backward.4 = (bf16[1,640,704]{2,1,0:T(8,128)(2,1)}, bf16[1,640,704]{2,1,0:T(8,128)(2,1)}, bf16[1,640,2048]{2,1,0:T(8,128)(2,1)}, f32[1,8,128]{2,1,0:T(8,128)}) custom-call(s32[4,8,128]{2,1,0:T(8,128)} %bitcast.231, f32[4,8,128]{2,1,0:T(8,128)} %bitcast.237, bf16[4,640,2048]{2,1,0:T(8,128)(2,1)} %dispatch.3.cot, ...), custom_call_target="tpu_custom_call" | custom-call | flops 1150000000 | bytes 65536 | tf_op jit(solution)/shard_map/expert_backward/pallas_call | solution.py:877
  574.8 14.6 %expert_backward.5 = (bf16[1,640,704]{2,1,0:T(8,128)(2,1)}, bf16[1,640,704]{2,1,0:T(8,128)(2,1)}, bf16[1,640,2048]{2,1,0:T(8,128)(2,1)}, f32[1,8,128]{2,1,0:T(8,128)}) custom-call(s32[4,8,128]{2,1,0:T(8,128)} %bitcast.232, f32[4,8,128]{2,1,0:T(8,128)} %bitcast.238, bf16[4,640,2048]{2,1,0:T(8,128)(2,1)} %dispatch.3.cot, ...), custom_call_target="tpu_custom_call" | custom-call | flops 1150000000 | bytes 65536 | tf_op jit(solution)/shard_map/expert_backward/pallas_call | solution.py:877
  594.8 11.8 %combine.3 = (bf16[1024,2048]{1,0:T(8,128)(2,1)}, f32[16,2048]{1,0:T(8,128)}) custom-call(s32[1024,4]{1,0:T(8,128)} %bitcast.205, f32[8,4,128]{2,1,0:T(4,128)} %maximum_bitcast_fusion.refs_0_, f32[8,4,128]{2,1,0:T(4,128)} %get-tuple-element.434.refs_1_, bf16[16,2048]{1,0:T(8,128)(2,1)} %pad.17.refs_9_.refs_2_, ...), custom_call_target="tpu_custom_call" | custom-call | flops 1150000000 | bytes 65536 | tf_op jit(solution)/shard_map/combine/pallas_call | solution.py:934
  624.8 10.3 %collective-permute-done.85 = bf16[128,2048]{1,0:T(8,128)(2,1)S(1)} collective-permute-done((bf16[128,2048]{1,0:T(8,128)(2,1)S(1)}, bf16[128,2048]{1,0:T(8,128)(2,1)S(1)}, u32[]{:S(2)}, u32[]{:S(2)}) %collective-permute-start.85) | collective-permute-done | bytes 524320 | tf_op jit(solution)/shard_map/ppermute | solution.py:76
  650.0 9.3 collective-permute-done.88
  730.2 13.6 %collective-permute-done.97.refs_2_ = bf16[128,2048]{1,0:T(8,128)(2,1)S(1)} collective-permute-done((bf16[128,2048]{1,0:T(8,128)(2,1)}, bf16[128,2048]{1,0:T(8,128)(2,1)S(1)}, u32[]{:S(2)}, u32[]{:S(2)}) %collective-permute-start.97) | collective-permute-done | bytes 524320 | tf_op jit(solution)/shard_map/ppermute | solution.py:76
  753.1 11.6 %collective-permute-start.102 = (bf16[128,2048]{1,0:T(8,128)(2,1)}, bf16[128,2048]{1,0:T(8,128)(2,1)S(1)}, u32[]{:S(2)}, u32[]{:S(2)}) collective-permute-start(bf16[128,2048]{1,0:T(8,128)(2,1)} %copy-done.62), channel_id=1, source_target_pairs={{0,2},{2,4},{4,6},{6,7},{7,5},{5,3},{3,1},{1,0},{8,10},{10,12},{12... | collective-permute-start | bytes 1572872 | tf_op jit(solution)/shard_map/ppermute | solution.py:76
  798.1 47.5 %attend_back.1 = (bf16[1024,2048]{1,0:T(8,128)(2,1)}, bf16[1024,1536]{1,0:T(8,128)(2,1)}, f32[16,2048]{1,0:T(8,128)}, bf16[1024,2048]{1,0:T(8,128)(2,1)}) custom-call(s32[1,4]{1,0:T(1,128)} %bitcast.245, bf16[128,2048]{1,0:T(8,128)(2,1)} %copy-done.38, bf16[128,2048]{1,0:T(8,128)(2,1)} %collective-permute-done.93.refs_1_, bf16[128,2048]{1,0:T(8,128)(2,1)} %copy-done.62, ...), custom_call_target="tpu_custom_call" | custom-call | flops 5175000064 | bytes 65536 | tf_op jit(solution)/shard_map/attend_back/pallas_call | solution.py:584
  849.2 10.0 %convolution_convert_fusion = bf16[2048,1536]{1,0:T(8,128)(2,1)S(1)} fusion(bf16[1024,2048]{1,0:T(8,128)(2,1)} %get-tuple-element.585.refs_21_, bf16[1024,1536]{1,0:T(8,128)(2,1)} %get-tuple-element.607), kind=kOutput, calls=%fused_computation.6 | convolution fusion | flops 6445596672 | bytes 13631488 | tf_op jit(solution)/shard_map/dot_general | solution.py:22
  881.3 11.1 %collective-permute-done.120 = f32[10,2048]{1,0:T(8,128)S(1)} collective-permute-done((f32[10,2048]{1,0:T(8,128)S(1)}, f32[10,2048]{1,0:T(8,128)S(1)}, u32[]{:S(2)}, u32[]{:S(2)}) %collective-permute-start.120) | collective-permute-done | bytes 81952 | tf_op jit(solution)/shard_map/ppermute | solution.py:306
  916.1 11.1 %collective-permute-done.122 = bf16[128,2048]{1,0:T(8,128)(2,1)S(1)} collective-permute-done((bf16[128,2048]{1,0:T(8,128)(2,1)}, bf16[128,2048]{1,0:T(8,128)(2,1)S(1)}, u32[]{:S(2)}, u32[]{:S(2)}) %collective-permute-start.122) | collective-permute-done | bytes 524320 | tf_op jit(solution)/shard_map/ppermute | solution.py:76
  (631 shorter events, 508.4 us)
Async XLA Ops:
  8.3 46.3 %all-to-all-start = ((bf16[8,384,256]{2,1,0:T(8,128)(2,1)}), bf16[8,384,256]{2,1,0:T(8,128)(2,1)S(1)}, u32[]{:S(2)}, u32[]{:S(2)}) async-start(bf16[8,384,256]{2,1,0:T(8,128)(2,1)} %pad_maximum_fusion), calls=%async_computation | async-start | bytes 3145728 | tf_op jit(solution)/shard_map/all_to_all | solution.py:301
  15.7 38.9 %collective-permute-start.2 = (bf16[256,2048]{1,0:T(8,128)(2,1)}, bf16[256,2048]{1,0:T(8,128)(2,1)}, u32[]{:S(2)}, u32[]{:S(2)}) collective-permute-start(bf16[256,2048]{1,0:T(8,128)(2,1)} %bitcast.206), channel_id=1, source_target_pairs={{0,16},{8,24},{16,0},{24,8},{1,17},{9,25},{17,1},{25,9},{2,18},{10... | collective-permute-start | bytes 3145736 | tf_op jit(solution)/shard_map/ppermute | solution.py:222
  17.2 35.8 %collective-permute-start = (bf16[128,2048]{1,0:T(8,128)(2,1)S(1)}, bf16[128,2048]{1,0:T(8,128)(2,1)}, u32[]{:S(2)}, u32[]{:S(2)}) collective-permute-start(bf16[128,2048]{1,0:T(8,128)(2,1)S(1)} %fusion.19.refs_0_), channel_id=1, source_target_pairs={{0,2},{2,4},{4,6},{6,7},{7,5},{5,3},{3,1},{1,0},{8,10},{10,12},{12... | collective-permute-start | bytes 1572872 | tf_op jit(solution)/shard_map/ppermute | solution.py:76
  19.3 35.3 %collective-permute-start.1 = (bf16[128,2048]{1,0:T(8,128)(2,1)S(1)}, bf16[128,2048]{1,0:T(8,128)(2,1)}, u32[]{:S(2)}, u32[]{:S(2)}) collective-permute-start(bf16[128,2048]{1,0:T(8,128)(2,1)S(1)} %fusion.19.refs_0_), channel_id=1, source_target_pairs={{0,1},{2,0},{4,2},{6,4},{7,6},{5,7},{3,5},{1,3},{8,9},{10,8},{12,1... | collective-permute-start | bytes 1572872 | tf_op jit(solution)/shard_map/ppermute | solution.py:76
  111.2 67.1 %all-to-all-start.1 = ((bf16[8,704,256]{2,1,0:T(8,128)(2,1)}), bf16[8,704,256]{2,1,0:T(8,128)(2,1)}, u32[]{:S(2)}, u32[]{:S(2)}) async-start(bf16[8,704,256]{2,1,0:T(8,128)(2,1)} %get-tuple-element.383), calls=%async_computation.1 | async-start | bytes 5767168 | tf_op jit(solution)/shard_map/all_to_all | solution.py:301
  121.9 39.5 %collective-permute-start.19 = (bf16[704,512]{1,0:T(8,128)(2,1)}, bf16[704,512]{1,0:T(8,128)(2,1)}, u32[]{:S(2)}, u32[]{:S(2)}) collective-permute-start(bf16[704,512]{1,0:T(8,128)(2,1)} %get-tuple-element.384), channel_id=1, source_target_pairs={{0,16},{8,24},{16,0},{24,8},{1,17},{9,25},{17,1},{25,9},{2,18},{10... | collective-permute-start | bytes 2162696 | tf_op jit(solution)/shard_map/ppermute | solution.py:222
  123.7 37.7 %collective-permute-start.20 = (bf16[704,512]{1,0:T(8,128)(2,1)}, bf16[704,512]{1,0:T(8,128)(2,1)}, u32[]{:S(2)}, u32[]{:S(2)}) collective-permute-start(bf16[704,512]{1,0:T(8,128)(2,1)} %get-tuple-element.385), channel_id=1, source_target_pairs={{0,16},{8,24},{16,0},{24,8},{1,17},{9,25},{17,1},{25,9},{2,18},{10... | collective-permute-start | bytes 2162696 | tf_op jit(solution)/shard_map/ppermute | solution.py:222
  183.5 93.6 %all-to-all-start.2 = ((bf16[8,704,256]{2,1,0:T(8,128)(2,1)}), bf16[8,704,256]{2,1,0:T(8,128)(2,1)}, u32[]{:S(2)}, u32[]{:S(2)}) async-start(bf16[8,704,256]{2,1,0:T(8,128)(2,1)} %get-tuple-element.398), calls=%async_computation.2 | async-start | bytes 5767168 | tf_op jit(solution)/shard_map/all_to_all | solution.py:301
  188.0 52.3 %collective-permute-start.22 = (bf16[64,2048]{1,0:T(8,128)(2,1)}, bf16[64,2048]{1,0:T(8,128)(2,1)S(1)}, u32[]{:S(2)}, u32[]{:S(2)}) collective-permute-start(bf16[64,2048]{1,0:T(8,128)(2,1)} %get-tuple-element.390), channel_id=1, source_target_pairs={{0,2},{2,4},{4,6},{6,7},{7,5},{5,3},{3,1},{1,0},{8,10},{10,12},{12... | collective-permute-start | bytes 786440 | tf_op jit(solution)/shard_map/ppermute | solution.py:76
  189.9 50.4 %collective-permute-start.21 = (bf16[64,2048]{1,0:T(8,128)(2,1)}, bf16[64,2048]{1,0:T(8,128)(2,1)S(1)}, u32[]{:S(2)}, u32[]{:S(2)}) collective-permute-start(bf16[64,2048]{1,0:T(8,128)(2,1)} %get-tuple-element.389), channel_id=1, source_target_pairs={{0,1},{2,0},{4,2},{6,4},{7,6},{5,7},{3,5},{1,3},{8,9},{10,8},{12,1... | collective-permute-start | bytes 786440 | tf_op jit(solution)/shard_map/ppermute | solution.py:76
  190.0 51.6 %collective-permute-start.23 = (bf16[2,704,256]{2,1,0:T(8,128)(2,1)}, bf16[2,704,256]{2,1,0:T(8,128)(2,1)S(1)}, u32[]{:S(2)}, u32[]{:S(2)}) collective-permute-start(bf16[2,704,256]{2,1,0:T(8,128)(2,1)} %get-tuple-element.391), channel_id=1, source_target_pairs={{0,16},{8,24},{16,0},{24,8},{1,17},{9,25},{17,1},{25,9},{2,18},{10... | collective-permute-start | bytes 2162696 | tf_op jit(solution)/shard_map/ppermute | solution.py:222
  191.5 50.1 %collective-permute-start.24 = (bf16[2,704,256]{2,1,0:T(8,128)(2,1)}, bf16[2,704,256]{2,1,0:T(8,128)(2,1)S(1)}, u32[]{:S(2)}, u32[]{:S(2)}) collective-permute-start(bf16[2,704,256]{2,1,0:T(8,128)(2,1)} %get-tuple-element.392), channel_id=1, source_target_pairs={{0,16},{8,24},{16,0},{24,8},{1,17},{9,25},{17,1},{25,9},{2,18},{10... | collective-permute-start | bytes 2162696 | tf_op jit(solution)/shard_map/ppermute | solution.py:222
  192.1 49.6 %collective-permute-start.25 = (bf16[2,704,256]{2,1,0:T(8,128)(2,1)}, bf16[2,704,256]{2,1,0:T(8,128)(2,1)S(1)}, u32[]{:S(2)}, u32[]{:S(2)}) collective-permute-start(bf16[2,704,256]{2,1,0:T(8,128)(2,1)} %get-tuple-element.393), channel_id=1, source_target_pairs={{0,16},{8,24},{16,0},{24,8},{1,17},{9,25},{17,1},{25,9},{2,18},{10... | collective-permute-start | bytes 2162696 | tf_op jit(solution)/shard_map/ppermute | solution.py:222
  241.7 28.7 %collective-permute-start.27 = (bf16[128,2048]{1,0:T(8,128)(2,1)S(1)}, bf16[128,2048]{1,0:T(8,128)(2,1)S(1)}, u32[]{:S(2)}, u32[]{:S(2)}) collective-permute-start(bf16[128,2048]{1,0:T(8,128)(2,1)S(1)} %get-tuple-element.397), channel_id=1, source_target_pairs={{0,2},{2,4},{4,6},{6,7},{7,5},{5,3},{3,1},{1,0},{8,10},{10,12},{12... | collective-permute-start | bytes 1572872 | tf_op jit(solution)/shard_map/ppermute | solution.py:76
  318.4 62.6 %collective-permute-start.52 = (bf16[704,2048]{1,0:T(8,128)(2,1)S(1)}, bf16[704,2048]{1,0:T(8,128)(2,1)S(1)}, u32[]{:S(2)}, u32[]{:S(2)}) collective-permute-start(bf16[704,2048]{1,0:T(8,128)(2,1)S(1)} %bitcast.196), channel_id=1, source_target_pairs={{0,8},{8,0},{16,24},{24,16},{1,9},{9,1},{17,25},{25,17},{2,10},{10... | collective-permute-start | bytes 8650760 | tf_op jit(solution)/shard_map/ppermute | solution.py:216
  346.6 63.8 %collective-permute-start.50 = (bf16[8,704,256]{2,1,0:T(8,128)(2,1)}, bf16[8,704,256]{2,1,0:T(8,128)(2,1)}, u32[]{:S(2)}, u32[]{:S(2)}) collective-permute-start(bf16[8,704,256]{2,1,0:T(8,128)(2,1)} %all-to-all-done.1.refs_0_), channel_id=1, source_target_pairs={{0,8},{8,0},{16,24},{24,16},{1,9},{9,1},{17,25},{25,17},{2,10},{10... | collective-permute-start | bytes 8650760 | tf_op jit(solution)/shard_map/ppermute | solution.py:216
  346.6 63.8 %collective-permute-start.51 = (bf16[8,704,256]{2,1,0:T(8,128)(2,1)}, bf16[8,704,256]{2,1,0:T(8,128)(2,1)}, u32[]{:S(2)}, u32[]{:S(2)}) collective-permute-start(bf16[8,704,256]{2,1,0:T(8,128)(2,1)} %all-to-all-done.2.refs_1_), channel_id=1, source_target_pairs={{0,8},{8,0},{16,24},{24,16},{1,9},{9,1},{17,25},{25,17},{2,10},{10... | collective-permute-start | bytes 8650760 | tf_op jit(solution)/shard_map/ppermute | solution.py:216
  410.4 38.0 %collective-permute-start.58 = (bf16[2,704,256]{2,1,0:T(8,128)(2,1)S(1)}, bf16[2,704,256]{2,1,0:T(8,128)(2,1)}, u32[]{:S(2)}, u32[]{:S(2)}) collective-permute-start(bf16[2,704,256]{2,1,0:T(8,128)(2,1)S(1)} %copy-done.21), channel_id=1, source_target_pairs={{0,8},{8,0},{16,24},{24,16},{1,9},{9,1},{17,25},{25,17},{2,10},{10... | collective-permute-start | bytes 2162696 | tf_op jit(solution)/shard_map/ppermute | solution.py:216
  410.5 38.6 %collective-permute-start.59 = (bf16[2,704,256]{2,1,0:T(8,128)(2,1)}, bf16[2,704,256]{2,1,0:T(8,128)(2,1)}, u32[]{:S(2)}, u32[]{:S(2)}) collective-permute-start(bf16[2,704,256]{2,1,0:T(8,128)(2,1)} %collective-permute-done.28.refs_3_), channel_id=1, source_target_pairs={{0,8},{8,0},{16,24},{24,16},{1,9},{9,1},{17,25},{25,17},{2,10},{10... | collective-permute-start | bytes 2162696 | tf_op jit(solution)/shard_map/ppermute | solution.py:216
  678.0 30.7 %collective-permute-start.96 = (bf16[704,512]{1,0:T(8,128)(2,1)}, bf16[704,512]{1,0:T(8,128)(2,1)}, u32[]{:S(2)}, u32[]{:S(2)}) collective-permute-start(bf16[704,512]{1,0:T(8,128)(2,1)} %get-tuple-element.544), channel_id=1, source_target_pairs={{0,16},{8,24},{16,0},{24,8},{1,17},{9,25},{17,1},{25,9},{2,18},{10... | collective-permute-start | bytes 2162696 | tf_op jit(solution)/shard_map/ppermute | solution.py:222
  681.1 71.3 %all-to-all-start.3 = ((bf16[8,704,256]{2,1,0:T(8,128)(2,1)}), bf16[8,704,256]{2,1,0:T(8,128)(2,1)}, u32[]{:S(2)}, u32[]{:S(2)}) async-start(bf16[8,704,256]{2,1,0:T(8,128)(2,1)} %bitcast.199), calls=%async_computation.3 | async-start | bytes 5767168 | tf_op jit(solution)/shard_map/all_to_all | solution.py:301
  711.3 53.3 %collective-permute-start.104 = (bf16[704,2048]{1,0:T(8,128)(2,1)}, bf16[704,2048]{1,0:T(8,128)(2,1)}, u32[]{:S(2)}, u32[]{:S(2)}) collective-permute-start(bf16[704,2048]{1,0:T(8,128)(2,1)} %convolution_convert_fusion.7), channel_id=1, source_target_pairs={{0,8},{8,0},{16,24},{24,16},{1,9},{9,1},{17,25},{25,17},{2,10},{10... | collective-permute-start | bytes 8650760 | tf_op jit(solution)/shard_map/ppermute | solution.py:216
  711.8 32.0 %collective-permute-start.97 = (bf16[128,2048]{1,0:T(8,128)(2,1)}, bf16[128,2048]{1,0:T(8,128)(2,1)S(1)}, u32[]{:S(2)}, u32[]{:S(2)}) collective-permute-start(bf16[128,2048]{1,0:T(8,128)(2,1)} %collective-permute-done.93.refs_1_), channel_id=1, source_target_pairs={{0,2},{2,4},{4,6},{6,7},{7,5},{5,3},{3,1},{1,0},{8,10},{10,12},{12... | collective-permute-start | bytes 1572872 | tf_op jit(solution)/shard_map/ppermute | solution.py:76
  712.4 31.4 %collective-permute-start.98 = (bf16[128,2048]{1,0:T(8,128)(2,1)}, bf16[128,2048]{1,0:T(8,128)(2,1)S(1)}, u32[]{:S(2)}, u32[]{:S(2)}) collective-permute-start(bf16[128,2048]{1,0:T(8,128)(2,1)} %collective-permute-done.94.refs_8_), channel_id=1, source_target_pairs={{0,1},{2,0},{4,2},{6,4},{7,6},{5,7},{3,5},{1,3},{8,9},{10,8},{12,1... | collective-permute-start | bytes 1572872 | tf_op jit(solution)/shard_map/ppermute | solution.py:76
  714.1 29.7 %collective-permute-start.100 = (bf16[704,512]{1,0:T(8,128)(2,1)S(1)}, bf16[704,512]{1,0:T(8,128)(2,1)S(1)}, u32[]{:S(2)}, u32[]{:S(2)}) collective-permute-start(bf16[704,512]{1,0:T(8,128)(2,1)S(1)} %copy-done.57), channel_id=1, source_target_pairs={{0,16},{8,24},{16,0},{24,8},{1,17},{9,25},{17,1},{25,9},{2,18},{10... | collective-permute-start | bytes 2162696 | tf_op jit(solution)/shard_map/ppermute | solution.py:222
  788.5 57.1 %collective-permute-start.108 = (bf16[704,512]{1,0:T(8,128)(2,1)}, bf16[704,512]{1,0:T(8,128)(2,1)}, u32[]{:S(2)}, u32[]{:S(2)}) collective-permute-start(bf16[704,512]{1,0:T(8,128)(2,1)} %get-tuple-element.595), channel_id=1, source_target_pairs={{0,16},{8,24},{16,0},{24,8},{1,17},{9,25},{17,1},{25,9},{2,18},{10... | collective-permute-start | bytes 2162696 | tf_op jit(solution)/shard_map/ppermute | solution.py:222
  789.2 56.4 %collective-permute-start.109 = (bf16[704,512]{1,0:T(8,128)(2,1)}, bf16[704,512]{1,0:T(8,128)(2,1)}, u32[]{:S(2)}, u32[]{:S(2)}) collective-permute-start(bf16[704,512]{1,0:T(8,128)(2,1)} %get-tuple-element.596), channel_id=1, source_target_pairs={{0,16},{8,24},{16,0},{24,8},{1,17},{9,25},{17,1},{25,9},{2,18},{10... | collective-permute-start | bytes 2162696 | tf_op jit(solution)/shard_map/ppermute | solution.py:222
  790.5 55.1 %collective-permute-start.110 = (bf16[704,512]{1,0:T(8,128)(2,1)}, bf16[704,512]{1,0:T(8,128)(2,1)}, u32[]{:S(2)}, u32[]{:S(2)}) collective-permute-start(bf16[704,512]{1,0:T(8,128)(2,1)} %get-tuple-element.597), channel_id=1, source_target_pairs={{0,16},{8,24},{16,0},{24,8},{1,17},{9,25},{17,1},{25,9},{2,18},{10... | collective-permute-start | bytes 2162696 | tf_op jit(solution)/shard_map/ppermute | solution.py:222
  792.9 83.0 %all-to-all-start.4 = ((bf16[8,704,256]{2,1,0:T(8,128)(2,1)}), bf16[8,704,256]{2,1,0:T(8,128)(2,1)}, u32[]{:S(2)}, u32[]{:S(2)}) async-start(bf16[8,704,256]{2,1,0:T(8,128)(2,1)} %bitcast.198), calls=%async_computation.4 | async-start | bytes 5767168 | tf_op jit(solution)/shard_map/all_to_all | solution.py:301
  881.3 62.2 %collective-permute-start.134 = (bf16[704,2048]{1,0:T(8,128)(2,1)}, bf16[704,2048]{1,0:T(8,128)(2,1)}, u32[]{:S(2)}, u32[]{:S(2)}) collective-permute-start(bf16[704,2048]{1,0:T(8,128)(2,1)} %convolution_convert_fusion.6), channel_id=1, source_target_pairs={{0,8},{8,0},{16,24},{24,16},{1,9},{9,1},{17,25},{25,17},{2,10},{10... | collective-permute-start | bytes 8650760 | tf_op jit(solution)/shard_map/ppermute | solution.py:216
  916.1 43.4 %collective-permute-start.131 = (bf16[256,2048]{1,0:T(8,128)(2,1)}, bf16[256,2048]{1,0:T(8,128)(2,1)}, u32[]{:S(2)}, u32[]{:S(2)}) collective-permute-start(bf16[256,2048]{1,0:T(8,128)(2,1)} %get-tuple-element.673), channel_id=1, source_target_pairs={{0,8},{8,0},{16,24},{24,16},{1,9},{9,1},{17,25},{25,17},{2,10},{10... | collective-permute-start | bytes 3145736 | tf_op jit(solution)/shard_map/ppermute | solution.py:216
  932.7 40.8 %all-to-all-start.5 = ((bf16[8,384,256]{2,1,0:T(8,128)(2,1)}), bf16[8,384,256]{2,1,0:T(8,128)(2,1)S(1)}, u32[]{:S(2)}, u32[]{:S(2)}) async-start(bf16[8,384,256]{2,1,0:T(8,128)(2,1)} %add_convert_fusion.8), calls=%async_computation.5 | async-start | bytes 3145728 | tf_op jit(solution)/shard_map/all_to_all | solution.py:301
  (213 other events, 3811.6 us)

commit v5 on v4

--- a/solution.py
+++ b/solution.py
@@ -245,6 +245,7 @@
 
 
 PARTS = 4
+PAIR = 2
 
 
 def part_of(value, which, parts=PARTS):
@@ -897,45 +898,52 @@
         *parts, out, small = refs
     else:
         *parts, out = refs
+    rows = rows // PAIR
     slot = lax.broadcasted_iota(jnp.int32, (rows, experts * capacity), 1)
-    pick = jnp.zeros(slot.shape, F32)
-    for k in range(experts):
-        at = jnp.where(rank[:, k : k + 1] >= 0, rank[:, k : k + 1] + k * capacity, -1)
-        pick = pick + (slot == at).astype(F32)
-    data = jnp.concatenate([part[i] for part in parts for i in range(part.shape[0])], axis=0)
-    total = dot(pick.astype(BF16), data)
     if extra:
-        grads = sums[0] - gates[0] * jnp.sum(sums[0], axis=0, keepdims=True)
-        pad = router.shape[0] - experts
-        grads = jnp.concatenate([grads, jnp.zeros((pad, rows), F32)], axis=0).astype(BF16)
-        total = total + dot(grads, router[...], ((0,), (0,)))
 
         @pl.when(pl.program_id(0) == 0)
         def _():
             small[...] = jnp.zeros_like(small)
 
-        small[...] += dot(grads, hidden[...])
-    out[...] = total.astype(BF16)
+    for b in range(PAIR):
+        here = slice(b * rows, (b + 1) * rows)
+        ranks = rank[here, :]
+        pick = jnp.zeros(slot.shape, F32)
+        for k in range(experts):
+            at = jnp.where(ranks[:, k : k + 1] >= 0, ranks[:, k : k + 1] + k * capacity, -1)
+            pick = pick + (slot == at).astype(F32)
+        mine = slice(b * capacity, (b + 1) * capacity)
+        data = jnp.concatenate([part[i, mine, :] for part in parts for i in range(part.shape[0])], axis=0)
+        total = dot(pick.astype(BF16), data)
+        if extra:
+            grads = sums[b] - gates[b] * jnp.sum(sums[b], axis=0, keepdims=True)
+            pad = router.shape[0] - experts
+            grads = jnp.concatenate([grads, jnp.zeros((pad, rows), F32)], axis=0).astype(BF16)
+            total = total + dot(grads, router[...], ((0,), (0,)))
+            small[...] += dot(grads, hidden[here, :])
+        out[here, :] = total.astype(BF16)
 
 
 def combine(rank_cols, parts, rows, capacity, extra=()):
     total_rows, experts = rank_cols.shape
     width = parts[0].shape[2]
-    out_specs = [tiles((rows, width))]
+    out_specs = [tiles((PAIR * rows, width))]
     out_shape = [jax.ShapeDtypeStruct((total_rows, width), BF16)]
-    in_specs = [tiles((rows, experts))]
+    in_specs = [tiles((PAIR * rows, experts))]
     if extra:
         router = extra[2]
         in_specs += [
-            tiles((1, experts, rows)), tiles((1, experts, rows)), whole(router.shape), tiles((rows, width)),
+            tiles((PAIR, experts, rows)), tiles((PAIR, experts, rows)), whole(router.shape),
+            tiles((PAIR * rows, width)),
         ]
         out_specs.append(whole(router.shape))
         out_shape.append(jax.ShapeDtypeStruct(router.shape, F32))
     return pl.pallas_call(
         functools.partial(combine_kernel, capacity, bool(extra)),
-        grid=(total_rows // rows,),
+        grid=(total_rows // rows // PAIR,),
         in_specs=in_specs
-        + [pl.BlockSpec((part.shape[0], capacity, width), lambda i: (0, i, 0)) for part in parts],
+        + [pl.BlockSpec((part.shape[0], PAIR * capacity, width), lambda i: (0, i, 0)) for part in parts],
         out_specs=out_specs,
         out_shape=out_shape,
         compiler_params=pltpu.CompilerParams(vmem_limit_bytes=VMEM_LIMIT),

time: 1000 us -> 998 us (level)
  transfers between devices with their start and end apart: 141 -> 141, of which waited for: 67 -> 68; matrix products, arithmetic and copies ran while one was open for 16% -> 16% of each run, Pallas kernels for 21% -> 21%
where the time goes in v5:
time: 998 us; the launch traced here: 991 us
  waiting for transfers between devices  368 us (37%)
  Pallas kernels  228 us (23%)
  starting transfers between devices  192 us (19%)
  matrix products  69.6 us (7%)
  local copies, waits for them, and re-layouts  67.4 us (7%)
  other arithmetic  62.9 us (6%)
    ppermute x64, waiting for transfers between devices, ring_move(): lax.ppermute(value, 'shard', [(cycle[i], cycle[(i + hops) % count]) for i...  241 us
    ppermute x64, starting transfers between devices, ring_move(): lax.ppermute(value, 'shard', [(cycle[i], cycle[(i + hops) % count]) for i...  104 us
    pallas_call x5, Pallas kernels, expert_call(): pl.pallas_call(functools.partial(kernel, capacity, layout), grid=(count,)...  95.1 us
    dot_general x14, matrix products, dot(): lax.dot_general(left, right, (contract, ((), ())), preferred_element_type...  69.5 us
    pallas_call x1, Pallas kernels, attend_back(): pl.pallas_call(functools.partial(attend_back_kernel, layout, steps, len(b...  47.5 us
    ppermute x31, waiting for transfers between devices, chip_shift(): lax.ppermute(value, 'expert', [(i, (i // 2 + hops) % chips * 2 + i % 2) f...  39.7 us
    ppermute x31, starting transfers between devices, chip_shift(): lax.ppermute(value, 'expert', [(i, (i // 2 + hops) % chips * 2 + i % 2) f...  38.4 us
    pallas_call x1, Pallas kernels, attend(): pl.pallas_call(functools.partial(attend_kernel, layout, len(blocks), chun...  35.1 us
  transfers between devices with their start and end apart: 141, of which 68 were waited for; matrix products, arithmetic and copies ran while one was open for 16% of the time, Pallas kernels for 21%

profile of v5, /device:TPU:0, one launch (start us, length us, event | category | flops | bytes accessed | tf_op | source)
XLA Modules:
  0.0 990.6 jit_solution(17040311786641475587)
XLA Ops:
  31.6 14.6 %collective-permute-done.3 = s32[1,8,128]{2,1,0:T(8,128)S(1)} collective-permute-done((s32[1,8,128]{2,1,0:T(8,128)S(1)}, s32[1,8,128]{2,1,0:T(8,128)S(1)}, u32[]{:S(2)}, u32[]{:S(2)}) %collective-permute-start.3) | collective-permute-done | bytes 4128 | tf_op jit(solution)/shard_map/ppermute | solution.py:205
  57.5 10.0 %collective-permute-start.4 = (bf16[128,2048]{1,0:T(8,128)(2,1)}, bf16[128,2048]{1,0:T(8,128)(2,1)}, u32[]{:S(2)}, u32[]{:S(2)}) collective-permute-start(bf16[128,2048]{1,0:T(8,128)(2,1)} %collective-permute-done.refs_1_), channel_id=1, source_target_pairs={{0,2},{2,4},{4,6},{6,7},{7,5},{5,3},{3,1},{1,0},{8,10},{10,12},{12... | collective-permute-start | bytes 1572872 | tf_op jit(solution)/shard_map/ppermute | solution.py:76
  70.9 9.7 collective-permute-done.7
  91.2 8.6 collective-permute-done.10
  126.3 35.1 %attend.1 = (bf16[1024,2048]{1,0:T(8,128)(2,1)}, bf16[1024,512]{1,0:T(8,128)(2,1)}, bf16[1024,256]{1,0:T(8,128)(2,1)}, bf16[1024,256]{1,0:T(8,128)(2,1)}, bf16[1...) custom-call(s32[1,4]{1,0:T(1,128)} %bitcast.244, ...), custom_call_target="tpu_custom_call" | custom-call | flops 4024999936 | bytes 65536 | tf_op jit(solution)/shard_map/attend/pallas_call | solution.py:436
  161.4 16.9 %all-to-all-done.1.refs_0_ = bf16[8,704,256]{2,1,0:T(8,128)(2,1)} async-done(((bf16[8,704,256]{2,1,0:T(8,128)(2,1)}), bf16[8,704,256]{2,1,0:T(8,128)(2,1)}, u32[]{:S(2)}, u32[]{:S(2)}) %all-to-all-start.1) | async-done | bytes 2883616 | tf_op jit(solution)/shard_map/all_to_all | solution.py:302
  193.6 46.7 %collective-permute-done.22 = bf16[64,2048]{1,0:T(8,128)(2,1)S(1)} collective-permute-done((bf16[64,2048]{1,0:T(8,128)(2,1)}, bf16[64,2048]{1,0:T(8,128)(2,1)S(1)}, u32[]{:S(2)}, u32[]{:S(2)}) %collective-permute-start.22) | collective-permute-done | bytes 262176 | tf_op jit(solution)/shard_map/ppermute | solution.py:76
  241.7 18.3 %collective-permute-start.27 = (bf16[128,2048]{1,0:T(8,128)(2,1)S(1)}, bf16[128,2048]{1,0:T(8,128)(2,1)S(1)}, u32[]{:S(2)}, u32[]{:S(2)}) collective-permute-start(bf16[128,2048]{1,0:T(8,128)(2,1)S(1)} %get-tuple-element.397), channel_id=1, source_target_pairs={{0,2},{2,4},{4,6},{6,7},{7,5},{5,3},{3,1},{1,0},{8,10},{10,12},{12... | collective-permute-start | bytes 1572872 | tf_op jit(solution)/shard_map/ppermute | solution.py:76
  261.5 8.9 collective-permute-done.27
  283.1 8.0 collective-permute-done.30
  301.4 8.6 collective-permute-done.32
  318.4 7.5 collective-permute-done.35.refs_1_
  354.3 8.6 collective-permute-done.42.refs_6_
  395.2 11.4 %dispatch.2 = (bf16[4,640,2048]{2,1,0:T(8,128)(2,1)}, f32[8,4,128]{2,1,0:T(4,128)}, bf16[1024,2048]{1,0:T(8,128)(2,1)}) custom-call(s32[8,4,128]{2,1,0:T(4,128)} %copy.91.rank, bf16[128,2048]{1,0:T(8,128)(2,1)} %copy-done.39, bf16[128,2048]{1,0:T(8,128)(2,1)} %copy-done.69, bf16[128,2048]{1,0:T(8,128)(2,1)} %copy-done.71, bf16[128,2048]{1,0:T(8,128)(2,1)} %copy-done.44, ...), custom_call_target="tpu_custom_call" | custom-call | flops 1150000000 | bytes 65536 | tf_op jit(solution)/shard_map/dispatch/pallas_call | solution.py:716
  410.8 10.3 %collective-permute-done.48.refs_2_ = bf16[128,2048]{1,0:T(8,128)(2,1)S(1)} collective-permute-done((bf16[128,2048]{1,0:T(8,128)(2,1)}, bf16[128,2048]{1,0:T(8,128)(2,1)S(1)}, u32[]{:S(2)}, u32[]{:S(2)}) %collective-permute-start.48) | collective-permute-done | bytes 524320 | tf_op jit(solution)/shard_map/ppermute | solution.py:76
  427.3 20.9 %expert_forward.2 = (bf16[2,640,704]{2,1,0:T(8,128)(2,1)}, bf16[2,640,704]{2,1,0:T(8,128)(2,1)}, bf16[2,640,704]{2,1,0:T(8,128)(2,1)}, bf16[2,640,2048]{2,1,0:T(8,128)(2,1)}) custom-call(s32[4,8,128]{2,1,0:T(8,128)} %bitcast.228, f32[4,8,128]{2,1,0:T(8,128)} %bitcast.234, bf16[4,640,2048]{2,1,0:T(8,128)(2,1)} %get-tuple-element.444.rows_in, ...), custom_call_target="tpu_custom_call" | custom-call | flops 2300000000 | bytes 65536 | tf_op jit(solution)/shard_map/expert_forward/pallas_call | solution.py:878
  453.6 20.6 %expert_forward.3 = (bf16[2,640,704]{2,1,0:T(8,128)(2,1)}, bf16[2,640,704]{2,1,0:T(8,128)(2,1)}, bf16[2,640,704]{2,1,0:T(8,128)(2,1)}, bf16[2,640,2048]{2,1,0:T(8,128)(2,1)}) custom-call(s32[4,8,128]{2,1,0:T(8,128)} %bitcast.229, f32[4,8,128]{2,1,0:T(8,128)} %bitcast.235, bf16[4,640,2048]{2,1,0:T(8,128)(2,1)} %get-tuple-element.444.rows_in, ...), custom_call_target="tpu_custom_call" | custom-call | flops 2300000000 | bytes 65536 | tf_op jit(solution)/shard_map/expert_forward/pallas_call | solution.py:878
  478.5 8.0 combine.2
  489.9 9.4 dispatch.3.cot
  500.8 24.2 %expert_backward.3 = (bf16[2,640,704]{2,1,0:T(8,128)(2,1)}, bf16[2,640,704]{2,1,0:T(8,128)(2,1)}, bf16[2,640,2048]{2,1,0:T(8,128)(2,1)}, f32[2,8,128]{2,1,0:T(8,128)}) custom-call(s32[4,8,128]{2,1,0:T(8,128)} %bitcast.230, f32[4,8,128]{2,1,0:T(8,128)} %bitcast.236, bf16[4,640,2048]{2,1,0:T(8,128)(2,1)} %dispatch.3.cot, ...), custom_call_target="tpu_custom_call" | custom-call | flops 2300000000 | bytes 65536 | tf_op jit(solution)/shard_map/expert_backward/pallas_call | solution.py:878
  536.2 7.9 collective-permute-done.73
  552.2 14.6 %expert_backward.4 = (bf16[1,640,704]{2,1,0:T(8,128)(2,1)}, bf16[1,640,704]{2,1,0:T(8,128)(2,1)}, bf16[1,640,2048]{2,1,0:T(8,128)(2,1)}, f32[1,8,128]{2,1,0:T(8,128)}) custom-call(s32[4,8,128]{2,1,0:T(8,128)} %bitcast.231, f32[4,8,128]{2,1,0:T(8,128)} %bitcast.237, bf16[4,640,2048]{2,1,0:T(8,128)(2,1)} %dispatch.3.cot, ...), custom_call_target="tpu_custom_call" | custom-call | flops 1150000000 | bytes 65536 | tf_op jit(solution)/shard_map/expert_backward/pallas_call | solution.py:878
  572.8 14.6 %expert_backward.5 = (bf16[1,640,704]{2,1,0:T(8,128)(2,1)}, bf16[1,640,704]{2,1,0:T(8,128)(2,1)}, bf16[1,640,2048]{2,1,0:T(8,128)(2,1)}, f32[1,8,128]{2,1,0:T(8,128)}) custom-call(s32[4,8,128]{2,1,0:T(8,128)} %bitcast.232, f32[4,8,128]{2,1,0:T(8,128)} %bitcast.238, bf16[4,640,2048]{2,1,0:T(8,128)(2,1)} %dispatch.3.cot, ...), custom_call_target="tpu_custom_call" | custom-call | flops 1150000000 | bytes 65536 | tf_op jit(solution)/shard_map/expert_backward/pallas_call | solution.py:878
  592.7 9.7 combine.3
  622.8 9.5 collective-permute-done.85
  647.1 9.3 collective-permute-done.88
  727.4 13.6 %collective-permute-done.97.refs_2_ = bf16[128,2048]{1,0:T(8,128)(2,1)S(1)} collective-permute-done((bf16[128,2048]{1,0:T(8,128)(2,1)}, bf16[128,2048]{1,0:T(8,128)(2,1)S(1)}, u32[]{:S(2)}, u32[]{:S(2)}) %collective-permute-start.97) | collective-permute-done | bytes 524320 | tf_op jit(solution)/shard_map/ppermute | solution.py:76
  751.0 11.6 %collective-permute-start.102 = (bf16[128,2048]{1,0:T(8,128)(2,1)}, bf16[128,2048]{1,0:T(8,128)(2,1)S(1)}, u32[]{:S(2)}, u32[]{:S(2)}) collective-permute-start(bf16[128,2048]{1,0:T(8,128)(2,1)} %copy-done.62), channel_id=1, source_target_pairs={{0,2},{2,4},{4,6},{6,7},{7,5},{5,3},{3,1},{1,0},{8,10},{10,12},{12... | collective-permute-start | bytes 1572872 | tf_op jit(solution)/shard_map/ppermute | solution.py:76
  796.0 47.5 %attend_back.1 = (bf16[1024,2048]{1,0:T(8,128)(2,1)}, bf16[1024,1536]{1,0:T(8,128)(2,1)}, f32[16,2048]{1,0:T(8,128)}, bf16[1024,2048]{1,0:T(8,128)(2,1)}) custom-call(s32[1,4]{1,0:T(1,128)} %bitcast.245, bf16[128,2048]{1,0:T(8,128)(2,1)} %copy-done.38, bf16[128,2048]{1,0:T(8,128)(2,1)} %collective-permute-done.93.refs_1_, bf16[128,2048]{1,0:T(8,128)(2,1)} %copy-done.62, ...), custom_call_target="tpu_custom_call" | custom-call | flops 5175000064 | bytes 65536 | tf_op jit(solution)/shard_map/attend_back/pallas_call | solution.py:585
  847.2 10.0 %convolution_convert_fusion = bf16[2048,1536]{1,0:T(8,128)(2,1)S(1)} fusion(bf16[1024,2048]{1,0:T(8,128)(2,1)} %get-tuple-element.585.refs_21_, bf16[1024,1536]{1,0:T(8,128)(2,1)} %get-tuple-element.607), kind=kOutput, calls=%fused_computation.6 | convolution fusion | flops 6445596672 | bytes 13631488 | tf_op jit(solution)/shard_map/dot_general | solution.py:22
  878.5 11.9 %collective-permute-done.120 = f32[10,2048]{1,0:T(8,128)S(1)} collective-permute-done((f32[10,2048]{1,0:T(8,128)S(1)}, f32[10,2048]{1,0:T(8,128)S(1)}, u32[]{:S(2)}, u32[]{:S(2)}) %collective-permute-start.120) | collective-permute-done | bytes 81952 | tf_op jit(solution)/shard_map/ppermute | solution.py:307
  914.0 10.5 %collective-permute-done.122 = bf16[128,2048]{1,0:T(8,128)(2,1)S(1)} collective-permute-done((bf16[128,2048]{1,0:T(8,128)(2,1)}, bf16[128,2048]{1,0:T(8,128)(2,1)S(1)}, u32[]{:S(2)}, u32[]{:S(2)}) %collective-permute-start.122) | collective-permute-done | bytes 524320 | tf_op jit(solution)/shard_map/ppermute | solution.py:76
  (631 shorter events, 511.0 us)
Async XLA Ops:
  8.3 46.3 %all-to-all-start = ((bf16[8,384,256]{2,1,0:T(8,128)(2,1)}), bf16[8,384,256]{2,1,0:T(8,128)(2,1)S(1)}, u32[]{:S(2)}, u32[]{:S(2)}) async-start(bf16[8,384,256]{2,1,0:T(8,128)(2,1)} %pad_maximum_fusion), calls=%async_computation | async-start | bytes 3145728 | tf_op jit(solution)/shard_map/all_to_all | solution.py:302
  15.7 38.9 %collective-permute-start.2 = (bf16[256,2048]{1,0:T(8,128)(2,1)}, bf16[256,2048]{1,0:T(8,128)(2,1)}, u32[]{:S(2)}, u32[]{:S(2)}) collective-permute-start(bf16[256,2048]{1,0:T(8,128)(2,1)} %bitcast.206), channel_id=1, source_target_pairs={{0,16},{8,24},{16,0},{24,8},{1,17},{9,25},{17,1},{25,9},{2,18},{10... | collective-permute-start | bytes 3145736 | tf_op jit(solution)/shard_map/ppermute | solution.py:222
  17.2 35.8 %collective-permute-start = (bf16[128,2048]{1,0:T(8,128)(2,1)S(1)}, bf16[128,2048]{1,0:T(8,128)(2,1)}, u32[]{:S(2)}, u32[]{:S(2)}) collective-permute-start(bf16[128,2048]{1,0:T(8,128)(2,1)S(1)} %fusion.19.refs_0_), channel_id=1, source_target_pairs={{0,2},{2,4},{4,6},{6,7},{7,5},{5,3},{3,1},{1,0},{8,10},{10,12},{12... | collective-permute-start | bytes 1572872 | tf_op jit(solution)/shard_map/ppermute | solution.py:76
  19.3 35.3 %collective-permute-start.1 = (bf16[128,2048]{1,0:T(8,128)(2,1)S(1)}, bf16[128,2048]{1,0:T(8,128)(2,1)}, u32[]{:S(2)}, u32[]{:S(2)}) collective-permute-start(bf16[128,2048]{1,0:T(8,128)(2,1)S(1)} %fusion.19.refs_0_), channel_id=1, source_target_pairs={{0,1},{2,0},{4,2},{6,4},{7,6},{5,7},{3,5},{1,3},{8,9},{10,8},{12,1... | collective-permute-start | bytes 1572872 | tf_op jit(solution)/shard_map/ppermute | solution.py:76
  111.2 67.1 %all-to-all-start.1 = ((bf16[8,704,256]{2,1,0:T(8,128)(2,1)}), bf16[8,704,256]{2,1,0:T(8,128)(2,1)}, u32[]{:S(2)}, u32[]{:S(2)}) async-start(bf16[8,704,256]{2,1,0:T(8,128)(2,1)} %get-tuple-element.383), calls=%async_computation.1 | async-start | bytes 5767168 | tf_op jit(solution)/shard_map/all_to_all | solution.py:302
  121.9 39.5 %collective-permute-start.19 = (bf16[704,512]{1,0:T(8,128)(2,1)}, bf16[704,512]{1,0:T(8,128)(2,1)}, u32[]{:S(2)}, u32[]{:S(2)}) collective-permute-start(bf16[704,512]{1,0:T(8,128)(2,1)} %get-tuple-element.384), channel_id=1, source_target_pairs={{0,16},{8,24},{16,0},{24,8},{1,17},{9,25},{17,1},{25,9},{2,18},{10... | collective-permute-start | bytes 2162696 | tf_op jit(solution)/shard_map/ppermute | solution.py:222
  123.7 37.7 %collective-permute-start.20 = (bf16[704,512]{1,0:T(8,128)(2,1)}, bf16[704,512]{1,0:T(8,128)(2,1)}, u32[]{:S(2)}, u32[]{:S(2)}) collective-permute-start(bf16[704,512]{1,0:T(8,128)(2,1)} %get-tuple-element.385), channel_id=1, source_target_pairs={{0,16},{8,24},{16,0},{24,8},{1,17},{9,25},{17,1},{25,9},{2,18},{10... | collective-permute-start | bytes 2162696 | tf_op jit(solution)/shard_map/ppermute | solution.py:222
  183.5 93.6 %all-to-all-start.2 = ((bf16[8,704,256]{2,1,0:T(8,128)(2,1)}), bf16[8,704,256]{2,1,0:T(8,128)(2,1)}, u32[]{:S(2)}, u32[]{:S(2)}) async-start(bf16[8,704,256]{2,1,0:T(8,128)(2,1)} %get-tuple-element.398), calls=%async_computation.2 | async-start | bytes 5767168 | tf_op jit(solution)/shard_map/all_to_all | solution.py:302
  188.0 52.3 %collective-permute-start.22 = (bf16[64,2048]{1,0:T(8,128)(2,1)}, bf16[64,2048]{1,0:T(8,128)(2,1)S(1)}, u32[]{:S(2)}, u32[]{:S(2)}) collective-permute-start(bf16[64,2048]{1,0:T(8,128)(2,1)} %get-tuple-element.390), channel_id=1, source_target_pairs={{0,2},{2,4},{4,6},{6,7},{7,5},{5,3},{3,1},{1,0},{8,10},{10,12},{12... | collective-permute-start | bytes 786440 | tf_op jit(solution)/shard_map/ppermute | solution.py:76
  189.9 50.4 %collective-permute-start.21 = (bf16[64,2048]{1,0:T(8,128)(2,1)}, bf16[64,2048]{1,0:T(8,128)(2,1)S(1)}, u32[]{:S(2)}, u32[]{:S(2)}) collective-permute-start(bf16[64,2048]{1,0:T(8,128)(2,1)} %get-tuple-element.389), channel_id=1, source_target_pairs={{0,1},{2,0},{4,2},{6,4},{7,6},{5,7},{3,5},{1,3},{8,9},{10,8},{12,1... | collective-permute-start | bytes 786440 | tf_op jit(solution)/shard_map/ppermute | solution.py:76
  190.0 51.6 %collective-permute-start.23 = (bf16[2,704,256]{2,1,0:T(8,128)(2,1)}, bf16[2,704,256]{2,1,0:T(8,128)(2,1)S(1)}, u32[]{:S(2)}, u32[]{:S(2)}) collective-permute-start(bf16[2,704,256]{2,1,0:T(8,128)(2,1)} %get-tuple-element.391), channel_id=1, source_target_pairs={{0,16},{8,24},{16,0},{24,8},{1,17},{9,25},{17,1},{25,9},{2,18},{10... | collective-permute-start | bytes 2162696 | tf_op jit(solution)/shard_map/ppermute | solution.py:222
  191.5 50.1 %collective-permute-start.24 = (bf16[2,704,256]{2,1,0:T(8,128)(2,1)}, bf16[2,704,256]{2,1,0:T(8,128)(2,1)S(1)}, u32[]{:S(2)}, u32[]{:S(2)}) collective-permute-start(bf16[2,704,256]{2,1,0:T(8,128)(2,1)} %get-tuple-element.392), channel_id=1, source_target_pairs={{0,16},{8,24},{16,0},{24,8},{1,17},{9,25},{17,1},{25,9},{2,18},{10... | collective-permute-start | bytes 2162696 | tf_op jit(solution)/shard_map/ppermute | solution.py:222
  192.1 49.6 %collective-permute-start.25 = (bf16[2,704,256]{2,1,0:T(8,128)(2,1)}, bf16[2,704,256]{2,1,0:T(8,128)(2,1)S(1)}, u32[]{:S(2)}, u32[]{:S(2)}) collective-permute-start(bf16[2,704,256]{2,1,0:T(8,128)(2,1)} %get-tuple-element.393), channel_id=1, source_target_pairs={{0,16},{8,24},{16,0},{24,8},{1,17},{9,25},{17,1},{25,9},{2,18},{10... | collective-permute-start | bytes 2162696 | tf_op jit(solution)/shard_map/ppermute | solution.py:222
  241.7 28.7 %collective-permute-start.27 = (bf16[128,2048]{1,0:T(8,128)(2,1)S(1)}, bf16[128,2048]{1,0:T(8,128)(2,1)S(1)}, u32[]{:S(2)}, u32[]{:S(2)}) collective-permute-start(bf16[128,2048]{1,0:T(8,128)(2,1)S(1)} %get-tuple-element.397), channel_id=1, source_target_pairs={{0,2},{2,4},{4,6},{6,7},{7,5},{5,3},{3,1},{1,0},{8,10},{10,12},{12... | collective-permute-start | bytes 1572872 | tf_op jit(solution)/shard_map/ppermute | solution.py:76
  318.4 62.6 %collective-permute-start.52 = (bf16[704,2048]{1,0:T(8,128)(2,1)S(1)}, bf16[704,2048]{1,0:T(8,128)(2,1)S(1)}, u32[]{:S(2)}, u32[]{:S(2)}) collective-permute-start(bf16[704,2048]{1,0:T(8,128)(2,1)S(1)} %bitcast.196), channel_id=1, source_target_pairs={{0,8},{8,0},{16,24},{24,16},{1,9},{9,1},{17,25},{25,17},{2,10},{10... | collective-permute-start | bytes 8650760 | tf_op jit(solution)/shard_map/ppermute | solution.py:216
  346.6 63.6 %collective-permute-start.50 = (bf16[8,704,256]{2,1,0:T(8,128)(2,1)}, bf16[8,704,256]{2,1,0:T(8,128)(2,1)}, u32[]{:S(2)}, u32[]{:S(2)}) collective-permute-start(bf16[8,704,256]{2,1,0:T(8,128)(2,1)} %all-to-all-done.1.refs_0_), channel_id=1, source_target_pairs={{0,8},{8,0},{16,24},{24,16},{1,9},{9,1},{17,25},{25,17},{2,10},{10... | collective-permute-start | bytes 8650760 | tf_op jit(solution)/shard_map/ppermute | solution.py:216
  346.6 63.6 %collective-permute-start.51 = (bf16[8,704,256]{2,1,0:T(8,128)(2,1)}, bf16[8,704,256]{2,1,0:T(8,128)(2,1)}, u32[]{:S(2)}, u32[]{:S(2)}) collective-permute-start(bf16[8,704,256]{2,1,0:T(8,128)(2,1)} %all-to-all-done.2.refs_1_), channel_id=1, source_target_pairs={{0,8},{8,0},{16,24},{24,16},{1,9},{9,1},{17,25},{25,17},{2,10},{10... | collective-permute-start | bytes 8650760 | tf_op jit(solution)/shard_map/ppermute | solution.py:216
  410.2 38.0 %collective-permute-start.58 = (bf16[2,704,256]{2,1,0:T(8,128)(2,1)S(1)}, bf16[2,704,256]{2,1,0:T(8,128)(2,1)}, u32[]{:S(2)}, u32[]{:S(2)}) collective-permute-start(bf16[2,704,256]{2,1,0:T(8,128)(2,1)S(1)} %copy-done.21), channel_id=1, source_target_pairs={{0,8},{8,0},{16,24},{24,16},{1,9},{9,1},{17,25},{25,17},{2,10},{10... | collective-permute-start | bytes 2162696 | tf_op jit(solution)/shard_map/ppermute | solution.py:216
  410.3 38.6 %collective-permute-start.59 = (bf16[2,704,256]{2,1,0:T(8,128)(2,1)}, bf16[2,704,256]{2,1,0:T(8,128)(2,1)}, u32[]{:S(2)}, u32[]{:S(2)}) collective-permute-start(bf16[2,704,256]{2,1,0:T(8,128)(2,1)} %collective-permute-done.28.refs_3_), channel_id=1, source_target_pairs={{0,8},{8,0},{16,24},{24,16},{1,9},{9,1},{17,25},{25,17},{2,10},{10... | collective-permute-start | bytes 2162696 | tf_op jit(solution)/shard_map/ppermute | solution.py:216
  676.0 29.9 %collective-permute-start.96 = (bf16[704,512]{1,0:T(8,128)(2,1)}, bf16[704,512]{1,0:T(8,128)(2,1)}, u32[]{:S(2)}, u32[]{:S(2)}) collective-permute-start(bf16[704,512]{1,0:T(8,128)(2,1)} %get-tuple-element.544), channel_id=1, source_target_pairs={{0,16},{8,24},{16,0},{24,8},{1,17},{9,25},{17,1},{25,9},{2,18},{10... | collective-permute-start | bytes 2162696 | tf_op jit(solution)/shard_map/ppermute | solution.py:222
  678.3 71.3 %all-to-all-start.3 = ((bf16[8,704,256]{2,1,0:T(8,128)(2,1)}), bf16[8,704,256]{2,1,0:T(8,128)(2,1)}, u32[]{:S(2)}, u32[]{:S(2)}) async-start(bf16[8,704,256]{2,1,0:T(8,128)(2,1)} %bitcast.199), calls=%async_computation.3 | async-start | bytes 5767168 | tf_op jit(solution)/shard_map/all_to_all | solution.py:302
  708.5 54.1 %collective-permute-start.104 = (bf16[704,2048]{1,0:T(8,128)(2,1)}, bf16[704,2048]{1,0:T(8,128)(2,1)}, u32[]{:S(2)}, u32[]{:S(2)}) collective-permute-start(bf16[704,2048]{1,0:T(8,128)(2,1)} %convolution_convert_fusion.7), channel_id=1, source_target_pairs={{0,8},{8,0},{16,24},{24,16},{1,9},{9,1},{17,25},{25,17},{2,10},{10... | collective-permute-start | bytes 8650760 | tf_op jit(solution)/shard_map/ppermute | solution.py:216
  709.0 32.0 %collective-permute-start.97 = (bf16[128,2048]{1,0:T(8,128)(2,1)}, bf16[128,2048]{1,0:T(8,128)(2,1)S(1)}, u32[]{:S(2)}, u32[]{:S(2)}) collective-permute-start(bf16[128,2048]{1,0:T(8,128)(2,1)} %collective-permute-done.93.refs_1_), channel_id=1, source_target_pairs={{0,2},{2,4},{4,6},{6,7},{7,5},{5,3},{3,1},{1,0},{8,10},{10,12},{12... | collective-permute-start | bytes 1572872 | tf_op jit(solution)/shard_map/ppermute | solution.py:76
  709.6 31.4 %collective-permute-start.98 = (bf16[128,2048]{1,0:T(8,128)(2,1)}, bf16[128,2048]{1,0:T(8,128)(2,1)S(1)}, u32[]{:S(2)}, u32[]{:S(2)}) collective-permute-start(bf16[128,2048]{1,0:T(8,128)(2,1)} %collective-permute-done.94.refs_8_), channel_id=1, source_target_pairs={{0,1},{2,0},{4,2},{6,4},{7,6},{5,7},{3,5},{1,3},{8,9},{10,8},{12,1... | collective-permute-start | bytes 1572872 | tf_op jit(solution)/shard_map/ppermute | solution.py:76
  711.3 29.7 %collective-permute-start.100 = (bf16[704,512]{1,0:T(8,128)(2,1)S(1)}, bf16[704,512]{1,0:T(8,128)(2,1)S(1)}, u32[]{:S(2)}, u32[]{:S(2)}) collective-permute-start(bf16[704,512]{1,0:T(8,128)(2,1)S(1)} %copy-done.57), channel_id=1, source_target_pairs={{0,16},{8,24},{16,0},{24,8},{1,17},{9,25},{17,1},{25,9},{2,18},{10... | collective-permute-start | bytes 2162696 | tf_op jit(solution)/shard_map/ppermute | solution.py:222
  785.7 57.9 %collective-permute-start.108 = (bf16[704,512]{1,0:T(8,128)(2,1)}, bf16[704,512]{1,0:T(8,128)(2,1)}, u32[]{:S(2)}, u32[]{:S(2)}) collective-permute-start(bf16[704,512]{1,0:T(8,128)(2,1)} %get-tuple-element.595), channel_id=1, source_target_pairs={{0,16},{8,24},{16,0},{24,8},{1,17},{9,25},{17,1},{25,9},{2,18},{10... | collective-permute-start | bytes 2162696 | tf_op jit(solution)/shard_map/ppermute | solution.py:222
  787.2 56.4 %collective-permute-start.109 = (bf16[704,512]{1,0:T(8,128)(2,1)}, bf16[704,512]{1,0:T(8,128)(2,1)}, u32[]{:S(2)}, u32[]{:S(2)}) collective-permute-start(bf16[704,512]{1,0:T(8,128)(2,1)} %get-tuple-element.596), channel_id=1, source_target_pairs={{0,16},{8,24},{16,0},{24,8},{1,17},{9,25},{17,1},{25,9},{2,18},{10... | collective-permute-start | bytes 2162696 | tf_op jit(solution)/shard_map/ppermute | solution.py:222
  787.7 55.9 %collective-permute-start.110 = (bf16[704,512]{1,0:T(8,128)(2,1)}, bf16[704,512]{1,0:T(8,128)(2,1)}, u32[]{:S(2)}, u32[]{:S(2)}) collective-permute-start(bf16[704,512]{1,0:T(8,128)(2,1)} %get-tuple-element.597), channel_id=1, source_target_pairs={{0,16},{8,24},{16,0},{24,8},{1,17},{9,25},{17,1},{25,9},{2,18},{10... | collective-permute-start | bytes 2162696 | tf_op jit(solution)/shard_map/ppermute | solution.py:222
  790.9 83.0 %all-to-all-start.4 = ((bf16[8,704,256]{2,1,0:T(8,128)(2,1)}), bf16[8,704,256]{2,1,0:T(8,128)(2,1)}, u32[]{:S(2)}, u32[]{:S(2)}) async-start(bf16[8,704,256]{2,1,0:T(8,128)(2,1)} %bitcast.198), calls=%async_computation.4 | async-start | bytes 5767168 | tf_op jit(solution)/shard_map/all_to_all | solution.py:302
  878.5 62.7 %collective-permute-start.134 = (bf16[704,2048]{1,0:T(8,128)(2,1)}, bf16[704,2048]{1,0:T(8,128)(2,1)}, u32[]{:S(2)}, u32[]{:S(2)}) collective-permute-start(bf16[704,2048]{1,0:T(8,128)(2,1)} %convolution_convert_fusion.6), channel_id=1, source_target_pairs={{0,8},{8,0},{16,24},{24,16},{1,9},{9,1},{17,25},{25,17},{2,10},{10... | collective-permute-start | bytes 8650760 | tf_op jit(solution)/shard_map/ppermute | solution.py:216
  914.0 43.1 %collective-permute-start.131 = (bf16[256,2048]{1,0:T(8,128)(2,1)}, bf16[256,2048]{1,0:T(8,128)(2,1)}, u32[]{:S(2)}, u32[]{:S(2)}) collective-permute-start(bf16[256,2048]{1,0:T(8,128)(2,1)} %get-tuple-element.673), channel_id=1, source_target_pairs={{0,8},{8,0},{16,24},{24,16},{1,9},{9,1},{17,25},{25,17},{2,10},{10... | collective-permute-start | bytes 3145736 | tf_op jit(solution)/shard_map/ppermute | solution.py:216
  930.5 41.0 %all-to-all-start.5 = ((bf16[8,384,256]{2,1,0:T(8,128)(2,1)}), bf16[8,384,256]{2,1,0:T(8,128)(2,1)S(1)}, u32[]{:S(2)}, u32[]{:S(2)}) async-start(bf16[8,384,256]{2,1,0:T(8,128)(2,1)} %add_convert_fusion.8), calls=%async_computation.5 | async-start | bytes 3145728 | tf_op jit(solution)/shard_map/all_to_all | solution.py:302
  (213 other events, 3805.0 us)
